TPU v7x, 32 devices: a whole 2x2x4 slice. The times are simulated.
32 devices in a mesh: group: 2 (over x), tensor: 8 (over z, y), dp: 2 (over core).
Axes of the slice: x: 2, y: 2, z: 4, core: 2. Of those that a mesh axis runs over, the one named last changes fastest.
Arguments:
- tokens_in: bfloat16 [1536, 5120], P(('group', 'tensor', 'dp')), parts along dimension 0, may hold values from -6 to 6
- grad_out: bfloat16 [1536, 5120], P(('group', 'tensor', 'dp')), parts along dimension 0, may hold values from -6 to 6
- gate_blocks: bfloat16 [960, 128, 128], P('tensor'), may hold values from -0.15625 to 0.15625
- up_blocks: bfloat16 [960, 128, 128], P('tensor'), may hold values from -0.15625 to 0.15625
- down_blocks: bfloat16 [960, 128, 128], P('tensor'), may hold values from -0.109375 to 0.109375
- gate_index: int32 [960], P('tensor'), may hold values from 0 to 479, as said below
- up_index: int32 [960], P('tensor'), may hold values from 0 to 479, as said below
- down_index: int32 [960], P('tensor'), may hold values from 0 to 479, as said below
Outputs:
- output: bfloat16 [1536, 5120], P(('group', 'tensor', 'dp')), parts along dimension 0
- input_grad: bfloat16 [1536, 5120], P(('group', 'tensor', 'dp')), parts along dimension 0
- gate_grad_blocks: float32 [1920, 128, 128], P(('group', 'tensor', 'dp')), parts along dimension 0
- up_grad_blocks: float32 [1920, 128, 128], P(('group', 'tensor', 'dp')), parts along dimension 0
- down_grad_blocks: float32 [1920, 128, 128], P(('group', 'tensor', 'dp')), parts along dimension 0
There are 2 independent parts, one for each index of `group`. A program takes and returns all parts, laid end to end along the dimension named above; an argument that names none is the same for every part. Nothing has to cross between parts.
Inputs may be any that keep to these rules, and one draw needn't show every extreme that they name: `gate_index`: each aligned run of 120 entries (the blocks of one tensor device) holds distinct values, among them 0 and 479. `up_index`: each aligned run of 120 entries (the blocks of one tensor device) holds distinct values, among them 0 and 479. `down_index`: each aligned run of 120 entries (the blocks of one tensor device) holds distinct values, among them 0 and 479.
All inputs are finite; a program needn't handle non-finite values.
Results may differ from a plain program's by a relative error of at most 0.0051.
Values may be sent and summed in bfloat16 or wider, within the bound.
No kernel may reach another device: no remote copies, remote signals or barrier semaphores. Data moves between devices by JAX's collectives and lax.ppermute only.
A program may use at most 320 MiB of HBM per device.

v0:
```python
import jax
import jax.numpy as jnp
from jax import lax
from jax.sharding import PartitionSpec as P

FF = 12288


def selector(positions, total, dtype):
    return (positions[:, None] == jnp.arange(total, dtype=jnp.int32)[None, :]).astype(dtype)


def select_blocks(values, positions, total):
    table = selector(positions, total, values.dtype)
    return jnp.einsum("tkb,nk->tnb", values, table)


def place(products, positions, total):
    table = selector(positions, total, jnp.float32)
    return jnp.einsum(
        "tnc,nk->tkc",
        products,
        table,
        precision=lax.Precision.HIGHEST,
        preferred_element_type=jnp.float32,
    )


def project_in(input_blocks, blocks, block_index, dim_blocks, columns):
    picked = select_blocks(input_blocks, block_index % dim_blocks, dim_blocks)
    products = jnp.einsum("tnb,nbc->tnc", picked, blocks, preferred_element_type=jnp.float32)
    return place(products, block_index // dim_blocks, columns)


def project_out(hidden, blocks, block_index, dim_blocks):
    picked = select_blocks(hidden, block_index // dim_blocks, hidden.shape[1])
    products = jnp.einsum("tnc,ncb->tnb", picked, blocks, preferred_element_type=jnp.float32)
    return place(products, block_index % dim_blocks, dim_blocks)


def project_back(grad_blocks, blocks, block_index, dim_blocks, columns):
    picked = select_blocks(grad_blocks, block_index % dim_blocks, dim_blocks)
    products = jnp.einsum("tnb,ncb->tnc", picked, blocks, preferred_element_type=jnp.float32)
    return place(products, block_index // dim_blocks, columns)


def back_in(hidden_part, blocks, block_index, dim_blocks):
    picked = select_blocks(hidden_part, block_index // dim_blocks, hidden_part.shape[1])
    products = jnp.einsum("tnc,nbc->tnb", picked, blocks, preferred_element_type=jnp.float32)
    return place(products, block_index % dim_blocks, dim_blocks)


def grad_in(input_blocks, hidden_part, block_index, dim_blocks):
    picked = select_blocks(input_blocks, block_index % dim_blocks, dim_blocks)
    partner = select_blocks(hidden_part, block_index // dim_blocks, hidden_part.shape[1])
    return jnp.einsum("tnb,tnc->nbc", picked, partner, preferred_element_type=jnp.float32)


def grad_from_hidden(hidden, grad_blocks, block_index, dim_blocks):
    picked = select_blocks(hidden, block_index // dim_blocks, hidden.shape[1])
    partner = select_blocks(grad_blocks, block_index % dim_blocks, dim_blocks)
    return jnp.einsum("tnc,tnb->ncb", picked, partner, preferred_element_type=jnp.float32)


def body(
    tokens_in, grad_out, gate_blocks, up_blocks, down_blocks, gate_index, up_index, down_index
):
    block_size = gate_blocks.shape[1]
    model_width = tokens_in.shape[1]
    dim_blocks = model_width // block_size
    owners = lax.axis_size("tensor")
    columns = FF // (block_size * owners)
    row_count = tokens_in.shape[0]
    input_full = lax.all_gather(tokens_in, "tensor", axis=0, tiled=True)
    token_count = input_full.shape[0]
    input_blocks = input_full.reshape(token_count, dim_blocks, block_size)
    gate_pre = project_in(input_blocks, gate_blocks, gate_index, dim_blocks, columns)
    up_pre = project_in(input_blocks, up_blocks, up_index, dim_blocks, columns)
    sigmoid_vals = jax.nn.sigmoid(gate_pre)
    activated = gate_pre * sigmoid_vals
    hidden = (activated * up_pre).astype(jnp.bfloat16)
    output = lax.psum_scatter(
        project_out(hidden, down_blocks, down_index, dim_blocks).reshape(
            row_count * lax.axis_size("tensor"), model_width
        ),
        "tensor",
        scatter_dimension=0,
        tiled=True,
    ).astype(jnp.bfloat16)
    grad_full = lax.all_gather(grad_out, "tensor", axis=0, tiled=True)
    grad_blocks = grad_full.reshape(token_count, dim_blocks, block_size)
    hidden_grad = project_back(grad_blocks, down_blocks, down_index, dim_blocks, columns)
    gate_grad = (
        hidden_grad * up_pre * sigmoid_vals * (1.0 + gate_pre * (1.0 - sigmoid_vals))
    ).astype(jnp.bfloat16)
    up_grad = (hidden_grad * activated).astype(jnp.bfloat16)
    summed = back_in(gate_grad, gate_blocks, gate_index, dim_blocks) + back_in(
        up_grad, up_blocks, up_index, dim_blocks
    )
    input_grad = lax.psum_scatter(
        summed.reshape(row_count * lax.axis_size("tensor"), model_width),
        "tensor",
        scatter_dimension=0,
        tiled=True,
    ).astype(jnp.bfloat16)
    grad_scale = jnp.float32(1.0) / jnp.sqrt(jnp.float32(token_count * lax.axis_size("dp")))
    gate_part = grad_in(input_blocks, gate_grad, gate_index, dim_blocks)
    up_part = grad_in(input_blocks, up_grad, up_index, dim_blocks)
    down_part = grad_from_hidden(hidden, grad_blocks, down_index, dim_blocks)
    gate_sum, up_sum, down_sum = (
        lax.psum_scatter(gate_part, "dp", scatter_dimension=0, tiled=True),
        lax.psum_scatter(up_part, "dp", scatter_dimension=0, tiled=True),
        lax.psum_scatter(down_part, "dp", scatter_dimension=0, tiled=True),
    )
    return (output, input_grad, gate_sum * grad_scale, up_sum * grad_scale, down_sum * grad_scale)


def solution(mesh):
    placed = (
        P(("group", "tensor", "dp"), None),
        P(("group", "tensor", "dp"), None),
        P("tensor", None, None),
        P("tensor", None, None),
        P("tensor", None, None),
        P("tensor"),
        P("tensor"),
        P("tensor"),
    )
    return jax.shard_map(
        body,
        mesh=mesh,
        in_specs=placed,
        out_specs=(
            P(("group", "tensor", "dp"), None),
            P(("group", "tensor", "dp"), None),
            P(("group", "tensor", "dp"), None, None),
            P(("group", "tensor", "dp"), None, None),
            P(("group", "tensor", "dp"), None, None),
        ),
        check_vma=False,
    )
```

profile of v0, /device:TPU:0, one launch (start us, length us, event | category | flops | bytes accessed | tf_op | source)
XLA Modules:
  0.0 798.3 jit_solution(16464482991136968312)
XLA Ops:
  10.7 72.3 %all-gather.3.cloned.1.call-done = bf16[384,5120]{1,0:T(8,128)(2,1)} async-done(((bf16[48,5120]{1,0:T(8,128)(2,1)}), bf16[384,5120]{1,0:T(8,128)(2,1)}) %all-gather.3.cloned.1.call-update) | async-done | bytes 3932176 | tf_op jit(solution)/shard_map/all_gather | solution.py:74
  88.0 65.7 %all-gather.5.cloned.1.call-done = bf16[384,5120]{1,0:T(8,128)(2,1)} async-done(((bf16[48,5120]{1,0:T(8,128)(2,1)}), bf16[384,5120]{1,0:T(8,128)(2,1)}) %all-gather.5.cloned.1.call-update) | async-done | bytes 3932176 | tf_op jit(solution)/shard_map/all_gather | solution.py:90
  165.0 16.1 %copy.15 = bf16[384,120,128]{0,2,1:T(8,128)(2,1)} copy(bf16[384,120,128]{2,1,0:T(8,128)(2,1)} %convolution_bitcast_fusion.4) | data formatting | bytes 23592960 | tf_op jit(solution)/shard_map/tkb,nk->tnb/transpose | solution.py:15
  190.8 17.0 %copy.13 = bf16[384,120,128]{0,2,1:T(8,128)(2,1)} copy(bf16[384,120,128]{2,1,0:T(8,128)(2,1)} %convolution_bitcast_fusion.5) | data formatting | bytes 23592960 | tf_op jit(solution)/shard_map/tkb,nk->tnb/transpose | solution.py:15
  229.9 26.7 %fusion.10 = f32[12,384,128]{2,0,1:T(8,128)S(1)} fusion(f32[120,384,128]{2,1,0:T(8,128)} %fusion.79, s32[120]{0:T(128)S(1)} %get-tuple-element.7), kind=kOutput, calls=%fused_computation.10 | convolution fusion | flops 849347968 | bytes 25952736 | tf_op jit(solution)/shard_map/tnc,nk->tkc/dot_general | solution.py:20
  256.6 12.9 %fusion.80 = f32[120,384,128]{2,1,0:T(8,128)} fusion(bf16[384,120,128]{0,2,1:T(8,128)(2,1)} %copy.15, bf16[120,128,128]{2,1,0:T(8,128)(2,1)} %param.11), kind=kOutput, calls=%fused_computation.92 | convolution fusion | flops 1509949440 | bytes 39321600 | tf_op jit(solution)/shard_map/tnb,nbc->tnc/dot_general | solution.py:31
  269.5 27.9 %fusion.8 = f32[12,384,128]{2,0,1:T(8,128)} fusion(f32[120,384,128]{2,1,0:T(8,128)} %fusion.80, s32[120]{0:T(128)S(1)} %get-tuple-element.9), kind=kOutput, calls=%fused_computation.8 | convolution fusion | flops 849347968 | bytes 25952736 | tf_op jit(solution)/shard_map/tnc,nk->tkc/dot_general | solution.py:20
  297.4 14.3 %fusion.18 = f32[120,384,128]{2,1,0:T(8,128)} fusion(bf16[120,128,128]{2,1,0:T(8,128)(2,1)} %param.12, bf16[384,120,128]{2,1,0:T(8,128)(2,1)} %convolution_bitcast_fusion.2), kind=kOutput, calls=%fused_computation.18 | convolution fusion | flops 1509949440 | bytes 39321600 | tf_op jit(solution)/shard_map/tnb,ncb->tnc/dot_general | solution.py:43
  311.7 26.8 %fusion.4 = f32[12,384,128]{2,0,1:T(8,128)S(1)} fusion(f32[120,384,128]{2,1,0:T(8,128)} %fusion.18, s32[120]{0:T(128)S(1)} %get-tuple-element.6), kind=kOutput, calls=%fused_computation.4 | convolution fusion | flops 849347968 | bytes 25952736 | tf_op jit(solution)/shard_map/tnc,nk->tkc/dot_general | solution.py:20
  350.7 14.5 %fusion.22 = f32[120,384,128]{2,1,0:T(8,128)} fusion(bf16[120,128,128]{2,1,0:T(8,128)(2,1)} %param.11, bf16[384,120,128]{2,1,0:T(8,128)(2,1)} %convolution_bitcast_fusion), kind=kOutput, calls=%fused_computation.22 | convolution fusion | flops 1509949440 | bytes 39321600 | tf_op jit(solution)/shard_map/tnc,nbc->tnb/dot_general | solution.py:49
  365.2 29.2 %fusion = f32[40,384,128]{2,0,1:T(8,128)} fusion(f32[120,384,128]{2,1,0:T(8,128)} %fusion.22, s32[120]{0:T(128)S(1)} %get-tuple-element.10), kind=kOutput, calls=%fused_computation | convolution fusion | flops 2831160064 | bytes 31457760 | tf_op jit(solution)/shard_map/tnc,nk->tkc/dot_general | solution.py:20
  394.5 14.7 %fusion.26 = f32[120,384,128]{2,1,0:T(8,128)} fusion(bf16[120,128,128]{2,1,0:T(8,128)(2,1)} %param.10, bf16[384,120,128]{2,1,0:T(8,128)(2,1)} %convolution_bitcast_fusion.1), kind=kOutput, calls=%fused_computation.26 | convolution fusion | flops 1509949440 | bytes 39321600 | tf_op jit(solution)/shard_map/tnc,nbc->tnb/dot_general | solution.py:49
  409.2 30.4 %fusion.39 = f32[40,384,128]{2,0,1:T(8,128)} fusion(f32[40,384,128]{2,0,1:T(8,128)} %fusion, f32[120,384,128]{2,1,0:T(8,128)} %fusion.26, s32[120]{0:T(128)S(1)} %copy-done.6), kind=kOutput, calls=%fused_computation.53 | convolution fusion | flops 2833126144 | bytes 39322080 | tf_op jit(solution)/shard_map/tnc,nk->tkc/dot_general | solution.py:20
  457.2 16.9 %copy.17 = bf16[384,120,128]{0,2,1:T(8,128)(2,1)} copy(bf16[384,120,128]{2,1,0:T(8,128)(2,1)} %convolution_bitcast_fusion.3) | data formatting | bytes 23592960 | tf_op jit(solution)/shard_map/tkb,nk->tnb/transpose | solution.py:15
  474.1 14.3 %fusion.20 = f32[120,128,128]{2,1,0:T(8,128)} fusion(bf16[384,120,128]{0,2,1:T(8,128)(2,1)} %copy.17, bf16[384,120,128]{2,1,0:T(8,128)(2,1)} %convolution_bitcast_fusion.2), kind=kOutput, calls=%fused_computation.20 | convolution fusion | flops 1509949440 | bytes 31457280 | tf_op jit(solution)/shard_map/tnc,tnb->ncb/dot_general | solution.py:62
  488.7 14.3 %fusion.28 = f32[120,128,128]{2,1,0:T(8,128)} fusion(bf16[384,120,128]{0,2,1:T(8,128)(2,1)} %copy.13, bf16[384,120,128]{2,1,0:T(8,128)(2,1)} %convolution_bitcast_fusion.1), kind=kOutput, calls=%fused_computation.28 | convolution fusion | flops 1509949440 | bytes 31457280 | tf_op jit(solution)/shard_map/tnb,tnc->nbc/dot_general | solution.py:56
  503.1 14.3 %fusion.24 = f32[120,128,128]{2,1,0:T(8,128)} fusion(bf16[384,120,128]{0,2,1:T(8,128)(2,1)} %copy.15, bf16[384,120,128]{2,1,0:T(8,128)(2,1)} %convolution_bitcast_fusion), kind=kOutput, calls=%fused_computation.24 | convolution fusion | flops 1509949440 | bytes 31457280 | tf_op jit(solution)/shard_map/tnb,tnc->nbc/dot_general | solution.py:56
  517.8 13.4 %fusion.81 = f32[120,384,128]{2,1,0:T(8,128)} fusion(bf16[384,120,128]{0,2,1:T(8,128)(2,1)} %copy.17, bf16[120,128,128]{2,1,0:T(8,128)(2,1)} %param.12), kind=kOutput, calls=%fused_computation.93 | convolution fusion | flops 1509949440 | bytes 39321600 | tf_op jit(solution)/shard_map/tnc,ncb->tnb/dot_general | solution.py:37
  531.1 28.0 %fusion.6 = f32[40,384,128]{2,0,1:T(8,128)S(1)} fusion(f32[120,384,128]{2,1,0:T(8,128)} %fusion.81, s32[120]{0:T(128)S(1)} %copy-done.4), kind=kOutput, calls=%fused_computation.6 | convolution fusion | flops 2831160064 | bytes 31457760 | tf_op jit(solution)/shard_map/tnc,nk->tkc/dot_general | solution.py:20
  563.9 22.2 %reduce-scatter.8.cloned.1.call-done = f32[48,5120]{1,0:T(8,128)} async-done(((f32[384,5120]{1,0:T(8,128)}), f32[48,5120]{1,0:T(8,128)}) %reduce-scatter.8.cloned.1.call-update) | async-done | bytes 983056 | tf_op jit(solution)/shard_map/reduce_scatter | solution.py:100
  588.2 15.8 %reduce-scatter.14.cloned.1.call-done = f32[60,128,128]{2,1,0:T(8,128)} async-done(((f32[120,128,128]{2,1,0:T(8,128)}), f32[60,128,128]{2,1,0:T(8,128)}) %reduce-scatter.14.cloned.1.call-update) | async-done | bytes 3932176 | tf_op jit(solution)/shard_map/reduce_scatter | solution.py:113
  608.7 15.2 %reduce-scatter.10.cloned.1.call-done = f32[60,128,128]{2,1,0:T(8,128)} async-done(((f32[120,128,128]{2,1,0:T(8,128)}), f32[60,128,128]{2,1,0:T(8,128)}) %reduce-scatter.10.cloned.1.call-update) | async-done | bytes 3932176 | tf_op jit(solution)/shard_map/reduce_scatter | solution.py:111
  628.6 15.1 %reduce-scatter.12.cloned.1.call-done = f32[60,128,128]{2,1,0:T(8,128)} async-done(((f32[120,128,128]{2,1,0:T(8,128)}), f32[60,128,128]{2,1,0:T(8,128)}) %reduce-scatter.12.cloned.1.call-update) | async-done | bytes 3932176 | tf_op jit(solution)/shard_map/reduce_scatter | solution.py:112
  648.4 140.5 %reduce-scatter.6.cloned.1.call-done = f32[48,5120]{1,0:T(8,128)} async-done(((f32[384,5120]{1,0:T(8,128)}), f32[48,5120]{1,0:T(8,128)}) %reduce-scatter.6.cloned.1.call-update) | async-done | bytes 983056 | tf_op jit(solution)/shard_map/reduce_scatter | solution.py:82
  (47 shorter events, 105.0 us)
Async XLA Ops:
  7.2 75.9 %all-gather.3.cloned.1.call-start = ((), (), s32[]{:S(2)}) async-start(), calls=%async_computation.5 | async-start | bytes 4423680 | tf_op jit(solution)/shard_map/all_gather | solution.py:74
  7.9 145.8 %all-gather.5.cloned.1.call-start = ((), (), s32[]{:S(2)}) async-start(), calls=%async_computation.7 | async-start | bytes 4423680 | tf_op jit(solution)/shard_map/all_gather | solution.py:90
  8.6 577.5 %reduce-scatter.8.cloned.1.call-start = ((), (), s32[]{:S(2)}) async-start(), calls=%async_computation.8 | async-start | bytes 8847360 | tf_op jit(solution)/shard_map/reduce_scatter | solution.py:100
  9.4 171.7 %copy-start.5 = (s32[120]{0:T(128)}, s32[120]{0:T(128)S(1)}, u32[]{:S(2)}) copy-start(s32[120]{0:T(128)S(1)} %get-tuple-element.8) | copy-start | bytes 1444
  10.7 197.1 %copy-start.3 = (s32[120]{0:T(128)}, s32[120]{0:T(128)S(1)}, u32[]{:S(2)}) copy-start(s32[120]{0:T(128)S(1)} %get-tuple-element.5) | copy-start | bytes 1444
  153.7 5.2 copy-start.1
  207.8 9.8 %copy-start = (bf16[120,128,128]{2,1,0:T(8,128)(2,1)S(1)}, bf16[120,128,128]{2,1,0:T(8,128)(2,1)}, u32[]{:S(2)}) copy-start(bf16[120,128,128]{2,1,0:T(8,128)(2,1)} %param.10) | copy-start | bytes 11796484
  338.5 6.0 copy-start.2
  394.5 14.7 %copy-start.6 = (s32[120]{0:T(128)S(1)}, s32[120]{0:T(128)}, u32[]{:S(2)}) copy-start(s32[120]{0:T(128)} %copy-done.5) | copy-start | bytes 1444
  447.6 156.3 %reduce-scatter.14.cloned.1.call-start = ((), (), s32[]{:S(2)}) async-start(), calls=%async_computation.11 | async-start | bytes 11796480 | tf_op jit(solution)/shard_map/reduce_scatter | solution.py:113
  488.5 135.4 %reduce-scatter.10.cloned.1.call-start = ((), (), s32[]{:S(2)}) async-start(), calls=%async_computation.9 | async-start | bytes 11796480 | tf_op jit(solution)/shard_map/reduce_scatter | solution.py:111
  503.1 140.6 %reduce-scatter.12.cloned.1.call-start = ((), (), s32[]{:S(2)}) async-start(), calls=%async_computation.10 | async-start | bytes 11796480 | tf_op jit(solution)/shard_map/reduce_scatter | solution.py:112
  517.5 13.7 %copy-start.4 = (s32[120]{0:T(128)S(1)}, s32[120]{0:T(128)}, u32[]{:S(2)}) copy-start(s32[120]{0:T(128)} %copy-done.3) | copy-start | bytes 1444
  517.5 271.5 %reduce-scatter.6.cloned.1.call-start = ((), (), s32[]{:S(2)}) async-start(), calls=%async_computation.6 | async-start | bytes 8847360 | tf_op jit(solution)/shard_map/reduce_scatter | solution.py:82
Sparse Core Ops, SparseCore 0:
  10.2 72.7 all-gather.2
  85.2 68.4 all-gather.4
  447.7 138.3 reduce-scatter.7
  588.3 15.5 reduce-scatter.13
  606.2 17.6 reduce-scatter.9
  626.0 17.6 reduce-scatter.11
  647.8 141.1 reduce-scatter.5
where the time goes:
time: 809 us; the launch traced here: 798 us
  waiting for transfers between devices  348 us (43%)
  matrix products  341 us (42%)
  local copies, waits for them, and re-layouts  73 us (9%)
  other arithmetic  20.3 us (3%)
  between operations  14.7 us (2%)
    dot_general x6, matrix products, place(): jnp.einsum('tnc,nk->tkc', products, table, precision=lax.Precision.HIGHES...  169 us
    reduce_scatter x1, waiting for transfers between devices, body(): lax.psum_scatter(project_out(hidden, down_blocks, down_index, dim_blocks)...  141 us
    all_gather x1, waiting for transfers between devices, body(): input_full = lax.all_gather(tokens_in, 'tensor', axis=0, tiled=True)  72.3 us
    all_gather x1, waiting for transfers between devices, body(): grad_full = lax.all_gather(grad_out, 'tensor', axis=0, tiled=True)  65.7 us
    transpose x3, local copies, waits for them, and re-layouts, select_blocks(): return jnp.einsum('tkb,nk->tnb', values, table)  50 us
    dot_general x6, matrix products, select_blocks(): return jnp.einsum('tkb,nk->tnb', values, table)  47.4 us
    dot_general x2, matrix products, back_in(): jnp.einsum('tnc,nbc->tnb', picked, blocks, preferred_element_type=jnp.flo...  29.2 us
    dot_general x2, matrix products, grad_in(): jnp.einsum('tnb,tnc->nbc', picked, partner, preferred_element_type=jnp.fl...  28.6 us
  transfers between devices with their start and end apart: 7, of which 7 were waited for; matrix products, arithmetic and copies ran while one was open for 17% of the time, Pallas kernels for 0%

commit v1 on v0

v1 whole, which is shorter than its diff:
```python
import functools

import jax
import jax.numpy as jnp
from jax import lax
from jax.experimental import pallas as pl
from jax.experimental.pallas import tpu as pltpu
from jax.sharding import PartitionSpec as P

FF = 12288
VMEM_LIMIT = 40 * 2**20
PARTS_IN = 3
PARTS_OUT = 2

SMEM_SPEC = pl.BlockSpec(memory_space=pltpu.SMEM)
VMEM_SPEC = pl.BlockSpec(memory_space=pltpu.VMEM)
ANY_SPEC = pl.BlockSpec(memory_space=pl.ANY)


def ring_order(size):
    return list(range(0, size, 2)) + list(range(1, size, 2))[::-1]


def ring_shifts(size):
    order = ring_order(size)
    ahead = [(order[i], order[(i + 1) % size]) for i in range(size)]
    back = [(b, a) for a, b in ahead]

    def to_right(value):
        return lax.ppermute(value, "tensor", ahead)

    def to_left(value):
        return lax.ppermute(value, "tensor", back)

    return to_right, to_left


def ring_gather(rows, size):
    to_right, to_left = ring_shifts(size)
    half = rows.shape[0] // 2
    blocks = [rows]
    from_left = from_right = rows
    for _ in range(size // 2 - 1):
        from_left, from_right = to_right(from_left), to_left(from_right)
        blocks += [from_left, from_right]
    blocks += [to_right(from_left[:half]), to_left(from_right[half:])]
    return jnp.concatenate(blocks, axis=0)


def ring_scatter(parts, size):
    to_right, to_left = ring_shifts(size)
    rows = parts.shape[0] // size
    half = rows // 2
    far = size // 2

    def block(place):
        return parts[place * rows:(place + 1) * rows]

    right = block(size - 1)[:half].astype(jnp.bfloat16)
    left = block(size - 1)[half:].astype(jnp.bfloat16)
    for distance in range(far - 1, -1, -1):
        right, left = to_right(right), to_left(left)
        if distance == 0:
            break
        toward_right, toward_left = block(2 * distance), block(2 * distance - 1)
        if distance == far - 1:
            right = jnp.concatenate(
                [right.astype(jnp.float32) + toward_right[:half], toward_right[half:]], axis=0
            )
            left = jnp.concatenate(
                [toward_left[:half], left.astype(jnp.float32) + toward_left[half:]], axis=0
            )
        else:
            right = right.astype(jnp.float32) + toward_right
            left = left.astype(jnp.float32) + toward_left
        right, left = right.astype(jnp.bfloat16), left.astype(jnp.bfloat16)
    return (block(0) + right.astype(jnp.float32) + left.astype(jnp.float32)).astype(jnp.bfloat16)


def slot_table(index, slots):
    count = index.shape[0]
    hit = index[None, :] == jnp.arange(slots, dtype=jnp.int32)[:, None]
    return jnp.min(jnp.where(hit, jnp.arange(count, dtype=jnp.int32)[None, :], count), axis=1)


def with_zero(blocks):
    return jnp.concatenate([blocks, jnp.zeros((1,) + blocks.shape[1:], blocks.dtype)], axis=0)


def columns_of(lhs, weights, place, first, depth, b):
    strip = jnp.concatenate(
        [
            jnp.concatenate([weights[place(first + n, m)] for n in range(2)], axis=1)
            for m in range(depth)
        ],
        axis=0,
    )
    return jnp.dot(lhs, strip, preferred_element_type=jnp.float32)


def columns_of_turned(lhs, weights, place, first, depth, b):
    strip = jnp.concatenate(
        [
            jnp.concatenate([weights[place(first + n, m)] for m in range(depth)], axis=1)
            for n in range(2)
        ],
        axis=0,
    )
    return lax.dot_general(
        lhs, strip, (((1,), (1,)), ((), ())), preferred_element_type=jnp.float32
    )


def hidden_kernel(dim_blocks, offset, gate_at, up_at, x, gate_w, up_w, *rest):
    hidden, act, slope = rest[-3:]
    first = (offset + pl.program_id(0)) * 2
    b = gate_w.shape[1]

    def strip(at, w):
        return columns_of(
            x[...], w, lambda n, m: at[n * dim_blocks + m], first, dim_blocks, b
        )

    gate = strip(gate_at, gate_w)
    up = strip(up_at, up_w)
    sig = jax.nn.sigmoid(gate)
    activated = gate * sig
    hidden[...] = (activated * up).astype(jnp.bfloat16)
    act[...] = activated
    slope[...] = up * sig * (1.0 + gate * (1.0 - sig))


def grads_kernel(dim_blocks, offset, down_at, g, down_w, act, slope, *rest):
    gate_grad, up_grad = rest[-2:]
    first = (offset + pl.program_id(0)) * 2
    b = down_w.shape[1]
    hidden_grad = columns_of_turned(
        g[...], down_w, lambda n, m: down_at[n * dim_blocks + m], first, dim_blocks, b
    )
    gate_grad[...] = (hidden_grad * slope[...]).astype(jnp.bfloat16)
    up_grad[...] = (hidden_grad * act[...]).astype(jnp.bfloat16)


def output_kernel(dim_blocks, columns, offset, down_at, hidden, down_w, *rest):
    out = rest[-1]
    first = (offset + pl.program_id(0)) * 2
    out[...] = columns_of(
        hidden[...], down_w, lambda n, m: down_at[m * dim_blocks + n], first, columns,
        down_w.shape[1],
    )


def input_grad_kernel(
    dim_blocks, columns, offset, gate_at, up_at, gate_grad, up_grad, gate_w, up_w, *rest
):
    out = rest[-1]
    first = (offset + pl.program_id(0)) * 2
    b = gate_w.shape[1]

    def strip(lhs, at, w):
        return columns_of_turned(
            lhs[...], w, lambda n, m: at[m * dim_blocks + n], first, columns, b
        )

    out[...] = strip(gate_grad, gate_at, gate_w) + strip(up_grad, up_at, up_w)


def strips(kernel, inputs, specs, outs, offset, count, block_outs, flops):
    rows = block_outs[0].shape[0]
    width = 2 * 128

    def strip_spec():
        return pl.BlockSpec((rows, width), lambda i: (0, offset + i))

    in_specs = [strip_spec() if spec is None else spec for spec in specs]
    aliases = {}
    if outs is not None:
        aliases = {len(inputs) + i: i for i in range(len(outs))}
        inputs = list(inputs) + list(outs)
        in_specs += [ANY_SPEC] * len(outs)
    return pl.pallas_call(
        functools.partial(kernel, offset),
        grid=(count,),
        in_specs=in_specs,
        out_specs=[strip_spec() for _ in block_outs],
        out_shape=list(block_outs),
        input_output_aliases=aliases,
        compiler_params=pltpu.CompilerParams(vmem_limit_bytes=VMEM_LIMIT),
        cost_estimate=pl.CostEstimate(flops=flops, bytes_accessed=8 * 2**20, transcendentals=0),
    )(*inputs)


def in_calls(kernel, inputs, specs, total, calls, block_outs, flops):
    outs = None
    calls = calls if total % calls == 0 else 1
    for call in range(calls):
        count = total // calls
        outs = strips(
            kernel, inputs, specs, outs, call * count, count, block_outs, flops // calls
        )
    return outs


def block_grads(left, right, index, dim_blocks, left_is_model, arrived, scale):
    count = index.shape[0]
    rows = left.shape[0]
    b = 128
    group = max(d for d in range(1, 13) if count % d == 0)

    def kernel(at, left_ref, right_ref, *rest):
        out = rest[-1]
        base = pl.program_id(0) * group
        for i in range(group):
            slot = at[base + i]
            model, hidden = slot % dim_blocks, slot // dim_blocks
            a, c = (model, hidden) if left_is_model else (hidden, model)
            value = lax.dot_general(
                left_ref[:, pl.ds(pl.multiple_of(a * b, b), b)],
                right_ref[:, pl.ds(pl.multiple_of(c * b, b), b)],
                (((0,), (0,)), ((), ())),
                preferred_element_type=jnp.float32,
            )
            if arrived is not None:
                value = (value + rest[0][i].astype(jnp.float32)) * scale
            out[i] = value.astype(out.dtype)

    spec = pl.BlockSpec((group, b, b), lambda i: (i, 0, 0))
    extra = [] if arrived is None else [arrived]
    dtype = jnp.bfloat16 if arrived is None else jnp.float32
    return pl.pallas_call(
        kernel,
        grid=(count // group,),
        in_specs=[SMEM_SPEC, VMEM_SPEC, VMEM_SPEC] + [spec] * len(extra),
        out_specs=spec,
        out_shape=jax.ShapeDtypeStruct((count, b, b), dtype),
        compiler_params=pltpu.CompilerParams(vmem_limit_bytes=VMEM_LIMIT),
        cost_estimate=pl.CostEstimate(
            flops=8 * count * rows * b * b, bytes_accessed=8 * 2**20, transcendentals=0
        ),
    )(index, left, right, *extra)


def body(
    tokens_in, grad_out, gate_blocks, up_blocks, down_blocks, gate_index, up_index, down_index
):
    block_size = gate_blocks.shape[1]
    model_width = tokens_in.shape[1]
    dim_blocks = model_width // block_size
    owners = lax.axis_size("tensor")
    columns = FF // (block_size * owners)
    width = columns * block_size
    token_count = tokens_in.shape[0] * owners
    count = gate_blocks.shape[0]
    slots = columns * dim_blocks

    gate_at, up_at, down_at = (slot_table(i, slots) for i in (gate_index, up_index, down_index))
    gate_w, up_w, down_w = (with_zero(w) for w in (gate_blocks, up_blocks, down_blocks))

    x = ring_gather(tokens_in, owners)
    g = ring_gather(grad_out, owners)

    unit = 2 * token_count * model_width * width
    narrow = jax.ShapeDtypeStruct((token_count, width), jnp.bfloat16)
    wide = jax.ShapeDtypeStruct((token_count, width), jnp.float32)
    total = jax.ShapeDtypeStruct((token_count, model_width), jnp.float32)

    hidden, act, slope = in_calls(
        functools.partial(hidden_kernel, dim_blocks),
        [gate_at, up_at, x, gate_w, up_w],
        [SMEM_SPEC] * 2 + [VMEM_SPEC] * 3,
        columns // 2, PARTS_IN, [narrow, wide, wide], 2 * unit,
    )
    (out_parts,) = in_calls(
        functools.partial(output_kernel, dim_blocks, columns),
        [down_at, hidden, down_w],
        [SMEM_SPEC] + [VMEM_SPEC] * 2,
        dim_blocks // 2, PARTS_OUT, [total], unit,
    )
    output = ring_scatter(out_parts, owners)

    gate_grad, up_grad = in_calls(
        functools.partial(grads_kernel, dim_blocks),
        [down_at, g, down_w, act, slope],
        [SMEM_SPEC] + [VMEM_SPEC] * 2 + [None] * 2,
        columns // 2, PARTS_IN, [narrow, narrow], unit,
    )
    (grad_parts,) = in_calls(
        functools.partial(input_grad_kernel, dim_blocks, columns),
        [gate_at, up_at, gate_grad, up_grad, gate_w, up_w],
        [SMEM_SPEC] * 2 + [VMEM_SPEC] * 4,
        dim_blocks // 2, PARTS_OUT, [total], 2 * unit,
    )
    input_grad = ring_scatter(grad_parts, owners)

    pairs = lax.axis_size("dp")
    share = count // pairs
    me = lax.axis_index("dp")
    scale = 1.0 / float(token_count * pairs) ** 0.5
    swap = [(0, 1), (1, 0)]
    sums = []
    for left, right, index, left_is_model in (
        (hidden, g, down_index, False),
        (x, gate_grad, gate_index, True),
        (x, up_grad, up_index, True),
    ):
        theirs = lax.dynamic_slice(index, ((1 - me) * share,), (share,))
        mine = lax.dynamic_slice(index, (me * share,), (share,))
        sent = block_grads(left, right, theirs, dim_blocks, left_is_model, None, None)
        arrived = lax.ppermute(sent, "dp", swap)
        sums.append(block_grads(left, right, mine, dim_blocks, left_is_model, arrived, scale))
    return output, input_grad, sums[1], sums[2], sums[0]


def solution(mesh):
    rows = P(("group", "tensor", "dp"), None)
    owned = P("tensor", None, None)
    grads = P(("group", "tensor", "dp"), None, None)
    return jax.shard_map(
        body,
        mesh=mesh,
        in_specs=(rows, rows, owned, owned, owned, P("tensor"), P("tensor"), P("tensor")),
        out_specs=(rows, rows, grads, grads, grads),
        check_vma=False,
    )
```

time: 809 us -> 273 us (0.34); the launches traced: 798 us -> 272 us
  matrix products: 341 us -> 0 us
  waiting for transfers between devices: 348 us -> 94.8 us
  Pallas kernels: 0 us -> 101 us
  local copies, waits for them, and re-layouts: 73 us -> 20 us
  starting transfers between devices: 0.75 us -> 37.1 us
  between operations: 14.7 us -> 1.18 us
    dot_general x21 -> x0, matrix products: 341 us -> none  [the longest x6 169 us: place(): jnp.einsum('tnc,nk->tkc', products, table, precision=lax.Precision.HIGHES...]
    reduce_scatter x5 -> x0, waiting for transfers between devices: 209 us -> none  [the longest x1 141 us: body(): lax.psum_scatter(project_out(hidden, down_blocks, down_index, dim_blocks)...]
    all_gather x2 -> x0, waiting for transfers between devices: 138 us -> none  [the longest x1 72.3 us: body(): input_full = lax.all_gather(tokens_in, 'tensor', axis=0, tiled=True)]
    pallas_call x0 -> x16, Pallas kernels: none -> 101 us  [the longest x10 68.6 us: strips(): pl.pallas_call(functools.partial(kernel, offset), grid=(count,), in_specs...]
    ppermute x0 -> x35, waiting for transfers between devices: none -> 94.8 us  [the longest x16 76.9 us: to_right(): return lax.ppermute(value, 'tensor', ahead)]
    transpose x3 -> x0, local copies, waits for them, and re-layouts: 50 us -> none  [select_blocks(): return jnp.einsum('tkb,nk->tnb', values, table)]
    ppermute x0 -> x35, starting transfers between devices: none -> 37.1 us  [the longest x16 30.5 us: to_right(): return lax.ppermute(value, 'tensor', ahead)]
    mul x3 -> x0, other arithmetic: 14.2 us -> none  [the longest x1 4.73 us: body(): gate_sum * grad_scale]
  transfers between devices with their start and end apart: 7 -> 35, of which waited for: 7 -> 14; matrix products, arithmetic and copies ran while one was open for 17% -> 11% of each run, Pallas kernels for 0% -> 35%
where the time goes in v1:
time: 273 us; the launch traced here: 272 us
  Pallas kernels  101 us (37%)
  waiting for transfers between devices  94.8 us (35%)
  starting transfers between devices  37.1 us (14%)
  local copies, waits for them, and re-layouts  20 us (7%)
  other arithmetic  17.8 us (7%)
    ppermute x16, waiting for transfers between devices, to_right(): return lax.ppermute(value, 'tensor', ahead)  76.9 us
    pallas_call x10, Pallas kernels, strips(): pl.pallas_call(functools.partial(kernel, offset), grid=(count,), in_specs...  68.6 us
    pallas_call x6, Pallas kernels, block_grads(): pl.pallas_call(kernel, grid=(count // group,), in_specs=[SMEM_SPEC, VMEM_...  32.6 us
    ppermute x16, starting transfers between devices, to_right(): return lax.ppermute(value, 'tensor', ahead)  30.5 us
    ppermute x16, waiting for transfers between devices, to_left(): return lax.ppermute(value, 'tensor', back)  17.9 us
    unnamed x56, local copies, waits for them, and re-layouts  9.68 us
    another operation x4, other arithmetic  8.97 us
    ppermute x16, starting transfers between devices, to_left(): return lax.ppermute(value, 'tensor', back)  5.99 us
  transfers between devices with their start and end apart: 35, of which 14 were waited for; matrix products, arithmetic and copies ran while one was open for 11% of the time, Pallas kernels for 35%

profile of v1, /device:TPU:0, one launch (start us, length us, event | category | flops | bytes accessed | tf_op | source)
XLA Modules:
  0.0 272.2 jit_solution(287572901244171142)
XLA Ops:
  28.7 8.3 %collective-permute-done.2 = bf16[48,5120]{1,0:T(8,128)(2,1)S(1)} collective-permute-done((bf16[48,5120]{1,0:T(8,128)(2,1)S(1)}, bf16[48,5120]{1,0:T(8,128)(2,1)S(1)}, u32[]{:S(2)}, u32[]{:S(2)}) %collective-permute-start.2) | collective-permute-done | bytes 491552 | tf_op jit(solution)/shard_map/ppermute | solution.py:30
  39.2 8.3 %collective-permute-done.18 = bf16[48,5120]{1,0:T(8,128)(2,1)S(1)} collective-permute-done((bf16[48,5120]{1,0:T(8,128)(2,1)S(1)}, bf16[48,5120]{1,0:T(8,128)(2,1)S(1)}, u32[]{:S(2)}, u32[]{:S(2)}) %collective-permute-start.18) | collective-permute-done | bytes 491552 | tf_op jit(solution)/shard_map/ppermute | solution.py:30
  49.8 8.3 %collective-permute-done.4 = bf16[48,5120]{1,0:T(8,128)(2,1)S(1)} collective-permute-done((bf16[48,5120]{1,0:T(8,128)(2,1)S(1)}, bf16[48,5120]{1,0:T(8,128)(2,1)S(1)}, u32[]{:S(2)}, u32[]{:S(2)}) %collective-permute-start.4) | collective-permute-done | bytes 491552 | tf_op jit(solution)/shard_map/ppermute | solution.py:30
  60.3 8.3 %collective-permute-done.20 = bf16[48,5120]{1,0:T(8,128)(2,1)S(1)} collective-permute-done((bf16[48,5120]{1,0:T(8,128)(2,1)S(1)}, bf16[48,5120]{1,0:T(8,128)(2,1)S(1)}, u32[]{:S(2)}, u32[]{:S(2)}) %collective-permute-start.20) | collective-permute-done | bytes 491552 | tf_op jit(solution)/shard_map/ppermute | solution.py:30
  76.0 8.3 %shard_map.119 = (bf16[384,1536]{1,0:T(8,128)(2,1)S(1)}, f32[384,1536]{1,0:T(8,128)S(1)}, f32[384,1536]{1,0:T(8,128)S(1)}) custom-call(s32[480]{0:T(512)S(1)} %get-tuple-element.62.gate_at, s32[480]{0:T(512)S(1)} %get-tuple-element.61.up_at, bf16[384,5120]{1,0:T(8,128)(2,1)S(1)} %constant_dynamic-update-slice_fusion.x.left_ref, ...), custom_call_target="tpu_custom_call" | custom-call | flops 4026531840 | bytes 8388608 | tf_op jit(solution)/shard_map/pallas_call | solution.py:181
  84.3 6.9 %shard_map.120 = (bf16[384,1536]{1,0:T(8,128)(2,1)S(1)}, f32[384,1536]{1,0:T(8,128)S(1)}, f32[384,1536]{1,0:T(8,128)S(1)}) custom-call(s32[480]{0:T(512)S(1)} %get-tuple-element.62.gate_at, s32[480]{0:T(512)S(1)} %get-tuple-element.61.up_at, ...), custom_call_target="tpu_custom_call", output_to_operand_aliasing={{0}: (5, {}), {1}: (6, {}), {2}: (7, {})} | custom-call | flops 4026531840 | bytes 8388608 | tf_op jit(solution)/shard_map/pallas_call | solution.py:181
  91.2 6.9 %shard_map.121 = (bf16[384,1536]{1,0:T(8,128)(2,1)S(1)}, f32[384,1536]{1,0:T(8,128)S(1)}, f32[384,1536]{1,0:T(8,128)S(1)}) custom-call(s32[480]{0:T(512)S(1)} %get-tuple-element.62.gate_at, s32[480]{0:T(512)S(1)} %get-tuple-element.61.up_at, ...), custom_call_target="tpu_custom_call", output_to_operand_aliasing={{0}: (5, {}), {1}: (6, {}), {2}: (7, {})} | custom-call | flops 4026531840 | bytes 8388608 | tf_op jit(solution)/shard_map/pallas_call | solution.py:181
  98.1 5.6 %shard_map.122.rest_0_ = f32[384,5120]{1,0:T(8,128)S(1)} custom-call(s32[480]{0:T(512)S(1)} %select_reduce_fusion.2.down_at, bf16[384,1536]{1,0:T(8,128)(2,1)S(1)} %get-tuple-element.26.hidden.left_ref, bf16[121,128,128]{2,1,0:T(8,128)(2,1)S(1)} %concatenate.34.down_w), custom_call_target="tpu_custom_call" | custom-call | flops 3019898880 | bytes 8388608 | tf_op jit(solution)/shard_map/pallas_call | solution.py:181
  103.8 5.6 %shard_map.123 = f32[384,5120]{1,0:T(8,128)S(1)} custom-call(s32[480]{0:T(512)S(1)} %select_reduce_fusion.2.down_at, bf16[384,1536]{1,0:T(8,128)(2,1)S(1)} %get-tuple-element.26.hidden.left_ref, bf16[121,128,128]{2,1,0:T(8,128)(2,1)S(1)} %concatenate.34.down_w, f32[384,5120]{1,0:T(8,128)S(1)} %shard_map.122.rest_0_), custom_call_target="tpu_custom_call", output_to_operand_aliasing={{}: (3, {})} | custom-call | flops 3019898880 | bytes 8388608 | tf_op jit(solution)/shard_map/pallas_call | solution.py:181
  119.0 6.1 %shard_map.124 = (bf16[384,1536]{1,0:T(8,128)(2,1)S(1)}, bf16[384,1536]{1,0:T(8,128)(2,1)S(1)}) custom-call(s32[480]{0:T(512)S(1)} %select_reduce_fusion.2.down_at, bf16[384,5120]{1,0:T(8,128)(2,1)S(1)} %constant_dynamic-update-slice_fusion.9.g.right_ref, bf16[121,128,128]{2,1,0:T(8,128)(2,1)} %copy-done, f32[384,1536]{1,0:T(8,128)S(1)} %get-tuple-element.27.act, ...), custom_call_target="tpu_custom_call" | custom-call | flops 2013265920 | bytes 8388608 | tf_op jit(solution)/shard_map/pallas_call | solution.py:181
  125.1 4.8 %shard_map.125 = (bf16[384,1536]{1,0:T(8,128)(2,1)S(1)}, bf16[384,1536]{1,0:T(8,128)(2,1)S(1)}) custom-call(s32[480]{0:T(512)S(1)} %select_reduce_fusion.2.down_at, bf16[384,5120]{1,0:T(8,128)(2,1)S(1)} %constant_dynamic-update-slice_fusion.9.g.right_ref, bf16[121,128,128]{2,1,0:T(8,128)(2,1)} %copy-done, ...), custom_call_target="tpu_custom_call", output_to_operand_aliasing={{0}: (5, {}), {1}: (6, {})} | custom-call | flops 2013265920 | bytes 8388608 | tf_op jit(solution)/shard_map/pallas_call | solution.py:181
  132.0 4.9 %shard_map.126 = (bf16[384,1536]{1,0:T(8,128)(2,1)S(1)}, bf16[384,1536]{1,0:T(8,128)(2,1)S(1)}) custom-call(s32[480]{0:T(512)S(1)} %select_reduce_fusion.2.down_at, bf16[384,5120]{1,0:T(8,128)(2,1)S(1)} %copy-done.8, bf16[121,128,128]{2,1,0:T(8,128)(2,1)} %copy-done, ...), custom_call_target="tpu_custom_call", output_to_operand_aliasing={{0}: (5, {}), {1}: (6, {})} | custom-call | flops 2013265920 | bytes 8388608 | tf_op jit(solution)/shard_map/pallas_call | solution.py:181
  136.9 9.8 %shard_map.127.rest_0_ = f32[384,5120]{1,0:T(8,128)} custom-call(s32[480]{0:T(512)S(1)} %get-tuple-element.62.gate_at, s32[480]{0:T(512)S(1)} %get-tuple-element.61.up_at, bf16[384,1536]{1,0:T(8,128)(2,1)S(1)} %get-tuple-element.33.gate_grad.right_ref, bf16[384,1536]{1,0:T(8,128)(2,1)S(1)} %get-tuple-element.34.up_grad.right_ref, ...), custom_call_target="tpu_custom_call" | custom-call | flops 6039797760 | bytes 8388608 | tf_op jit(solution)/shard_map/pallas_call | solution.py:181
  146.7 9.8 %shard_map.128 = f32[384,5120]{1,0:T(8,128)} custom-call(s32[480]{0:T(512)S(1)} %get-tuple-element.62.gate_at, s32[480]{0:T(512)S(1)} %get-tuple-element.61.up_at, bf16[384,1536]{1,0:T(8,128)(2,1)S(1)} %get-tuple-element.33.gate_grad.right_ref, bf16[384,1536]{1,0:T(8,128)(2,1)S(1)} %get-tuple-element.34.up_grad.right_ref, ...), custom_call_target="tpu_custom_call", output_to_operand_aliasing={{}: (6, {})} | custom-call | flops 6039797760 | bytes 8388608 | tf_op jit(solution)/shard_map/pallas_call | solution.py:181
  168.2 4.8 %shard_map.131 = bf16[60,128,128]{2,1,0:T(8,128)(2,1)} custom-call(s32[60]{0:T(128)S(1)} %get-tuple-element.57.at, bf16[384,5120]{1,0:T(8,128)(2,1)S(1)} %copy-done.14, bf16[384,1536]{1,0:T(8,128)(2,1)S(1)} %get-tuple-element.34.up_grad.right_ref), custom_call_target="tpu_custom_call" | custom-call | flops 3019898880 | bytes 8388608 | tf_op jit(solution)/shard_map/pallas_call | solution.py:230
  182.3 10.0 %collective-permute-done.9 = bf16[48,5120]{1,0:T(8,128)(2,1)S(1)} collective-permute-done((bf16[48,5120]{1,0:T(8,128)(2,1)S(1)}, bf16[48,5120]{1,0:T(8,128)(2,1)S(1)}, u32[]{:S(2)}, u32[]{:S(2)}) %collective-permute-start.9) | collective-permute-done | bytes 491552 | tf_op jit(solution)/shard_map/ppermute | solution.py:30
  194.6 10.5 %collective-permute-done.25 = bf16[48,5120]{1,0:T(8,128)(2,1)S(1)} collective-permute-done((bf16[48,5120]{1,0:T(8,128)(2,1)S(1)}, bf16[48,5120]{1,0:T(8,128)(2,1)S(1)}, u32[]{:S(2)}, u32[]{:S(2)}) %collective-permute-start.25) | collective-permute-done | bytes 491552 | tf_op jit(solution)/shard_map/ppermute | solution.py:30
  208.9 8.1 %collective-permute-done.10 = bf16[48,5120]{1,0:T(8,128)(2,1)S(1)} collective-permute-done((bf16[48,5120]{1,0:T(8,128)(2,1)S(1)}, bf16[48,5120]{1,0:T(8,128)(2,1)S(1)}, u32[]{:S(2)}, u32[]{:S(2)}) %collective-permute-start.10) | collective-permute-done | bytes 491552 | tf_op jit(solution)/shard_map/ppermute | solution.py:30
  219.2 8.7 %collective-permute-done.26 = bf16[48,5120]{1,0:T(8,128)(2,1)S(1)} collective-permute-done((bf16[48,5120]{1,0:T(8,128)(2,1)S(1)}, bf16[48,5120]{1,0:T(8,128)(2,1)S(1)}, u32[]{:S(2)}, u32[]{:S(2)}) %collective-permute-start.26) | collective-permute-done | bytes 491552 | tf_op jit(solution)/shard_map/ppermute | solution.py:30
  234.3 5.5 %collective-permute-done.15 = bf16[48,5120]{1,0:T(8,128)(2,1)S(1)} collective-permute-done((bf16[48,5120]{1,0:T(8,128)(2,1)S(1)}, bf16[48,5120]{1,0:T(8,128)(2,1)S(1)}, u32[]{:S(2)}, u32[]{:S(2)}) %collective-permute-start.15) | collective-permute-done | bytes 491552 | tf_op jit(solution)/shard_map/ppermute | solution.py:33
  242.7 7.9 %collective-permute-done.31 = bf16[48,5120]{1,0:T(8,128)(2,1)S(1)} collective-permute-done((bf16[48,5120]{1,0:T(8,128)(2,1)S(1)}, bf16[48,5120]{1,0:T(8,128)(2,1)S(1)}, u32[]{:S(2)}, u32[]{:S(2)}) %collective-permute-start.31) | collective-permute-done | bytes 491552 | tf_op jit(solution)/shard_map/ppermute | solution.py:33
  252.8 6.4 %shard_map.130 = f32[60,128,128]{2,1,0:T(8,128)} custom-call(s32[60]{0:T(128)S(1)} %get-tuple-element.63.at, bf16[384,5120]{1,0:T(8,128)(2,1)S(1)} %copy-done.14, bf16[384,1536]{1,0:T(8,128)(2,1)S(1)} %get-tuple-element.33.gate_grad.right_ref, bf16[60,128,128]{2,1,0:T(8,128)(2,1)} %collective-permute-done.32.rest_0_), custom_call_target="tpu_custom_call" | custom-call | flops 3019898880 | bytes 8388608 | tf_op jit(solution)/shard_map/pallas_call | solution.py:230
  259.3 6.4 %shard_map.132 = f32[60,128,128]{2,1,0:T(8,128)} custom-call(s32[60]{0:T(128)S(1)} %get-tuple-element.58.at, bf16[384,5120]{1,0:T(8,128)(2,1)S(1)} %copy-done.14, bf16[384,1536]{1,0:T(8,128)(2,1)S(1)} %get-tuple-element.34.up_grad.right_ref, bf16[60,128,128]{2,1,0:T(8,128)(2,1)} %collective-permute-done.33.rest_0_), custom_call_target="tpu_custom_call" | custom-call | flops 3019898880 | bytes 8388608 | tf_op jit(solution)/shard_map/pallas_call | solution.py:230
  265.7 6.4 %shard_map.134 = f32[60,128,128]{2,1,0:T(8,128)} custom-call(s32[60]{0:T(128)S(1)} %get-tuple-element.56.at, bf16[384,1536]{1,0:T(8,128)(2,1)S(1)} %copy-done.11, bf16[384,5120]{1,0:T(8,128)(2,1)S(1)} %copy-done.9, bf16[60,128,128]{2,1,0:T(8,128)(2,1)} %collective-permute-done.34.rest_0_), custom_call_target="tpu_custom_call" | custom-call | flops 3019898880 | bytes 8388608 | tf_op jit(solution)/shard_map/pallas_call | solution.py:230
  (148 shorter events, 94.5 us)
Async XLA Ops:
  0.6 18.2 %collective-permute-start = (bf16[48,5120]{1,0:T(8,128)(2,1)}, bf16[48,5120]{1,0:T(8,128)(2,1)S(1)}, u32[]{:S(2)}, u32[]{:S(2)}) collective-permute-start(bf16[48,5120]{1,0:T(8,128)(2,1)} %param.8), channel_id=1, source_target_pairs={{0,4},{4,8},{8,12},{12,14},{14,10},{10,6},{6,2},{2,0},{1,5},{5,9},... | collective-permute-start | bytes 1474568 | tf_op jit(solution)/shard_map/ppermute | solution.py:30
  3.7 17.2 %collective-permute-start.1 = (bf16[48,5120]{1,0:T(8,128)(2,1)}, bf16[48,5120]{1,0:T(8,128)(2,1)S(1)}, u32[]{:S(2)}, u32[]{:S(2)}) collective-permute-start(bf16[48,5120]{1,0:T(8,128)(2,1)} %param.8), channel_id=1, source_target_pairs={{4,0},{8,4},{12,8},{14,12},{10,14},{6,10},{2,6},{0,2},{5,1},{9,5},... | collective-permute-start | bytes 1474568 | tf_op jit(solution)/shard_map/ppermute | solution.py:33
  3.7 22.7 %collective-permute-start.16 = (bf16[48,5120]{1,0:T(8,128)(2,1)}, bf16[48,5120]{1,0:T(8,128)(2,1)S(1)}, u32[]{:S(2)}, u32[]{:S(2)}) collective-permute-start(bf16[48,5120]{1,0:T(8,128)(2,1)} %param.9), channel_id=1, source_target_pairs={{0,4},{4,8},{8,12},{12,14},{14,10},{10,6},{6,2},{2,0},{1,5},{5,9},... | collective-permute-start | bytes 1474568 | tf_op jit(solution)/shard_map/ppermute | solution.py:30
  5.7 22.9 %collective-permute-start.17 = (bf16[48,5120]{1,0:T(8,128)(2,1)}, bf16[48,5120]{1,0:T(8,128)(2,1)S(1)}, u32[]{:S(2)}, u32[]{:S(2)}) collective-permute-start(bf16[48,5120]{1,0:T(8,128)(2,1)} %param.9), channel_id=1, source_target_pairs={{4,0},{8,4},{12,8},{14,12},{10,14},{6,10},{2,6},{0,2},{5,1},{9,5},... | collective-permute-start | bytes 1474568 | tf_op jit(solution)/shard_map/ppermute | solution.py:33
  18.8 18.2 %collective-permute-start.2 = (bf16[48,5120]{1,0:T(8,128)(2,1)S(1)}, bf16[48,5120]{1,0:T(8,128)(2,1)S(1)}, u32[]{:S(2)}, u32[]{:S(2)}) collective-permute-start(bf16[48,5120]{1,0:T(8,128)(2,1)S(1)} %collective-permute-done), channel_id=1, source_target_pairs={{0,4},{4,8},{8,12},{12,14},{14,10},{10,6},{6,2},{2,0},{1,5},{5,9},... | collective-permute-start | bytes 1474568 | tf_op jit(solution)/shard_map/ppermute | solution.py:30
  20.9 18.2 %collective-permute-start.3 = (bf16[48,5120]{1,0:T(8,128)(2,1)S(1)}, bf16[48,5120]{1,0:T(8,128)(2,1)S(1)}, u32[]{:S(2)}, u32[]{:S(2)}) collective-permute-start(bf16[48,5120]{1,0:T(8,128)(2,1)S(1)} %collective-permute-done.1), channel_id=1, source_target_pairs={{4,0},{8,4},{12,8},{14,12},{10,14},{6,10},{2,6},{0,2},{5,1},{9,5},... | collective-permute-start | bytes 1474568 | tf_op jit(solution)/shard_map/ppermute | solution.py:33
  26.4 21.1 %collective-permute-start.18 = (bf16[48,5120]{1,0:T(8,128)(2,1)S(1)}, bf16[48,5120]{1,0:T(8,128)(2,1)S(1)}, u32[]{:S(2)}, u32[]{:S(2)}) collective-permute-start(bf16[48,5120]{1,0:T(8,128)(2,1)S(1)} %collective-permute-done.16), channel_id=1, source_target_pairs={{0,4},{4,8},{8,12},{12,14},{14,10},{10,6},{6,2},{2,0},{1,5},{5,9},... | collective-permute-start | bytes 1474568 | tf_op jit(solution)/shard_map/ppermute | solution.py:30
  28.6 21.1 %collective-permute-start.19 = (bf16[48,5120]{1,0:T(8,128)(2,1)S(1)}, bf16[48,5120]{1,0:T(8,128)(2,1)S(1)}, u32[]{:S(2)}, u32[]{:S(2)}) collective-permute-start(bf16[48,5120]{1,0:T(8,128)(2,1)S(1)} %collective-permute-done.17), channel_id=1, source_target_pairs={{4,0},{8,4},{12,8},{14,12},{10,14},{6,10},{2,6},{0,2},{5,1},{9,5},... | collective-permute-start | bytes 1474568 | tf_op jit(solution)/shard_map/ppermute | solution.py:33
  37.0 21.1 %collective-permute-start.4 = (bf16[48,5120]{1,0:T(8,128)(2,1)S(1)}, bf16[48,5120]{1,0:T(8,128)(2,1)S(1)}, u32[]{:S(2)}, u32[]{:S(2)}) collective-permute-start(bf16[48,5120]{1,0:T(8,128)(2,1)S(1)} %collective-permute-done.2), channel_id=1, source_target_pairs={{0,4},{4,8},{8,12},{12,14},{14,10},{10,6},{6,2},{2,0},{1,5},{5,9},... | collective-permute-start | bytes 1474568 | tf_op jit(solution)/shard_map/ppermute | solution.py:30
  39.1 21.1 %collective-permute-start.5 = (bf16[48,5120]{1,0:T(8,128)(2,1)S(1)}, bf16[48,5120]{1,0:T(8,128)(2,1)S(1)}, u32[]{:S(2)}, u32[]{:S(2)}) collective-permute-start(bf16[48,5120]{1,0:T(8,128)(2,1)S(1)} %collective-permute-done.3), channel_id=1, source_target_pairs={{4,0},{8,4},{12,8},{14,12},{10,14},{6,10},{2,6},{0,2},{5,1},{9,5},... | collective-permute-start | bytes 1474568 | tf_op jit(solution)/shard_map/ppermute | solution.py:33
  47.5 21.1 %collective-permute-start.20 = (bf16[48,5120]{1,0:T(8,128)(2,1)S(1)}, bf16[48,5120]{1,0:T(8,128)(2,1)S(1)}, u32[]{:S(2)}, u32[]{:S(2)}) collective-permute-start(bf16[48,5120]{1,0:T(8,128)(2,1)S(1)} %collective-permute-done.18), channel_id=1, source_target_pairs={{0,4},{4,8},{8,12},{12,14},{14,10},{10,6},{6,2},{2,0},{1,5},{5,9},... | collective-permute-start | bytes 1474568 | tf_op jit(solution)/shard_map/ppermute | solution.py:30
  49.7 21.1 %collective-permute-start.21 = (bf16[48,5120]{1,0:T(8,128)(2,1)S(1)}, bf16[48,5120]{1,0:T(8,128)(2,1)S(1)}, u32[]{:S(2)}, u32[]{:S(2)}) collective-permute-start(bf16[48,5120]{1,0:T(8,128)(2,1)S(1)} %collective-permute-done.19), channel_id=1, source_target_pairs={{4,0},{8,4},{12,8},{14,12},{10,14},{6,10},{2,6},{0,2},{5,1},{9,5},... | collective-permute-start | bytes 1474568 | tf_op jit(solution)/shard_map/ppermute | solution.py:33
  58.1 15.8 %collective-permute-start.6 = (bf16[24,5120]{1,0:T(8,128)(2,1)S(1)}, bf16[24,5120]{1,0:T(8,128)(2,1)S(1)}, u32[]{:S(2)}, u32[]{:S(2)}) collective-permute-start(bf16[24,5120]{1,0:T(8,128)(2,1)S(1)} %slice.132), channel_id=1, source_target_pairs={{0,4},{4,8},{8,12},{12,14},{14,10},{10,6},{6,2},{2,0},{1,5},{5,9},... | collective-permute-start | bytes 737288 | tf_op jit(solution)/shard_map/ppermute | solution.py:30
  60.3 15.7 %collective-permute-start.7 = (bf16[24,5120]{1,0:T(8,128)(2,1)S(1)}, bf16[24,5120]{1,0:T(8,128)(2,1)S(1)}, u32[]{:S(2)}, u32[]{:S(2)}) collective-permute-start(bf16[24,5120]{1,0:T(8,128)(2,1)S(1)} %slice.133), channel_id=1, source_target_pairs={{4,0},{8,4},{12,8},{14,12},{10,14},{6,10},{2,6},{0,2},{5,1},{9,5},... | collective-permute-start | bytes 737288 | tf_op jit(solution)/shard_map/ppermute | solution.py:33
  68.6 50.4 %collective-permute-start.22 = (bf16[24,5120]{1,0:T(8,128)(2,1)S(1)}, bf16[24,5120]{1,0:T(8,128)(2,1)S(1)}, u32[]{:S(2)}, u32[]{:S(2)}) collective-permute-start(bf16[24,5120]{1,0:T(8,128)(2,1)S(1)} %slice.145), channel_id=1, source_target_pairs={{0,4},{4,8},{8,12},{12,14},{14,10},{10,6},{6,2},{2,0},{1,5},{5,9},... | collective-permute-start | bytes 737288 | tf_op jit(solution)/shard_map/ppermute | solution.py:30
  70.8 48.2 %collective-permute-start.23 = (bf16[24,5120]{1,0:T(8,128)(2,1)S(1)}, bf16[24,5120]{1,0:T(8,128)(2,1)S(1)}, u32[]{:S(2)}, u32[]{:S(2)}) collective-permute-start(bf16[24,5120]{1,0:T(8,128)(2,1)S(1)} %slice.146), channel_id=1, source_target_pairs={{4,0},{8,4},{12,8},{14,12},{10,14},{6,10},{2,6},{0,2},{5,1},{9,5},... | collective-permute-start | bytes 737288 | tf_op jit(solution)/shard_map/ppermute | solution.py:33
  116.9 59.8 %collective-permute-start.8 = (bf16[24,5120]{1,0:T(8,128)(2,1)}, bf16[24,5120]{1,0:T(8,128)(2,1)}, u32[]{:S(2)}, u32[]{:S(2)}) collective-permute-start(bf16[24,5120]{1,0:T(8,128)(2,1)} %get-tuple-element.51), channel_id=1, source_target_pairs={{0,4},{4,8},{8,12},{12,14},{14,10},{10,6},{6,2},{2,0},{1,5},{5,9},... | collective-permute-start | bytes 737288 | tf_op jit(solution)/shard_map/ppermute | solution.py:30
  118.5 58.8 %collective-permute-start.12 = (bf16[24,5120]{1,0:T(8,128)(2,1)}, bf16[24,5120]{1,0:T(8,128)(2,1)}, u32[]{:S(2)}, u32[]{:S(2)}) collective-permute-start(bf16[24,5120]{1,0:T(8,128)(2,1)} %get-tuple-element.52), channel_id=1, source_target_pairs={{4,0},{8,4},{12,8},{14,12},{10,14},{6,10},{2,6},{0,2},{5,1},{9,5},... | collective-permute-start | bytes 737288 | tf_op jit(solution)/shard_map/ppermute | solution.py:33
  161.4 17.3 %collective-permute-start.24 = (bf16[24,5120]{1,0:T(8,128)(2,1)}, bf16[24,5120]{1,0:T(8,128)(2,1)}, u32[]{:S(2)}, u32[]{:S(2)}) collective-permute-start(bf16[24,5120]{1,0:T(8,128)(2,1)} %get-tuple-element.47), channel_id=1, source_target_pairs={{0,4},{4,8},{8,12},{12,14},{14,10},{10,6},{6,2},{2,0},{1,5},{5,9},... | collective-permute-start | bytes 737288 | tf_op jit(solution)/shard_map/ppermute | solution.py:30
  163.0 17.4 %collective-permute-start.28 = (bf16[24,5120]{1,0:T(8,128)(2,1)}, bf16[24,5120]{1,0:T(8,128)(2,1)}, u32[]{:S(2)}, u32[]{:S(2)}) collective-permute-start(bf16[24,5120]{1,0:T(8,128)(2,1)} %get-tuple-element.48), channel_id=1, source_target_pairs={{4,0},{8,4},{12,8},{14,12},{10,14},{6,10},{2,6},{0,2},{5,1},{9,5},... | collective-permute-start | bytes 737288 | tf_op jit(solution)/shard_map/ppermute | solution.py:33
  168.1 84.7 %collective-permute-start.32 = (bf16[60,128,128]{2,1,0:T(8,128)(2,1)}, bf16[60,128,128]{2,1,0:T(8,128)(2,1)}, u32[]{:S(2)}, u32[]{:S(2)}) collective-permute-start(bf16[60,128,128]{2,1,0:T(8,128)(2,1)} %shard_map.129), channel_id=1, source_target_pairs={{0,1},{1,0},{2,3},{3,2},{4,5},{5,4},{6,7},{7,6},{8,9},{9,8},{10,11... | collective-permute-start | bytes 5898248 | tf_op jit(solution)/shard_map/ppermute | solution.py:309
  176.8 82.5 %collective-permute-start.33 = (bf16[60,128,128]{2,1,0:T(8,128)(2,1)}, bf16[60,128,128]{2,1,0:T(8,128)(2,1)}, u32[]{:S(2)}, u32[]{:S(2)}) collective-permute-start(bf16[60,128,128]{2,1,0:T(8,128)(2,1)} %shard_map.131), channel_id=1, source_target_pairs={{0,1},{1,0},{2,3},{3,2},{4,5},{5,4},{6,7},{7,6},{8,9},{9,8},{10,11... | collective-permute-start | bytes 5898248 | tf_op jit(solution)/shard_map/ppermute | solution.py:309
  177.3 88.4 %collective-permute-start.34 = (bf16[60,128,128]{2,1,0:T(8,128)(2,1)S(1)}, bf16[60,128,128]{2,1,0:T(8,128)(2,1)}, u32[]{:S(2)}, u32[]{:S(2)}) collective-permute-start(bf16[60,128,128]{2,1,0:T(8,128)(2,1)S(1)} %shard_map.133), channel_id=1, source_target_pairs={{0,1},{1,0},{2,3},{3,2},{4,5},{5,4},{6,7},{7,6},{8,9},{9,8},{10,11... | collective-permute-start | bytes 5898248 | tf_op jit(solution)/shard_map/ppermute | solution.py:309
  178.7 13.6 %collective-permute-start.9 = (bf16[48,5120]{1,0:T(8,128)(2,1)S(1)}, bf16[48,5120]{1,0:T(8,128)(2,1)S(1)}, u32[]{:S(2)}, u32[]{:S(2)}) collective-permute-start(bf16[48,5120]{1,0:T(8,128)(2,1)S(1)} %pad_maximum_fusion), channel_id=1, source_target_pairs={{0,4},{4,8},{8,12},{12,14},{14,10},{10,6},{6,2},{2,0},{1,5},{5,9},... | collective-permute-start | bytes 1474568 | tf_op jit(solution)/shard_map/ppermute | solution.py:30
  (31 other events, 323.5 us)

commit v2 on v1

v2 whole, which is shorter than its diff:
```python
import functools

import jax
import jax.numpy as jnp
from jax import lax
from jax.experimental import pallas as pl
from jax.experimental.pallas import tpu as pltpu
from jax.sharding import PartitionSpec as P

FF = 12288

SMEM_SPEC = pl.BlockSpec(memory_space=pltpu.SMEM)
WHOLE = "whole"
ANY_SPEC = pl.BlockSpec(memory_space=pl.ANY)


def ring_order(size):
    return list(range(0, size, 2)) + list(range(1, size, 2))[::-1]


def ring_shifts(size):
    order = ring_order(size)
    ahead = [(order[i], order[(i + 1) % size]) for i in range(size)]
    back = [(b, a) for a, b in ahead]

    def to_right(value):
        return lax.ppermute(value, "tensor", ahead)

    def to_left(value):
        return lax.ppermute(value, "tensor", back)

    return to_right, to_left


def after_all(values, events):
    values = tuple(values)
    return lax.optimization_barrier(values + tuple(events))[:len(values)] if events else values


class Gather:
    def __init__(self, rows, size):
        self.to_right, self.to_left = ring_shifts(size)
        self.half = rows.shape[0] // 2
        self.last = size // 2 - 1
        self.blocks = [rows]
        self.from_left = self.from_right = rows
        self.taken = 0

    def step(self, events=()):
        left, right = after_all((self.from_left, self.from_right), events)
        if self.taken == self.last:
            left, right = left[:self.half], right[self.half:]
        self.from_left, self.from_right = self.to_right(left), self.to_left(right)
        self.blocks += [self.from_left, self.from_right]
        self.taken += 1
        return self.from_left, self.from_right

    def result(self, events=()):
        return jnp.concatenate(after_all(self.blocks, events), axis=0)


class Scatter:
    def __init__(self, near, far, size):
        self.to_right, self.to_left = ring_shifts(size)
        self.near = near
        self.rows = far.shape[0]
        self.half = self.rows // 2
        self.distance = size // 2
        self.right, self.left = far[:self.half], far[self.half:]

    def block(self, place):
        return self.near[place * self.rows:(place + 1) * self.rows]

    def step(self, events=()):
        right, left = after_all((self.right, self.left), events)
        right, left = self.to_right(right), self.to_left(left)
        self.distance -= 1
        self.right, self.left = right, left
        if self.distance > 0:
            if right.shape[0] == self.half:
                none = jnp.zeros_like(right)
                right = jnp.concatenate([right, none], axis=0)
                left = jnp.concatenate([none, left], axis=0)
            right = right.astype(jnp.float32) + self.block(2 * self.distance)
            left = left.astype(jnp.float32) + self.block(2 * self.distance - 1)
            self.right, self.left = right.astype(jnp.bfloat16), left.astype(jnp.bfloat16)
        return self.right, self.left

    def result(self):
        total = self.block(0) + self.right.astype(jnp.float32) + self.left.astype(jnp.float32)
        return total.astype(jnp.bfloat16)


def slot_table(index, slots):
    count = index.shape[0]
    hit = index[None, :] == jnp.arange(slots, dtype=jnp.int32)[:, None]
    return jnp.min(jnp.where(hit, jnp.arange(count, dtype=jnp.int32)[None, :], count), axis=1)


def with_zero(blocks):
    return jnp.concatenate([blocks, jnp.zeros((1,) + blocks.shape[1:], blocks.dtype)], axis=0)


def columns_of(lhs, weights, place, first, depth, b):
    strip = jnp.concatenate(
        [
            jnp.concatenate([weights[place(first + n, m)] for n in range(2)], axis=1)
            for m in range(depth)
        ],
        axis=0,
    )
    return jnp.dot(lhs, strip, preferred_element_type=jnp.float32)


def columns_of_turned(lhs, weights, place, first, depth, b):
    strip = jnp.concatenate(
        [
            jnp.concatenate([weights[place(first + n, m)] for m in range(depth)], axis=1)
            for n in range(2)
        ],
        axis=0,
    )
    return lax.dot_general(
        lhs, strip, (((1,), (1,)), ((), ())), preferred_element_type=jnp.float32
    )


def hidden_kernel(dim_blocks, offset, gate_at, up_at, x, gate_w, up_w, *rest):
    hidden, act, slope = rest[-4:-1]
    first = (offset + pl.program_id(0)) * 2
    b = gate_w.shape[1]

    def strip(at, w):
        return columns_of(
            x[...], w, lambda n, m: at[n * dim_blocks + m], first, dim_blocks, b
        )

    gate = strip(gate_at, gate_w)
    up = strip(up_at, up_w)
    sig = jax.nn.sigmoid(gate)
    activated = gate * sig
    hidden[...] = (activated * up).astype(jnp.bfloat16)
    act[...] = activated
    slope[...] = up * sig * (1.0 + gate * (1.0 - sig))


def grads_kernel(dim_blocks, offset, down_at, g, down_w, act, slope, *rest):
    gate_grad, up_grad = rest[-3:-1]
    first = (offset + pl.program_id(0)) * 2
    b = down_w.shape[1]
    hidden_grad = columns_of_turned(
        g[...], down_w, lambda n, m: down_at[n * dim_blocks + m], first, dim_blocks, b
    )
    gate_grad[...] = (hidden_grad * slope[...]).astype(jnp.bfloat16)
    up_grad[...] = (hidden_grad * act[...]).astype(jnp.bfloat16)


def split_rows(value, near, far):
    rows = near.shape[0]
    near[...] = value[:rows]
    far[...] = value[rows:].astype(far.dtype)


def output_kernel(dim_blocks, columns, offset, down_at, hidden, down_w, *rest):
    first = (offset + pl.program_id(0)) * 2
    split_rows(
        columns_of(
            hidden[...], down_w, lambda n, m: down_at[m * dim_blocks + n], first, columns,
            down_w.shape[1],
        ),
        *rest[-3:-1],
    )


def input_grad_kernel(
    dim_blocks, columns, offset, gate_at, up_at, gate_grad, up_grad, gate_w, up_w, *rest
):
    first = (offset + pl.program_id(0)) * 2
    b = gate_w.shape[1]

    def strip(lhs, at, w):
        return columns_of_turned(
            lhs[...], w, lambda n, m: at[m * dim_blocks + n], first, columns, b
        )

    split_rows(
        strip(gate_grad, gate_at, gate_w) + strip(up_grad, up_at, up_w), *rest[-3:-1]
    )


def whole_spec(array):
    zeros = (0,) * len(array.shape)
    return pl.BlockSpec(array.shape, lambda i: zeros, pipeline_mode=pl.Buffered(1))


def room(arrays, spare):
    held = sum(a.dtype.itemsize * a.size for a in arrays)
    return pltpu.CompilerParams(vmem_limit_bytes=held + spare * 2**20)


class Strips:
    def __init__(self, kernel, inputs, specs, total, block_outs, flops):
        self.kernel, self.inputs, self.specs = kernel, inputs, specs
        self.total, self.block_outs, self.flops = total, block_outs, flops
        self.outs = []
        self.done = 0

    def run(self, share, events=()):
        offset = self.done
        count = round(self.total * share) - offset
        self.done += count

        def strip_spec(array):
            return pl.BlockSpec((array.shape[0], 2 * 128), lambda i: (0, offset + i))

        inputs = [*after_all(self.inputs[:1], events), *self.inputs[1:], *self.outs]
        in_specs = [
            strip_spec(array) if spec is None else whole_spec(array) if spec is WHOLE else spec
            for array, spec in zip(inputs, self.specs)
        ] + [ANY_SPEC] * len(self.outs)
        first_out = len(self.inputs)

        def kernel(*refs):
            self.kernel(offset, *refs)
            refs[-1][...] = jnp.zeros_like(refs[-1])

        *outs, token = pl.pallas_call(
            kernel,
            grid=(count,),
            in_specs=in_specs,
            out_specs=[strip_spec(out) for out in self.block_outs]
            + [pl.BlockSpec((8, 128), lambda i: (0, 0))],
            out_shape=list(self.block_outs) + [jax.ShapeDtypeStruct((8, 128), jnp.int32)],
            input_output_aliases={first_out + i: i for i in range(len(self.outs))},
            compiler_params=room(
                [array for array, spec in zip(inputs, self.specs) if spec is WHOLE], 12
            ),
            cost_estimate=pl.CostEstimate(
                flops=2 * self.flops * count // self.total, bytes_accessed=8 * 2**20,
                transcendentals=0,
            ),
        )(*inputs)
        self.outs = outs
        return (token,)


def block_grads(left, right, index, dim_blocks, left_is_model, arrived, scale):
    count = index.shape[0]
    rows = left.shape[0]
    b = 128
    group = max(d for d in range(1, 13) if count % d == 0)

    def kernel(at, left_ref, right_ref, *rest):
        out = rest[-1]
        base = pl.program_id(0) * group
        for i in range(group):
            slot = at[base + i]
            model, hidden = slot % dim_blocks, slot // dim_blocks
            a, c = (model, hidden) if left_is_model else (hidden, model)
            value = lax.dot_general(
                left_ref[:, pl.ds(pl.multiple_of(a * b, b), b)],
                right_ref[:, pl.ds(pl.multiple_of(c * b, b), b)],
                (((0,), (0,)), ((), ())),
                preferred_element_type=jnp.float32,
            )
            if arrived is not None:
                value = (value + rest[0][i].astype(jnp.float32)) * scale
            out[i] = value.astype(out.dtype)

    spec = pl.BlockSpec((group, b, b), lambda i: (i, 0, 0))
    extra = [] if arrived is None else [arrived]
    dtype = jnp.bfloat16 if arrived is None else jnp.float32
    return pl.pallas_call(
        kernel,
        grid=(count // group,),
        in_specs=[SMEM_SPEC, whole_spec(left), whole_spec(right)] + [spec] * len(extra),
        out_specs=spec,
        out_shape=jax.ShapeDtypeStruct((count, b, b), dtype),
        compiler_params=room([left, right], 10),
        cost_estimate=pl.CostEstimate(
            flops=8 * count * rows * b * b, bytes_accessed=8 * 2**20, transcendentals=0
        ),
    )(index, left, right, *extra)


def body(
    tokens_in, grad_out, gate_blocks, up_blocks, down_blocks, gate_index, up_index, down_index
):
    block_size = gate_blocks.shape[1]
    model_width = tokens_in.shape[1]
    dim_blocks = model_width // block_size
    owners = lax.axis_size("tensor")
    columns = FF // (block_size * owners)
    width = columns * block_size
    token_count = tokens_in.shape[0] * owners
    count = gate_blocks.shape[0]
    slots = columns * dim_blocks

    steps = owners // 2
    unit = 2 * token_count * model_width * width
    narrow = jax.ShapeDtypeStruct((token_count, width), jnp.bfloat16)
    wide = jax.ShapeDtypeStruct((token_count, width), jnp.float32)
    held_rows = tokens_in.shape[0]
    totals = [
        jax.ShapeDtypeStruct((token_count - held_rows, model_width), jnp.float32),
        jax.ShapeDtypeStruct((held_rows, model_width), jnp.bfloat16),
    ]

    assert steps % 4 == 0

    def several(chain, quarters, events=()):
        for _ in range(steps * quarters // 4):
            events = chain.step(events)
        return tuple(events)

    x_ring, g_ring = Gather(tokens_in, owners), Gather(grad_out, owners)
    events = several(x_ring, 1)
    gate_at, up_at = slot_table(gate_index, slots), slot_table(up_index, slots)
    gate_w = with_zero(gate_blocks)
    events = several(x_ring, 1, events + (gate_at, up_at, gate_w[-1, :8]))
    up_w = with_zero(up_blocks)
    events = several(x_ring, 1, events + (up_w[-1, :8],))
    down_at, down_w = slot_table(down_index, slots), with_zero(down_blocks)
    events = several(x_ring, 1, events + (down_at, down_w[-1, :8]))
    x = x_ring.result()

    hidden_strips = Strips(
        functools.partial(hidden_kernel, dim_blocks),
        [gate_at, up_at, x, gate_w, up_w],
        [SMEM_SPEC] * 2 + [WHOLE] * 3,
        columns // 2, [narrow, wide, wide], 2 * unit,
    )
    events = several(g_ring, 1, events) + hidden_strips.run(0.5, events)
    events = several(g_ring, 1, events) + hidden_strips.run(1, events)
    hidden, act, slope = hidden_strips.outs
    out_strips = Strips(
        functools.partial(output_kernel, dim_blocks, columns),
        [down_at, hidden, down_w],
        [SMEM_SPEC] + [WHOLE] * 2,
        dim_blocks // 2, totals, unit,
    )
    events = several(g_ring, 1, events) + out_strips.run(1, events)
    out_ring = Scatter(*out_strips.outs, owners)
    events = several(g_ring, 1, events) + several(out_ring, 1)
    g = g_ring.result(events)

    grads_strips = Strips(
        functools.partial(grads_kernel, dim_blocks),
        [down_at, g, down_w, act, slope],
        [SMEM_SPEC] + [WHOLE] * 2 + [None] * 2,
        columns // 2, [narrow, narrow], unit,
    )
    events = several(out_ring, 1, events) + grads_strips.run(1, events)
    gate_grad, up_grad = grads_strips.outs
    in_strips = Strips(
        functools.partial(input_grad_kernel, dim_blocks, columns),
        [gate_at, up_at, gate_grad, up_grad, gate_w, up_w],
        [SMEM_SPEC] * 2 + [WHOLE] * 4,
        dim_blocks // 2, totals, 2 * unit,
    )
    events = several(out_ring, 1, events) + in_strips.run(0.5, events)
    events = several(out_ring, 1, events) + in_strips.run(1, events)
    output = out_ring.result()

    in_ring = Scatter(*in_strips.outs, owners)
    pairs = lax.axis_size("dp")
    share = count // pairs
    me = lax.axis_index("dp")
    scale = 1.0 / float(token_count * pairs) ** 0.5
    work = (
        (hidden, g, down_index, False),
        (x, gate_grad, gate_index, True),
        (x, up_grad, up_index, True),
    )

    def theirs(i, events):
        left, right, index, left_is_model = work[i]
        (held,) = after_all([lax.dynamic_slice(index, ((1 - me) * share,), (share,))], events)
        return block_grads(left, right, held, dim_blocks, left_is_model, None, None)

    def mine(i, arrived, events):
        left, right, index, left_is_model = work[i]
        (held,) = after_all([lax.dynamic_slice(index, (me * share,), (share,))], events)
        return block_grads(left, right, held, dim_blocks, left_is_model, arrived, scale)

    def swap(sent):
        return lax.ppermute(sent, "dp", [(0, 1), (1, 0)])

    sent_down = theirs(0, events)
    events = several(in_ring, 1, events) + (sent_down,)
    down_arrived = swap(sent_down)
    sent = [theirs(1, events), theirs(2, events)]
    events = several(in_ring, 1, events) + (*sent, down_arrived)
    gate_arrived, up_arrived = swap(sent[0]), swap(sent[1])
    down_sum = mine(0, down_arrived, events)
    events = several(in_ring, 1, events) + (down_sum[:1, :8], gate_arrived, up_arrived)
    gate_sum = mine(1, gate_arrived, events)
    up_sum = mine(2, up_arrived, events)
    several(in_ring, 1, events)
    input_grad = in_ring.result()
    return output, input_grad, gate_sum, up_sum, down_sum


def solution(mesh):
    rows = P(("group", "tensor", "dp"), None)
    owned = P("tensor", None, None)
    grads = P(("group", "tensor", "dp"), None, None)
    return jax.shard_map(
        body,
        mesh=mesh,
        in_specs=(rows, rows, owned, owned, owned, P("tensor"), P("tensor"), P("tensor")),
        out_specs=(rows, rows, grads, grads, grads),
        check_vma=False,
    )
```

time: 273 us -> 191 us (0.70)
  waiting for transfers between devices: 94.8 us -> 55.5 us
  Pallas kernels: 101 us -> 83.1 us
  other arithmetic: 17.8 us -> 4.15 us
  local copies, waits for them, and re-layouts: 20 us -> 11.4 us
    ppermute x16, waiting for transfers between devices: 76.9 us -> 33.7 us  [to_right(): return lax.ppermute(value, 'tensor', ahead)]
    pallas_call x16 -> x12, Pallas kernels: 101 us -> 83.1 us  [the longest x6 56.2 us: run(): pl.pallas_call(kernel, grid=(count,), in_specs=in_specs, out_specs=[strip...]
    ppermute x16, starting transfers between devices: 30.5 us -> 21.3 us  [to_right(): return lax.ppermute(value, 'tensor', ahead)]
    another operation x4 -> x0, other arithmetic: 8.97 us -> none
    unnamed x56 -> x36, local copies, waits for them, and re-layouts: 9.68 us -> 1.78 us
    ppermute x16, starting transfers between devices: 5.99 us -> 13.9 us  [to_left(): return lax.ppermute(value, 'tensor', back)]
    ppermute x16, waiting for transfers between devices: 17.9 us -> 21.8 us  [to_left(): return lax.ppermute(value, 'tensor', back)]
    convert_element_type x6 -> x8, other arithmetic: 7.02 us -> 3.13 us  [the longest x2 1.9 us: result(): return total.astype(jnp.bfloat16)]
  transfers between devices with their start and end apart: 35 -> 35, of which waited for: 14 -> 24; matrix products, arithmetic and copies ran while one was open for 11% -> 7% of each run, Pallas kernels for 35% -> 43%
where the time goes in v2:
time: 191 us
  Pallas kernels  83.1 us (44%)
  waiting for transfers between devices  55.5 us (29%)
  starting transfers between devices  35.9 us (19%)
  local copies, waits for them, and re-layouts  11.4 us (6%)
  other arithmetic  4.15 us (2%)
    pallas_call x6, Pallas kernels, run(): pl.pallas_call(kernel, grid=(count,), in_specs=in_specs, out_specs=[strip...  56.2 us
    ppermute x16, waiting for transfers between devices, to_right(): return lax.ppermute(value, 'tensor', ahead)  33.7 us
    pallas_call x6, Pallas kernels, block_grads(): pl.pallas_call(kernel, grid=(count // group,), in_specs=[SMEM_SPEC, whole...  26.8 us
    ppermute x16, waiting for transfers between devices, to_left(): return lax.ppermute(value, 'tensor', back)  21.8 us
    ppermute x16, starting transfers between devices, to_right(): return lax.ppermute(value, 'tensor', ahead)  21.3 us
    ppermute x16, starting transfers between devices, to_left(): return lax.ppermute(value, 'tensor', back)  13.9 us
    concatenate x3, local copies, waits for them, and re-layouts, with_zero(): jnp.concatenate([blocks, jnp.zeros((1,) + blocks.shape[1:], blocks.dtype)...  9.25 us
  transfers between devices with their start and end apart: 35, of which 24 were waited for; matrix products, arithmetic and copies ran while one was open for 7% of the time, Pallas kernels for 43%

profile of v2, /device:TPU:0, one launch (start us, length us, event | category | flops | bytes accessed | tf_op | source)
XLA Modules:
  0.0 191.1 jit_solution(15214562626364523599)
XLA Ops:
  0.6 3.1 %collective-permute-start = (bf16[48,5120]{1,0:T(8,128)(2,1)}, bf16[48,5120]{1,0:T(8,128)(2,1)S(1)}, u32[]{:S(2)}, u32[]{:S(2)}) collective-permute-start(bf16[48,5120]{1,0:T(8,128)(2,1)} %param.8), channel_id=1, source_target_pairs={{0,4},{4,8},{8,12},{12,14},{14,10},{10,6},{6,2},{2,0},{1,5},{5,9},... | collective-permute-start | bytes 1474568 | tf_op jit(solution)/shard_map/ppermute | solution.py:27
  4.5 4.7 %concatenate.28.refs_3_.refs_4_ = bf16[121,128,128]{2,1,0:T(8,128)(2,1)} pad(bf16[120,128,128]{2,1,0:T(8,128)(2,1)} %param.10, bf16[]{:T(256)} %constant.9.clone.1), padding=0_1x0_0x0_0 | pad | bytes 7897090 | tf_op jit(solution)/shard_map/concatenate | solution.py:101
  9.2 2.3 %concatenate.29.refs_4_.refs_5_ = bf16[121,128,128]{2,1,0:T(8,128)(2,1)} pad(bf16[120,128,128]{2,1,0:T(8,128)(2,1)S(1)} %copy-done.3, bf16[]{:T(256)} %constant.9.clone.1), padding=0_1x0_0x0_0 | pad | bytes 7897090 | tf_op jit(solution)/shard_map/concatenate | solution.py:101
  18.7 9.7 %collective-permute-done.2 = bf16[48,5120]{1,0:T(8,128)(2,1)S(1)} collective-permute-done((bf16[48,5120]{1,0:T(8,128)(2,1)S(1)}, bf16[48,5120]{1,0:T(8,128)(2,1)S(1)}, u32[]{:S(2)}, u32[]{:S(2)}) %collective-permute-start.2) | collective-permute-done | bytes 491552 | tf_op jit(solution)/shard_map/ppermute | solution.py:27
  31.8 8.5 %collective-permute-done.4 = bf16[48,5120]{1,0:T(8,128)(2,1)S(1)} collective-permute-done((bf16[48,5120]{1,0:T(8,128)(2,1)S(1)}, bf16[48,5120]{1,0:T(8,128)(2,1)S(1)}, u32[]{:S(2)}, u32[]{:S(2)}) %collective-permute-start.4) | collective-permute-done | bytes 491552 | tf_op jit(solution)/shard_map/ppermute | solution.py:27
  43.8 4.0 %collective-permute-done.6 = bf16[24,5120]{1,0:T(8,128)(2,1)S(1)} collective-permute-done((bf16[24,5120]{1,0:T(8,128)(2,1)S(1)}, bf16[24,5120]{1,0:T(8,128)(2,1)S(1)}, u32[]{:S(2)}, u32[]{:S(2)}) %collective-permute-start.6) | collective-permute-done | bytes 245792 | tf_op jit(solution)/shard_map/ppermute | solution.py:27
  49.9 3.2 %collective-permute-start.8 = (bf16[48,5120]{1,0:T(8,128)(2,1)S(1)}, bf16[48,5120]{1,0:T(8,128)(2,1)S(1)}, u32[]{:S(2)}, u32[]{:S(2)}) collective-permute-start(bf16[48,5120]{1,0:T(8,128)(2,1)S(1)} %copy-done.6), channel_id=1, source_target_pairs={{0,4},{4,8},{8,12},{12,14},{14,10},{10,6},{6,2},{2,0},{1,5},{5,9},... | collective-permute-start | bytes 1474568 | tf_op jit(solution)/shard_map/ppermute | solution.py:27
  53.1 8.2 %shard_map.119 = (bf16[384,1536]{1,0:T(8,128)(2,1)S(1)}, f32[384,1536]{1,0:T(8,128)S(1)}, f32[384,1536]{1,0:T(8,128)S(1)}, s32[8,128]{1,0:T(8,128)}) custom-call(s32[480]{0:T(512)S(1)} %get-tuple-element.121.refs_0_, s32[480]{0:T(512)S(1)} %get-tuple-element.163.refs_1_, bf16[384,5120]{1,0:T(8,128)(2,1)S(1)} %constant_dynamic-update-slice_fusion.refs_2_.left_ref, ...), custom_call_target="tpu_custom_call" | custom-call | flops 12079595520 | bytes 8388608 | tf_op jit(solution)/shard_map/pallas_call | solution.py:227
  61.6 2.8 %collective-permute-done.9 = bf16[48,5120]{1,0:T(8,128)(2,1)S(1)} collective-permute-done((bf16[48,5120]{1,0:T(8,128)(2,1)S(1)}, bf16[48,5120]{1,0:T(8,128)(2,1)S(1)}, u32[]{:S(2)}, u32[]{:S(2)}) %collective-permute-start.9) | collective-permute-done | bytes 491552 | tf_op jit(solution)/shard_map/ppermute | solution.py:30
  66.4 8.2 %shard_map.120 = (bf16[384,1536]{1,0:T(8,128)(2,1)S(1)}, f32[384,1536]{1,0:T(8,128)S(1)}, f32[384,1536]{1,0:T(8,128)S(1)}, s32[8,128]{1,0:T(8,128)}) custom-call(s32[480]{0:T(512)S(1)} %get-tuple-element.121.refs_0_, s32[480]{0:T(512)S(1)} %get-tuple-element.163.refs_1_, ...), custom_call_target="tpu_custom_call", output_to_operand_aliasing={{0}: (5, {}), {1}: (6, {}), {2}: (7, {})} | custom-call | flops 12079595520 | bytes 8388608 | tf_op jit(solution)/shard_map/pallas_call | solution.py:227
  80.0 11.4 %shard_map.121 = (f32[336,5120]{1,0:T(8,128)S(1)}, bf16[48,5120]{1,0:T(8,128)(2,1)S(1)}, s32[8,128]{1,0:T(8,128)}) custom-call(s32[480]{0:T(512)S(1)} %select_reduce_fusion.2.refs_0_, bf16[384,1536]{1,0:T(8,128)(2,1)S(1)} %get-tuple-element.91.refs_1_.left_ref, bf16[121,128,128]{2,1,0:T(8,128)(2,1)S(1)} %copy-done.2), custom_call_target="tpu_custom_call" | custom-call | flops 12079595520 | bytes 8388608 | tf_op jit(solution)/shard_map/pallas_call | solution.py:227
  95.9 4.4 %collective-permute-done.13 = bf16[24,5120]{1,0:T(8,128)(2,1)S(1)} collective-permute-done((bf16[24,5120]{1,0:T(8,128)(2,1)S(1)}, bf16[24,5120]{1,0:T(8,128)(2,1)S(1)}, u32[]{:S(2)}, u32[]{:S(2)}) %collective-permute-start.13) | collective-permute-done | bytes 245792 | tf_op jit(solution)/shard_map/ppermute | solution.py:30
  101.6 4.7 %collective-permute-done.16 = bf16[24,5120]{1,0:T(8,128)(2,1)S(1)} collective-permute-done((bf16[24,5120]{1,0:T(8,128)(2,1)S(1)}, bf16[24,5120]{1,0:T(8,128)(2,1)S(1)}, u32[]{:S(2)}, u32[]{:S(2)}) %collective-permute-start.16) | collective-permute-done | bytes 245792 | tf_op jit(solution)/shard_map/ppermute | solution.py:27
  108.6 9.1 %shard_map.122 = (bf16[384,1536]{1,0:T(8,128)(2,1)S(1)}, bf16[384,1536]{1,0:T(8,128)(2,1)S(1)}, s32[8,128]{1,0:T(8,128)}) custom-call(s32[480]{0:T(512)S(1)} %select_reduce_fusion.2.refs_0_, bf16[384,5120]{1,0:T(8,128)(2,1)S(1)} %constant_dynamic-update-slice_fusion.9.refs_1_.right_ref, bf16[121,128,128]{2,1,0:T(8,128)(2,1)S(1)} %copy-done.2, ...), custom_call_target="tpu_custom_call" | custom-call | flops 12079595520 | bytes 8388608 | tf_op jit(solution)/shard_map/pallas_call | solution.py:227
  121.8 9.7 %shard_map.123 = (f32[336,5120]{1,0:T(8,128)S(1)}, bf16[48,5120]{1,0:T(8,128)(2,1)S(1)}, s32[8,128]{1,0:T(8,128)}) custom-call(s32[480]{0:T(512)S(1)} %get-tuple-element.121.refs_0_, s32[480]{0:T(512)S(1)} %get-tuple-element.163.refs_1_, bf16[384,1536]{1,0:T(8,128)(2,1)S(1)} %get-tuple-element.116.refs_2_.right_ref, ...), custom_call_target="tpu_custom_call" | custom-call | flops 12079595520 | bytes 8388608 | tf_op jit(solution)/shard_map/pallas_call | solution.py:227
  134.7 9.7 %shard_map.124 = (f32[336,5120]{1,0:T(8,128)S(1)}, bf16[48,5120]{1,0:T(8,128)(2,1)S(1)}, s32[8,128]{1,0:T(8,128)}) custom-call(s32[480]{0:T(512)S(1)} %get-tuple-element.121.refs_0_, s32[480]{0:T(512)S(1)} %get-tuple-element.163.refs_1_, bf16[384,1536]{1,0:T(8,128)(2,1)S(1)} %get-tuple-element.116.refs_2_.right_ref, ...), custom_call_target="tpu_custom_call", output_to_operand_aliasing={{0}: (6, {}), {1}: (7, {})} | custom-call | flops 12079595520 | bytes 8388608 | tf_op jit(solution)/shard_map/pallas_call | solution.py:227
  146.5 3.8 %shard_map.125 = bf16[60,128,128]{2,1,0:T(8,128)(2,1)S(1)} custom-call(s32[60]{0:T(128)S(1)} %get-tuple-element.129.at, bf16[384,1536]{1,0:T(8,128)(2,1)S(1)} %get-tuple-element.91.refs_1_.left_ref, bf16[384,5120]{1,0:T(8,128)(2,1)S(1)} %constant_dynamic-update-slice_fusion.9.refs_1_.right_ref), custom_call_target="tpu_custom_call" | custom-call | flops 3019898880 | bytes 8388608 | tf_op jit(solution)/shard_map/pallas_call | solution.py:273
  153.7 3.8 %shard_map.126 = bf16[60,128,128]{2,1,0:T(8,128)(2,1)S(1)} custom-call(s32[60]{0:T(128)S(1)} %get-tuple-element.132.at, bf16[384,5120]{1,0:T(8,128)(2,1)S(1)} %constant_dynamic-update-slice_fusion.refs_2_.left_ref, bf16[384,1536]{1,0:T(8,128)(2,1)S(1)} %get-tuple-element.116.refs_2_.right_ref), custom_call_target="tpu_custom_call" | custom-call | flops 3019898880 | bytes 8388608 | tf_op jit(solution)/shard_map/pallas_call | solution.py:273
  157.6 3.8 %shard_map.127 = bf16[60,128,128]{2,1,0:T(8,128)(2,1)S(1)} custom-call(s32[60]{0:T(128)S(1)} %get-tuple-element.133.at, bf16[384,5120]{1,0:T(8,128)(2,1)S(1)} %constant_dynamic-update-slice_fusion.refs_2_.left_ref, bf16[384,1536]{1,0:T(8,128)(2,1)S(1)} %get-tuple-element.117.refs_3_.right_ref), custom_call_target="tpu_custom_call" | custom-call | flops 3019898880 | bytes 8388608 | tf_op jit(solution)/shard_map/pallas_call | solution.py:273
  162.0 2.3 %collective-permute-done.27 = bf16[48,5120]{1,0:T(8,128)(2,1)S(1)} collective-permute-done((bf16[48,5120]{1,0:T(8,128)(2,1)S(1)}, bf16[48,5120]{1,0:T(8,128)(2,1)S(1)}, u32[]{:S(2)}, u32[]{:S(2)}) %collective-permute-start.27) | collective-permute-done | bytes 491552 | tf_op jit(solution)/shard_map/ppermute | solution.py:30
  168.0 5.1 %shard_map.128 = f32[60,128,128]{2,1,0:T(8,128)} custom-call(s32[60]{0:T(128)S(1)} %get-tuple-element.136.at, bf16[384,1536]{1,0:T(8,128)(2,1)S(1)} %get-tuple-element.91.refs_1_.left_ref, bf16[384,5120]{1,0:T(8,128)(2,1)S(1)} %constant_dynamic-update-slice_fusion.9.refs_1_.right_ref, bf16[60,128,128]{2,1,0:T(8,128)(2,1)S(1)} %collective-permute-done.28.rest_0_), custom_call_target="tpu_custom_call" | custom-call | flops 3019898880 | bytes 8388608 | tf_op jit(solution)/shard_map/pallas_call | solution.py:273
  173.2 3.0 %collective-permute-done.30 = bf16[48,5120]{1,0:T(8,128)(2,1)S(1)} collective-permute-done((bf16[48,5120]{1,0:T(8,128)(2,1)S(1)}, bf16[48,5120]{1,0:T(8,128)(2,1)S(1)}, u32[]{:S(2)}, u32[]{:S(2)}) %collective-permute-start.30) | collective-permute-done | bytes 491552 | tf_op jit(solution)/shard_map/ppermute | solution.py:30
  179.8 5.1 %shard_map.129 = f32[60,128,128]{2,1,0:T(8,128)} custom-call(s32[60]{0:T(128)S(1)} %get-tuple-element.139.at, bf16[384,5120]{1,0:T(8,128)(2,1)S(1)} %constant_dynamic-update-slice_fusion.refs_2_.left_ref, bf16[384,1536]{1,0:T(8,128)(2,1)S(1)} %get-tuple-element.116.refs_2_.right_ref, bf16[60,128,128]{2,1,0:T(8,128)(2,1)S(1)} %collective-permute-done.31.rest_0_), custom_call_target="tpu_custom_call" | custom-call | flops 3019898880 | bytes 8388608 | tf_op jit(solution)/shard_map/pallas_call | solution.py:273
  185.0 5.1 %shard_map.130 = f32[60,128,128]{2,1,0:T(8,128)} custom-call(s32[60]{0:T(128)S(1)} %get-tuple-element.140.at, bf16[384,5120]{1,0:T(8,128)(2,1)S(1)} %constant_dynamic-update-slice_fusion.refs_2_.left_ref, bf16[384,1536]{1,0:T(8,128)(2,1)S(1)} %get-tuple-element.117.refs_3_.right_ref, bf16[60,128,128]{2,1,0:T(8,128)(2,1)S(1)} %collective-permute-done.32.rest_0_), custom_call_target="tpu_custom_call" | custom-call | flops 3019898880 | bytes 8388608 | tf_op jit(solution)/shard_map/pallas_call | solution.py:273
  (118 shorter events, 54.4 us)
Async XLA Ops:
  0.6 14.7 %collective-permute-start = (bf16[48,5120]{1,0:T(8,128)(2,1)}, bf16[48,5120]{1,0:T(8,128)(2,1)S(1)}, u32[]{:S(2)}, u32[]{:S(2)}) collective-permute-start(bf16[48,5120]{1,0:T(8,128)(2,1)} %param.8), channel_id=1, source_target_pairs={{0,4},{4,8},{8,12},{12,14},{14,10},{10,6},{6,2},{2,0},{1,5},{5,9},... | collective-permute-start | bytes 1474568 | tf_op jit(solution)/shard_map/ppermute | solution.py:27
  3.7 12.9 %collective-permute-start.1 = (bf16[48,5120]{1,0:T(8,128)(2,1)}, bf16[48,5120]{1,0:T(8,128)(2,1)S(1)}, u32[]{:S(2)}, u32[]{:S(2)}) collective-permute-start(bf16[48,5120]{1,0:T(8,128)(2,1)} %param.8), channel_id=1, source_target_pairs={{4,0},{8,4},{12,8},{14,12},{10,14},{6,10},{2,6},{0,2},{5,1},{9,5},... | collective-permute-start | bytes 1474568 | tf_op jit(solution)/shard_map/ppermute | solution.py:30
  16.6 11.8 %collective-permute-start.2 = (bf16[48,5120]{1,0:T(8,128)(2,1)S(1)}, bf16[48,5120]{1,0:T(8,128)(2,1)S(1)}, u32[]{:S(2)}, u32[]{:S(2)}) collective-permute-start(bf16[48,5120]{1,0:T(8,128)(2,1)S(1)} %collective-permute-done), channel_id=1, source_target_pairs={{0,4},{4,8},{8,12},{12,14},{14,10},{10,6},{6,2},{2,0},{1,5},{5,9},... | collective-permute-start | bytes 1474568 | tf_op jit(solution)/shard_map/ppermute | solution.py:27
  18.2 11.5 %collective-permute-start.3 = (bf16[48,5120]{1,0:T(8,128)(2,1)S(1)}, bf16[48,5120]{1,0:T(8,128)(2,1)S(1)}, u32[]{:S(2)}, u32[]{:S(2)}) collective-permute-start(bf16[48,5120]{1,0:T(8,128)(2,1)S(1)} %collective-permute-done.1), channel_id=1, source_target_pairs={{4,0},{8,4},{12,8},{14,12},{10,14},{6,10},{2,6},{0,2},{5,1},{9,5},... | collective-permute-start | bytes 1474568 | tf_op jit(solution)/shard_map/ppermute | solution.py:30
  49.9 11.8 %collective-permute-start.8 = (bf16[48,5120]{1,0:T(8,128)(2,1)S(1)}, bf16[48,5120]{1,0:T(8,128)(2,1)S(1)}, u32[]{:S(2)}, u32[]{:S(2)}) collective-permute-start(bf16[48,5120]{1,0:T(8,128)(2,1)S(1)} %copy-done.6), channel_id=1, source_target_pairs={{0,4},{4,8},{8,12},{12,14},{14,10},{10,6},{6,2},{2,0},{1,5},{5,9},... | collective-permute-start | bytes 1474568 | tf_op jit(solution)/shard_map/ppermute | solution.py:27
  53.1 11.4 %collective-permute-start.9 = (bf16[48,5120]{1,0:T(8,128)(2,1)S(1)}, bf16[48,5120]{1,0:T(8,128)(2,1)S(1)}, u32[]{:S(2)}, u32[]{:S(2)}) collective-permute-start(bf16[48,5120]{1,0:T(8,128)(2,1)S(1)} %copy-done.6), channel_id=1, source_target_pairs={{4,0},{8,4},{12,8},{14,12},{10,14},{6,10},{2,6},{0,2},{5,1},{9,5},... | collective-permute-start | bytes 1474568 | tf_op jit(solution)/shard_map/ppermute | solution.py:30
  64.4 12.4 %collective-permute-start.10 = (bf16[48,5120]{1,0:T(8,128)(2,1)S(1)}, bf16[48,5120]{1,0:T(8,128)(2,1)S(1)}, u32[]{:S(2)}, u32[]{:S(2)}) collective-permute-start(bf16[48,5120]{1,0:T(8,128)(2,1)S(1)} %collective-permute-done.8), channel_id=1, source_target_pairs={{0,4},{4,8},{8,12},{12,14},{14,10},{10,6},{6,2},{2,0},{1,5},{5,9},... | collective-permute-start | bytes 1474568 | tf_op jit(solution)/shard_map/ppermute | solution.py:27
  65.1 12.9 %collective-permute-start.11 = (bf16[48,5120]{1,0:T(8,128)(2,1)S(1)}, bf16[48,5120]{1,0:T(8,128)(2,1)S(1)}, u32[]{:S(2)}, u32[]{:S(2)}) collective-permute-start(bf16[48,5120]{1,0:T(8,128)(2,1)S(1)} %collective-permute-done.9), channel_id=1, source_target_pairs={{4,0},{8,4},{12,8},{14,12},{10,14},{6,10},{2,6},{0,2},{5,1},{9,5},... | collective-permute-start | bytes 1474568 | tf_op jit(solution)/shard_map/ppermute | solution.py:30
  77.9 15.8 %collective-permute-start.14 = (bf16[48,5120]{1,0:T(8,128)(2,1)S(1)}, bf16[48,5120]{1,0:T(8,128)(2,1)S(1)}, u32[]{:S(2)}, u32[]{:S(2)}) collective-permute-start(bf16[48,5120]{1,0:T(8,128)(2,1)S(1)} %collective-permute-done.10), channel_id=1, source_target_pairs={{0,4},{4,8},{8,12},{12,14},{14,10},{10,6},{6,2},{2,0},{1,5},{5,9},... | collective-permute-start | bytes 1474568 | tf_op jit(solution)/shard_map/ppermute | solution.py:27
  78.3 15.4 %collective-permute-start.15 = (bf16[48,5120]{1,0:T(8,128)(2,1)S(1)}, bf16[48,5120]{1,0:T(8,128)(2,1)S(1)}, u32[]{:S(2)}, u32[]{:S(2)}) collective-permute-start(bf16[48,5120]{1,0:T(8,128)(2,1)S(1)} %collective-permute-done.11), channel_id=1, source_target_pairs={{4,0},{8,4},{12,8},{14,12},{10,14},{6,10},{2,6},{0,2},{5,1},{9,5},... | collective-permute-start | bytes 1474568 | tf_op jit(solution)/shard_map/ppermute | solution.py:30
  93.7 12.5 %collective-permute-start.16 = (bf16[24,5120]{1,0:T(8,128)(2,1)S(1)}, bf16[24,5120]{1,0:T(8,128)(2,1)S(1)}, u32[]{:S(2)}, u32[]{:S(2)}) collective-permute-start(bf16[24,5120]{1,0:T(8,128)(2,1)S(1)} %slice.76), channel_id=1, source_target_pairs={{0,4},{4,8},{8,12},{12,14},{14,10},{10,6},{6,2},{2,0},{1,5},{5,9},... | collective-permute-start | bytes 737288 | tf_op jit(solution)/shard_map/ppermute | solution.py:27
  94.2 12.1 %collective-permute-start.17 = (bf16[24,5120]{1,0:T(8,128)(2,1)S(1)}, bf16[24,5120]{1,0:T(8,128)(2,1)S(1)}, u32[]{:S(2)}, u32[]{:S(2)}) collective-permute-start(bf16[24,5120]{1,0:T(8,128)(2,1)S(1)} %slice.77), channel_id=1, source_target_pairs={{4,0},{8,4},{12,8},{14,12},{10,14},{6,10},{2,6},{0,2},{5,1},{9,5},... | collective-permute-start | bytes 737288 | tf_op jit(solution)/shard_map/ppermute | solution.py:30
  106.2 13.1 %collective-permute-start.19 = (bf16[48,5120]{1,0:T(8,128)(2,1)S(1)}, bf16[48,5120]{1,0:T(8,128)(2,1)S(1)}, u32[]{:S(2)}, u32[]{:S(2)}) collective-permute-start(bf16[48,5120]{1,0:T(8,128)(2,1)S(1)} %get-tuple-element.99), channel_id=1, source_target_pairs={{4,0},{8,4},{12,8},{14,12},{10,14},{6,10},{2,6},{0,2},{5,1},{9,5},... | collective-permute-start | bytes 1474568 | tf_op jit(solution)/shard_map/ppermute | solution.py:30
  106.5 13.0 %collective-permute-start.18 = (bf16[48,5120]{1,0:T(8,128)(2,1)S(1)}, bf16[48,5120]{1,0:T(8,128)(2,1)S(1)}, u32[]{:S(2)}, u32[]{:S(2)}) collective-permute-start(bf16[48,5120]{1,0:T(8,128)(2,1)S(1)} %get-tuple-element.98), channel_id=1, source_target_pairs={{0,4},{4,8},{8,12},{12,14},{14,10},{10,6},{6,2},{2,0},{1,5},{5,9},... | collective-permute-start | bytes 1474568 | tf_op jit(solution)/shard_map/ppermute | solution.py:27
  119.8 12.2 %collective-permute-start.21 = (bf16[48,5120]{1,0:T(8,128)(2,1)S(1)}, bf16[48,5120]{1,0:T(8,128)(2,1)S(1)}, u32[]{:S(2)}, u32[]{:S(2)}) collective-permute-start(bf16[48,5120]{1,0:T(8,128)(2,1)S(1)} %get-tuple-element.114), channel_id=1, source_target_pairs={{4,0},{8,4},{12,8},{14,12},{10,14},{6,10},{2,6},{0,2},{5,1},{9,5},... | collective-permute-start | bytes 1474568 | tf_op jit(solution)/shard_map/ppermute | solution.py:30
  120.3 12.1 %collective-permute-start.20 = (bf16[48,5120]{1,0:T(8,128)(2,1)S(1)}, bf16[48,5120]{1,0:T(8,128)(2,1)S(1)}, u32[]{:S(2)}, u32[]{:S(2)}) collective-permute-start(bf16[48,5120]{1,0:T(8,128)(2,1)S(1)} %get-tuple-element.113), channel_id=1, source_target_pairs={{0,4},{4,8},{8,12},{12,14},{14,10},{10,6},{6,2},{2,0},{1,5},{5,9},... | collective-permute-start | bytes 1474568 | tf_op jit(solution)/shard_map/ppermute | solution.py:27
  132.7 11.8 %collective-permute-start.23 = (bf16[48,5120]{1,0:T(8,128)(2,1)S(1)}, bf16[48,5120]{1,0:T(8,128)(2,1)S(1)}, u32[]{:S(2)}, u32[]{:S(2)}) collective-permute-start(bf16[48,5120]{1,0:T(8,128)(2,1)S(1)} %get-tuple-element.120), channel_id=1, source_target_pairs={{4,0},{8,4},{12,8},{14,12},{10,14},{6,10},{2,6},{0,2},{5,1},{9,5},... | collective-permute-start | bytes 1474568 | tf_op jit(solution)/shard_map/ppermute | solution.py:30
  150.3 14.7 %collective-permute-start.28 = (bf16[60,128,128]{2,1,0:T(8,128)(2,1)S(1)}, bf16[60,128,128]{2,1,0:T(8,128)(2,1)S(1)}, u32[]{:S(2)}, u32[]{:S(2)}) collective-permute-start(bf16[60,128,128]{2,1,0:T(8,128)(2,1)S(1)} %shard_map.125), channel_id=1, source_target_pairs={{0,1},{1,0},{2,3},{3,2},{4,5},{5,4},{6,7},{7,6},{8,9},{9,8},{10,11... | collective-permute-start | bytes 5898248 | tf_op jit(solution)/shard_map/ppermute | solution.py:387
  151.7 12.6 %collective-permute-start.27 = (bf16[48,5120]{1,0:T(8,128)(2,1)S(1)}, bf16[48,5120]{1,0:T(8,128)(2,1)S(1)}, u32[]{:S(2)}, u32[]{:S(2)}) collective-permute-start(bf16[48,5120]{1,0:T(8,128)(2,1)S(1)} %get-tuple-element.131), channel_id=1, source_target_pairs={{4,0},{8,4},{12,8},{14,12},{10,14},{6,10},{2,6},{0,2},{5,1},{9,5},... | collective-permute-start | bytes 1474568 | tf_op jit(solution)/shard_map/ppermute | solution.py:30
  152.9 11.9 %collective-permute-start.26 = (bf16[48,5120]{1,0:T(8,128)(2,1)S(1)}, bf16[48,5120]{1,0:T(8,128)(2,1)S(1)}, u32[]{:S(2)}, u32[]{:S(2)}) collective-permute-start(bf16[48,5120]{1,0:T(8,128)(2,1)S(1)} %get-tuple-element.130), channel_id=1, source_target_pairs={{0,4},{4,8},{8,12},{12,14},{14,10},{10,6},{6,2},{2,0},{1,5},{5,9},... | collective-permute-start | bytes 1474568 | tf_op jit(solution)/shard_map/ppermute | solution.py:27
  157.5 20.2 %collective-permute-start.31 = (bf16[60,128,128]{2,1,0:T(8,128)(2,1)S(1)}, bf16[60,128,128]{2,1,0:T(8,128)(2,1)S(1)}, u32[]{:S(2)}, u32[]{:S(2)}) collective-permute-start(bf16[60,128,128]{2,1,0:T(8,128)(2,1)S(1)} %shard_map.126), channel_id=1, source_target_pairs={{0,1},{1,0},{2,3},{3,2},{4,5},{5,4},{6,7},{7,6},{8,9},{9,8},{10,11... | collective-permute-start | bytes 5898248 | tf_op jit(solution)/shard_map/ppermute | solution.py:387
  161.4 16.3 %collective-permute-start.32 = (bf16[60,128,128]{2,1,0:T(8,128)(2,1)S(1)}, bf16[60,128,128]{2,1,0:T(8,128)(2,1)S(1)}, u32[]{:S(2)}, u32[]{:S(2)}) collective-permute-start(bf16[60,128,128]{2,1,0:T(8,128)(2,1)S(1)} %shard_map.127), channel_id=1, source_target_pairs={{0,1},{1,0},{2,3},{3,2},{4,5},{5,4},{6,7},{7,6},{8,9},{9,8},{10,11... | collective-permute-start | bytes 5898248 | tf_op jit(solution)/shard_map/ppermute | solution.py:387
  166.2 11.3 %collective-permute-start.29 = (bf16[48,5120]{1,0:T(8,128)(2,1)S(1)}, bf16[48,5120]{1,0:T(8,128)(2,1)S(1)}, u32[]{:S(2)}, u32[]{:S(2)}) collective-permute-start(bf16[48,5120]{1,0:T(8,128)(2,1)S(1)} %get-tuple-element.134), channel_id=1, source_target_pairs={{0,4},{4,8},{8,12},{12,14},{14,10},{10,6},{6,2},{2,0},{1,5},{5,9},... | collective-permute-start | bytes 1474568 | tf_op jit(solution)/shard_map/ppermute | solution.py:27
  177.7 12.4 %collective-permute-start.34 = (bf16[48,5120]{1,0:T(8,128)(2,1)S(1)}, bf16[48,5120]{1,0:T(8,128)(2,1)S(1)}, u32[]{:S(2)}, u32[]{:S(2)}) collective-permute-start(bf16[48,5120]{1,0:T(8,128)(2,1)S(1)} %get-tuple-element.138), channel_id=1, source_target_pairs={{4,0},{8,4},{12,8},{14,12},{10,14},{6,10},{2,6},{0,2},{5,1},{9,5},... | collective-permute-start | bytes 1474568 | tf_op jit(solution)/shard_map/ppermute | solution.py:30
  (21 other events, 247.6 us)

commit v3 on v2

--- a/solution.py
+++ b/solution.py
@@ -55,8 +55,14 @@
         self.taken += 1
         return self.from_left, self.from_right
 
-    def result(self, events=()):
+    def first_rows(self, events):
+        return jnp.concatenate(after_all(self.blocks[:self.last + 1], events), axis=0)
+
+    def all_rows(self, events):
         return jnp.concatenate(after_all(self.blocks, events), axis=0)
+
+    def last_rows(self, events):
+        return jnp.concatenate(after_all(self.blocks[self.last + 1:], events), axis=0)
 
 
 class Scatter:
@@ -101,7 +107,7 @@
     return jnp.concatenate([blocks, jnp.zeros((1,) + blocks.shape[1:], blocks.dtype)], axis=0)
 
 
-def columns_of(lhs, weights, place, first, depth, b):
+def columns_of(lhs, weights, place, first, depth):
     strip = jnp.concatenate(
         [
             jnp.concatenate([weights[place(first + n, m)] for n in range(2)], axis=1)
@@ -112,7 +118,7 @@
     return jnp.dot(lhs, strip, preferred_element_type=jnp.float32)
 
 
-def columns_of_turned(lhs, weights, place, first, depth, b):
+def columns_of_turned(lhs, weights, place, first, depth):
     strip = jnp.concatenate(
         [
             jnp.concatenate([weights[place(first + n, m)] for m in range(depth)], axis=1)
@@ -125,15 +131,11 @@
     )
 
 
-def hidden_kernel(dim_blocks, offset, gate_at, up_at, x, gate_w, up_w, *rest):
-    hidden, act, slope = rest[-4:-1]
+def hidden_kernel(dim_blocks, offset, gate_at, up_at, x, gate_w, up_w, hidden, act, slope):
     first = (offset + pl.program_id(0)) * 2
-    b = gate_w.shape[1]
 
     def strip(at, w):
-        return columns_of(
-            x[...], w, lambda n, m: at[n * dim_blocks + m], first, dim_blocks, b
-        )
+        return columns_of(x[...], w, lambda n, m: at[n * dim_blocks + m], first, dim_blocks)
 
     gate = strip(gate_at, gate_w)
     up = strip(up_at, up_w)
@@ -144,12 +146,10 @@
     slope[...] = up * sig * (1.0 + gate * (1.0 - sig))
 
 
-def grads_kernel(dim_blocks, offset, down_at, g, down_w, act, slope, *rest):
-    gate_grad, up_grad = rest[-3:-1]
+def grads_kernel(dim_blocks, offset, down_at, g, down_w, act, slope, gate_grad, up_grad):
     first = (offset + pl.program_id(0)) * 2
-    b = down_w.shape[1]
     hidden_grad = columns_of_turned(
-        g[...], down_w, lambda n, m: down_at[n * dim_blocks + m], first, dim_blocks, b
+        g[...], down_w, lambda n, m: down_at[n * dim_blocks + m], first, dim_blocks
     )
     gate_grad[...] = (hidden_grad * slope[...]).astype(jnp.bfloat16)
     up_grad[...] = (hidden_grad * act[...]).astype(jnp.bfloat16)
@@ -161,31 +161,25 @@
     far[...] = value[rows:].astype(far.dtype)
 
 
-def output_kernel(dim_blocks, columns, offset, down_at, hidden, down_w, *rest):
+def output_kernel(dim_blocks, columns, offset, down_at, hidden, down_w, near, far):
     first = (offset + pl.program_id(0)) * 2
-    split_rows(
-        columns_of(
-            hidden[...], down_w, lambda n, m: down_at[m * dim_blocks + n], first, columns,
-            down_w.shape[1],
-        ),
-        *rest[-3:-1],
-    )
+    value = columns_of(
+        hidden[...], down_w, lambda n, m: down_at[m * dim_blocks + n], first, columns
+    )
+    split_rows(value, near, far)
 
 
 def input_grad_kernel(
-    dim_blocks, columns, offset, gate_at, up_at, gate_grad, up_grad, gate_w, up_w, *rest
+    dim_blocks, columns, offset, gate_at, up_at, gate_grad, up_grad, gate_w, up_w, near, far
 ):
     first = (offset + pl.program_id(0)) * 2
-    b = gate_w.shape[1]
 
     def strip(lhs, at, w):
         return columns_of_turned(
-            lhs[...], w, lambda n, m: at[m * dim_blocks + n], first, columns, b
+            lhs[...], w, lambda n, m: at[m * dim_blocks + n], first, columns
         )
 
-    split_rows(
-        strip(gate_grad, gate_at, gate_w) + strip(up_grad, up_at, up_w), *rest[-3:-1]
-    )
+    split_rows(strip(gate_grad, gate_at, gate_w) + strip(up_grad, up_at, up_w), near, far)
 
 
 def whole_spec(array):
@@ -199,30 +193,31 @@
 
 
 class Strips:
-    def __init__(self, kernel, inputs, specs, total, block_outs, flops):
-        self.kernel, self.inputs, self.specs = kernel, inputs, specs
-        self.total, self.block_outs, self.flops = total, block_outs, flops
+    def __init__(self, kernel, total, block_outs, flops):
+        self.kernel, self.total, self.block_outs, self.flops = kernel, total, block_outs, flops
         self.outs = []
-        self.done = 0
-
-    def run(self, share, events=()):
-        offset = self.done
-        count = round(self.total * share) - offset
-        self.done += count
+
+    def run(self, inputs, specs, strips, events=(), half=None):
+        first, end = strips
+        count = end - first
+        parts = 1 if half is None else 2
 
         def strip_spec(array):
-            return pl.BlockSpec((array.shape[0], 2 * 128), lambda i: (0, offset + i))
-
-        inputs = [*after_all(self.inputs[:1], events), *self.inputs[1:], *self.outs]
+            return pl.BlockSpec(
+                (array.shape[0] // parts, 2 * 128), lambda i: (half or 0, first + i)
+            )
+
         in_specs = [
             strip_spec(array) if spec is None else whole_spec(array) if spec is WHOLE else spec
-            for array, spec in zip(inputs, self.specs)
+            for array, spec in zip(inputs, specs)
         ] + [ANY_SPEC] * len(self.outs)
-        first_out = len(self.inputs)
+        first_out = len(inputs)
+        inputs = [*after_all(inputs[:1], events), *inputs[1:], *self.outs]
 
         def kernel(*refs):
-            self.kernel(offset, *refs)
-            refs[-1][...] = jnp.zeros_like(refs[-1])
+            outs = refs[len(inputs):]
+            self.kernel(first, *refs[:first_out], *outs[:-1])
+            outs[-1][...] = jnp.zeros_like(outs[-1])
 
         *outs, token = pl.pallas_call(
             kernel,
@@ -233,10 +228,10 @@
             out_shape=list(self.block_outs) + [jax.ShapeDtypeStruct((8, 128), jnp.int32)],
             input_output_aliases={first_out + i: i for i in range(len(self.outs))},
             compiler_params=room(
-                [array for array, spec in zip(inputs, self.specs) if spec is WHOLE], 12
+                [array for array, spec in zip(inputs, specs) if spec is WHOLE], 12
             ),
             cost_estimate=pl.CostEstimate(
-                flops=2 * self.flops * count // self.total, bytes_accessed=8 * 2**20,
+                flops=2 * self.flops * count // (self.total * parts), bytes_accessed=8 * 2**20,
                 transcendentals=0,
             ),
         )(*inputs)
@@ -244,43 +239,48 @@
         return (token,)
 
 
-def block_grads(left, right, index, dim_blocks, left_is_model, arrived, scale):
+def block_grads(model, hidden, index, dim_blocks, model_first, arrived, scale):
     count = index.shape[0]
-    rows = left.shape[0]
+    rows = model[0].shape[0]
     b = 128
     group = max(d for d in range(1, 13) if count % d == 0)
-
-    def kernel(at, left_ref, right_ref, *rest):
+    extra = [] if arrived is None else [arrived]
+
+    def kernel(at, *refs):
+        model_refs, hidden_ref, rest = refs[:len(model)], refs[len(model)], refs[len(model) + 1:]
         out = rest[-1]
         base = pl.program_id(0) * group
         for i in range(group):
             slot = at[base + i]
-            model, hidden = slot % dim_blocks, slot // dim_blocks
-            a, c = (model, hidden) if left_is_model else (hidden, model)
-            value = lax.dot_general(
-                left_ref[:, pl.ds(pl.multiple_of(a * b, b), b)],
-                right_ref[:, pl.ds(pl.multiple_of(c * b, b), b)],
-                (((0,), (0,)), ((), ())),
-                preferred_element_type=jnp.float32,
-            )
+            model_at = pl.ds(pl.multiple_of(slot % dim_blocks * b, b), b)
+            hidden_at = pl.ds(pl.multiple_of(slot // dim_blocks * b, b), b)
+            value = None
+            for part, ref in enumerate(model_refs):
+                pair = (ref[:, model_at], hidden_ref[pl.ds(part * rows, rows), hidden_at])
+                term = lax.dot_general(
+                    *(pair if model_first else pair[::-1]),
+                    (((0,), (0,)), ((), ())),
+                    preferred_element_type=jnp.float32,
+                )
+                value = term if value is None else value + term
             if arrived is not None:
                 value = (value + rest[0][i].astype(jnp.float32)) * scale
             out[i] = value.astype(out.dtype)
 
     spec = pl.BlockSpec((group, b, b), lambda i: (i, 0, 0))
-    extra = [] if arrived is None else [arrived]
+    whole = [*model, hidden]
     dtype = jnp.bfloat16 if arrived is None else jnp.float32
     return pl.pallas_call(
         kernel,
         grid=(count // group,),
-        in_specs=[SMEM_SPEC, whole_spec(left), whole_spec(right)] + [spec] * len(extra),
+        in_specs=[SMEM_SPEC] + [whole_spec(a) for a in whole] + [spec] * len(extra),
         out_specs=spec,
         out_shape=jax.ShapeDtypeStruct((count, b, b), dtype),
-        compiler_params=room([left, right], 10),
+        compiler_params=room(whole, 10),
         cost_estimate=pl.CostEstimate(
-            flops=8 * count * rows * b * b, bytes_accessed=8 * 2**20, transcendentals=0
+            flops=8 * count * rows * len(model) * b * b, bytes_accessed=8 * 2**20, transcendentals=0
         ),
-    )(index, left, right, *extra)
+    )(index, *whole, *extra)
 
 
 def body(
@@ -313,54 +313,67 @@
             events = chain.step(events)
         return tuple(events)
 
+    hidden_strips = Strips(
+        functools.partial(hidden_kernel, dim_blocks), columns // 2, [narrow, wide, wide], 2 * unit
+    )
+    out_strips = Strips(
+        functools.partial(output_kernel, dim_blocks, columns), dim_blocks // 2, totals, unit
+    )
+    grads_strips = Strips(
+        functools.partial(grads_kernel, dim_blocks), columns // 2, [narrow, narrow], unit
+    )
+    in_strips = Strips(
+        functools.partial(input_grad_kernel, dim_blocks, columns), dim_blocks // 2, totals, 2 * unit
+    )
+    hidden_all, model_all = columns // 2, dim_blocks // 2
+
     x_ring, g_ring = Gather(tokens_in, owners), Gather(grad_out, owners)
     events = several(x_ring, 1)
     gate_at, up_at = slot_table(gate_index, slots), slot_table(up_index, slots)
     gate_w = with_zero(gate_blocks)
-    events = several(x_ring, 1, events + (gate_at, up_at, gate_w[-1, :8]))
-    up_w = with_zero(up_blocks)
-    events = several(x_ring, 1, events + (up_w[-1, :8],))
+    events = several(x_ring, 1, events + (gate_at, up_at, gate_w))
+    (up_w,) = after_all([with_zero(up_blocks)], events[:0])
+    x_low = x_ring.first_rows(events + (up_w,))
+
+    def hidden_run(x, strips, events, half):
+        return hidden_strips.run(
+            [gate_at, up_at, x, gate_w, up_w], [SMEM_SPEC] * 2 + [WHOLE] * 3, strips, events, half
+        )
+
+    events = several(x_ring, 1, events) + hidden_run(x_low, (0, hidden_all // 2), events, 0)
     down_at, down_w = slot_table(down_index, slots), with_zero(down_blocks)
-    events = several(x_ring, 1, events + (down_at, down_w[-1, :8]))
-    x = x_ring.result()
-
-    hidden_strips = Strips(
-        functools.partial(hidden_kernel, dim_blocks),
-        [gate_at, up_at, x, gate_w, up_w],
-        [SMEM_SPEC] * 2 + [WHOLE] * 3,
-        columns // 2, [narrow, wide, wide], 2 * unit,
-    )
-    events = several(g_ring, 1, events) + hidden_strips.run(0.5, events)
-    events = several(g_ring, 1, events) + hidden_strips.run(1, events)
+    events = (
+        several(x_ring, 1, events)
+        + several(g_ring, 1, events)
+        + hidden_run(x_low, (hidden_all // 2, hidden_all), events, 0)
+        + (down_at, down_w)
+    )
+    x_high = x_ring.last_rows(events)
+
+    events = several(g_ring, 1, events) + hidden_run(x_high, (0, hidden_all), events, 1)
     hidden, act, slope = hidden_strips.outs
-    out_strips = Strips(
-        functools.partial(output_kernel, dim_blocks, columns),
-        [down_at, hidden, down_w],
-        [SMEM_SPEC] + [WHOLE] * 2,
-        dim_blocks // 2, totals, unit,
-    )
-    events = several(g_ring, 1, events) + out_strips.run(1, events)
+    events = several(g_ring, 1, events) + out_strips.run(
+        [down_at, hidden, down_w], [SMEM_SPEC] + [WHOLE] * 2, (0, model_all), events
+    )
+
     out_ring = Scatter(*out_strips.outs, owners)
     events = several(g_ring, 1, events) + several(out_ring, 1)
-    g = g_ring.result(events)
-
-    grads_strips = Strips(
-        functools.partial(grads_kernel, dim_blocks),
-        [down_at, g, down_w, act, slope],
-        [SMEM_SPEC] + [WHOLE] * 2 + [None] * 2,
-        columns // 2, [narrow, narrow], unit,
-    )
-    events = several(out_ring, 1, events) + grads_strips.run(1, events)
+    g = g_ring.all_rows(events)
+
+    def in_run(strips, events):
+        return in_strips.run(
+            [gate_at, up_at, *grads_strips.outs, gate_w, up_w], [SMEM_SPEC] * 2 + [WHOLE] * 4,
+            strips, events,
+        )
+
+    events = several(out_ring, 1, events) + grads_strips.run(
+        [down_at, g, down_w, act, slope], [SMEM_SPEC] + [WHOLE] * 2 + [None] * 2,
+        (0, hidden_all), events,
+    )
+    events = several(out_ring, 1, events) + in_run((0, model_all // 2), events)
+    events = several(out_ring, 1, events) + in_run((model_all // 2, model_all), events)
+    output = out_ring.result()
     gate_grad, up_grad = grads_strips.outs
-    in_strips = Strips(
-        functools.partial(input_grad_kernel, dim_blocks, columns),
-        [gate_at, up_at, gate_grad, up_grad, gate_w, up_w],
-        [SMEM_SPEC] * 2 + [WHOLE] * 4,
-        dim_blocks // 2, totals, 2 * unit,
-    )
-    events = several(out_ring, 1, events) + in_strips.run(0.5, events)
-    events = several(out_ring, 1, events) + in_strips.run(1, events)
-    output = out_ring.result()
 
     in_ring = Scatter(*in_strips.outs, owners)
     pairs = lax.axis_size("dp")
@@ -368,27 +381,27 @@
     me = lax.axis_index("dp")
     scale = 1.0 / float(token_count * pairs) ** 0.5
     work = (
-        (hidden, g, down_index, False),
-        (x, gate_grad, gate_index, True),
-        (x, up_grad, up_index, True),
+        ((g,), hidden, down_index, False),
+        ((x_low, x_high), gate_grad, gate_index, True),
+        ((x_low, x_high), up_grad, up_index, True),
     )
 
     def theirs(i, events):
-        left, right, index, left_is_model = work[i]
+        model, hidden, index, model_first = work[i]
         (held,) = after_all([lax.dynamic_slice(index, ((1 - me) * share,), (share,))], events)
-        return block_grads(left, right, held, dim_blocks, left_is_model, None, None)
+        return block_grads(model, hidden, held, dim_blocks, model_first, None, None)
 
     def mine(i, arrived, events):
-        left, right, index, left_is_model = work[i]
+        model, hidden, index, model_first = work[i]
         (held,) = after_all([lax.dynamic_slice(index, (me * share,), (share,))], events)
-        return block_grads(left, right, held, dim_blocks, left_is_model, arrived, scale)
+        return block_grads(model, hidden, held, dim_blocks, model_first, arrived, scale)
 
     def swap(sent):
         return lax.ppermute(sent, "dp", [(0, 1), (1, 0)])
 
-    sent_down = theirs(0, events)
-    events = several(in_ring, 1, events) + (sent_down,)
-    down_arrived = swap(sent_down)
+    sent = theirs(0, events)
+    events = several(in_ring, 1, events) + (sent,)
+    down_arrived = swap(sent)
     sent = [theirs(1, events), theirs(2, events)]
     events = several(in_ring, 1, events) + (*sent, down_arrived)
     gate_arrived, up_arrived = swap(sent[0]), swap(sent[1])

time: 191 us -> 187 us (0.979)
  waiting for transfers between devices: 55.5 us -> 42.1 us
  local copies, waits for them, and re-layouts: 11.4 us -> 18.1 us
  Pallas kernels: 83.1 us -> 86.7 us
    ppermute x16, waiting for transfers between devices: 33.7 us -> 26.9 us  [to_right(): return lax.ppermute(value, 'tensor', ahead)]
    ppermute x16, waiting for transfers between devices: 21.8 us -> 15.2 us  [to_left(): return lax.ppermute(value, 'tensor', back)]
    unnamed x36 -> x53, local copies, waits for them, and re-layouts: 1.78 us -> 6.18 us
    pallas_call x6 -> x7, Pallas kernels: 56.2 us -> 59.1 us  [run(): pl.pallas_call(kernel, grid=(count,), in_specs=in_specs, out_specs=[strip...]
    concatenate x3, local copies, waits for them, and re-layouts: 9.25 us -> 11.5 us  [with_zero(): jnp.concatenate([blocks, jnp.zeros((1,) + blocks.shape[1:], blocks.dtype)...]
  transfers between devices with their start and end apart: 35 -> 35, of which waited for: 24 -> 19; matrix products, arithmetic and copies ran while one was open for 7% -> 8% of each run, Pallas kernels for 43% -> 46%
where the time goes in v3:
time: 187 us
  Pallas kernels  86.7 us (46%)
  waiting for transfers between devices  42.1 us (23%)
  starting transfers between devices  35.2 us (19%)
  local copies, waits for them, and re-layouts  18.1 us (10%)
  other arithmetic  3.5 us (2%)
    pallas_call x7, Pallas kernels, run(): pl.pallas_call(kernel, grid=(count,), in_specs=in_specs, out_specs=[strip...  59.1 us
    pallas_call x6, Pallas kernels, block_grads(): pl.pallas_call(kernel, grid=(count // group,), in_specs=[SMEM_SPEC] + [wh...  27.6 us
    ppermute x16, waiting for transfers between devices, to_right(): return lax.ppermute(value, 'tensor', ahead)  26.9 us
    ppermute x16, starting transfers between devices, to_right(): return lax.ppermute(value, 'tensor', ahead)  22.3 us
    ppermute x16, waiting for transfers between devices, to_left(): return lax.ppermute(value, 'tensor', back)  15.2 us
    ppermute x16, starting transfers between devices, to_left(): return lax.ppermute(value, 'tensor', back)  12.3 us
    concatenate x3, local copies, waits for them, and re-layouts, with_zero(): jnp.concatenate([blocks, jnp.zeros((1,) + blocks.shape[1:], blocks.dtype)...  11.5 us
    unnamed x53, local copies, waits for them, and re-layouts  6.18 us
  transfers between devices with their start and end apart: 35, of which 19 were waited for; matrix products, arithmetic and copies ran while one was open for 8% of the time, Pallas kernels for 46%

profile of v3, /device:TPU:0, one launch (start us, length us, event | category | flops | bytes accessed | tf_op | source)
XLA Modules:
  0.0 186.7 jit_solution(17915837449517445031)
XLA Ops:
  0.7 3.1 %collective-permute-start = (bf16[48,5120]{1,0:T(8,128)(2,1)}, bf16[48,5120]{1,0:T(8,128)(2,1)S(1)}, u32[]{:S(2)}, u32[]{:S(2)}) collective-permute-start(bf16[48,5120]{1,0:T(8,128)(2,1)} %param.8), channel_id=1, source_target_pairs={{0,4},{4,8},{8,12},{12,14},{14,10},{10,6},{6,2},{2,0},{1,5},{5,9},... | collective-permute-start | bytes 1474568 | tf_op jit(solution)/shard_map/ppermute | solution.py:27
  3.7 4.5 %concatenate.30.refs_3_.refs_4_ = bf16[121,128,128]{2,1,0:T(8,128)(2,1)} pad(bf16[120,128,128]{2,1,0:T(8,128)(2,1)} %param.10, bf16[]{:T(256)} %constant.1.clone.1), padding=0_1x0_0x0_0 | pad | bytes 7897090 | tf_op jit(solution)/shard_map/concatenate | solution.py:107
  8.5 6.6 %collective-permute-done = bf16[48,5120]{1,0:T(8,128)(2,1)S(1)} collective-permute-done((bf16[48,5120]{1,0:T(8,128)(2,1)}, bf16[48,5120]{1,0:T(8,128)(2,1)S(1)}, u32[]{:S(2)}, u32[]{:S(2)}) %collective-permute-start) | collective-permute-done | bytes 491552 | tf_op jit(solution)/shard_map/ppermute | solution.py:27
  18.6 4.8 %concatenate.31.refs_4_.refs_5_ = bf16[121,128,128]{2,1,0:T(8,128)(2,1)} pad(bf16[120,128,128]{2,1,0:T(8,128)(2,1)} %param.11, bf16[]{:T(256)} %constant.1.clone.1), padding=0_1x0_0x0_0 | pad | bytes 7897090 | tf_op jit(solution)/shard_map/concatenate | solution.py:107
  23.4 2.2 %concatenate.33.refs_2_ = bf16[121,128,128]{2,1,0:T(8,128)(2,1)} pad(bf16[120,128,128]{2,1,0:T(8,128)(2,1)S(1)} %copy-done.13, bf16[]{:T(256)} %constant.1.clone.1), padding=0_1x0_0x0_0 | pad | bytes 7897090 | tf_op jit(solution)/shard_map/concatenate | solution.py:107
  25.8 2.6 %collective-permute-done.2 = bf16[48,5120]{1,0:T(8,128)(2,1)S(1)} collective-permute-done((bf16[48,5120]{1,0:T(8,128)(2,1)S(1)}, bf16[48,5120]{1,0:T(8,128)(2,1)S(1)}, u32[]{:S(2)}, u32[]{:S(2)}) %collective-permute-start.2) | collective-permute-done | bytes 491552 | tf_op jit(solution)/shard_map/ppermute | solution.py:27
  36.1 5.1 %shard_map.119 = (bf16[384,1536]{1,0:T(8,128)(2,1)S(1)}, f32[384,1536]{1,0:T(8,128)S(1)}, f32[384,1536]{1,0:T(8,128)S(1)}, s32[8,128]{1,0:T(8,128)}) custom-call(s32[480]{0:T(512)S(1)} %get-tuple-element.149.refs_0_, s32[480]{0:T(512)S(1)} %get-tuple-element.191.refs_1_, bf16[192,5120]{1,0:T(8,128)(2,1)S(1)} %constant_dynamic-update-slice_fusion.refs_2_.refs_0_, ...), custom_call_target="tpu_custom_call" | custom-call | flops 6039797760 | bytes 8388608 | tf_op jit(solution)/shard_map/pallas_call | solution.py:222
  45.8 5.1 %shard_map.120 = (bf16[384,1536]{1,0:T(8,128)(2,1)S(1)}, f32[384,1536]{1,0:T(8,128)S(1)}, f32[384,1536]{1,0:T(8,128)S(1)}, s32[8,128]{1,0:T(8,128)}) custom-call(s32[480]{0:T(512)S(1)} %get-tuple-element.149.refs_0_, s32[480]{0:T(512)S(1)} %get-tuple-element.191.refs_1_, ...), custom_call_target="tpu_custom_call", output_to_operand_aliasing={{0}: (5, {}), {1}: (6, {}), {2}: (7, {})} | custom-call | flops 6039797760 | bytes 8388608 | tf_op jit(solution)/shard_map/pallas_call | solution.py:222
  50.9 6.3 %collective-permute-done.8 = bf16[24,5120]{1,0:T(8,128)(2,1)S(1)} collective-permute-done((bf16[24,5120]{1,0:T(8,128)(2,1)S(1)}, bf16[24,5120]{1,0:T(8,128)(2,1)S(1)}, u32[]{:S(2)}, u32[]{:S(2)}) %collective-permute-start.8) | collective-permute-done | bytes 245792 | tf_op jit(solution)/shard_map/ppermute | solution.py:27
  60.6 9.0 %shard_map.121 = (bf16[384,1536]{1,0:T(8,128)(2,1)S(1)}, f32[384,1536]{1,0:T(8,128)S(1)}, f32[384,1536]{1,0:T(8,128)S(1)}, s32[8,128]{1,0:T(8,128)}) custom-call(s32[480]{0:T(512)S(1)} %get-tuple-element.149.refs_0_, s32[480]{0:T(512)S(1)} %get-tuple-element.191.refs_1_, ...), custom_call_target="tpu_custom_call", output_to_operand_aliasing={{0}: (5, {}), {1}: (6, {}), {2}: (7, {})} | custom-call | flops 12079595520 | bytes 8388608 | tf_op jit(solution)/shard_map/pallas_call | solution.py:222
  73.1 11.5 %shard_map.122 = (f32[336,5120]{1,0:T(8,128)S(1)}, bf16[48,5120]{1,0:T(8,128)(2,1)S(1)}, s32[8,128]{1,0:T(8,128)}) custom-call(s32[480]{0:T(512)S(1)} %select_reduce_fusion.2.refs_0_, bf16[384,1536]{1,0:T(8,128)(2,1)S(1)} %get-tuple-element.119.refs_1_, bf16[121,128,128]{2,1,0:T(8,128)(2,1)S(1)} %copy-done.4), custom_call_target="tpu_custom_call" | custom-call | flops 12079595520 | bytes 8388608 | tf_op jit(solution)/shard_map/pallas_call | solution.py:222
  89.2 2.9 %collective-permute-done.13 = bf16[24,5120]{1,0:T(8,128)(2,1)S(1)} collective-permute-done((bf16[24,5120]{1,0:T(8,128)(2,1)S(1)}, bf16[24,5120]{1,0:T(8,128)(2,1)S(1)}, u32[]{:S(2)}, u32[]{:S(2)}) %collective-permute-start.13) | collective-permute-done | bytes 245792 | tf_op jit(solution)/shard_map/ppermute | solution.py:30
  93.3 5.1 %collective-permute-done.16 = bf16[24,5120]{1,0:T(8,128)(2,1)S(1)} collective-permute-done((bf16[24,5120]{1,0:T(8,128)(2,1)S(1)}, bf16[24,5120]{1,0:T(8,128)(2,1)S(1)}, u32[]{:S(2)}, u32[]{:S(2)}) %collective-permute-start.16) | collective-permute-done | bytes 245792 | tf_op jit(solution)/shard_map/ppermute | solution.py:27
  101.0 9.1 %shard_map.123 = (bf16[384,1536]{1,0:T(8,128)(2,1)S(1)}, bf16[384,1536]{1,0:T(8,128)(2,1)S(1)}, s32[8,128]{1,0:T(8,128)}) custom-call(s32[480]{0:T(512)S(1)} %select_reduce_fusion.2.refs_0_, bf16[384,5120]{1,0:T(8,128)(2,1)S(1)} %constant_dynamic-update-slice_fusion.9.refs_1_.refs_0_, bf16[121,128,128]{2,1,0:T(8,128)(2,1)S(1)} %copy-done.4, ...), custom_call_target="tpu_custom_call" | custom-call | flops 12079595520 | bytes 8388608 | tf_op jit(solution)/shard_map/pallas_call | solution.py:222
  110.1 2.5 %collective-permute-done.19 = bf16[48,5120]{1,0:T(8,128)(2,1)S(1)} collective-permute-done((bf16[48,5120]{1,0:T(8,128)(2,1)S(1)}, bf16[48,5120]{1,0:T(8,128)(2,1)S(1)}, u32[]{:S(2)}, u32[]{:S(2)}) %collective-permute-start.19) | collective-permute-done | bytes 491552 | tf_op jit(solution)/shard_map/ppermute | solution.py:30
  115.0 9.7 %shard_map.124 = (f32[336,5120]{1,0:T(8,128)S(1)}, bf16[48,5120]{1,0:T(8,128)(2,1)S(1)}, s32[8,128]{1,0:T(8,128)}) custom-call(s32[480]{0:T(512)S(1)} %get-tuple-element.149.refs_0_, s32[480]{0:T(512)S(1)} %get-tuple-element.191.refs_1_, bf16[384,1536]{1,0:T(8,128)(2,1)S(1)} %get-tuple-element.144.refs_2_, ...), custom_call_target="tpu_custom_call" | custom-call | flops 12079595520 | bytes 8388608 | tf_op jit(solution)/shard_map/pallas_call | solution.py:222
  129.1 9.7 %shard_map.125 = (f32[336,5120]{1,0:T(8,128)S(1)}, bf16[48,5120]{1,0:T(8,128)(2,1)S(1)}, s32[8,128]{1,0:T(8,128)}) custom-call(s32[480]{0:T(512)S(1)} %get-tuple-element.149.refs_0_, s32[480]{0:T(512)S(1)} %get-tuple-element.191.refs_1_, bf16[384,1536]{1,0:T(8,128)(2,1)S(1)} %get-tuple-element.144.refs_2_, ...), custom_call_target="tpu_custom_call", output_to_operand_aliasing={{0}: (6, {}), {1}: (7, {})} | custom-call | flops 12079595520 | bytes 8388608 | tf_op jit(solution)/shard_map/pallas_call | solution.py:222
  140.9 3.8 %shard_map.126 = bf16[60,128,128]{2,1,0:T(8,128)(2,1)S(1)} custom-call(s32[60]{0:T(128)S(1)} %get-tuple-element.157.at, bf16[384,5120]{1,0:T(8,128)(2,1)S(1)} %constant_dynamic-update-slice_fusion.9.refs_1_.refs_0_, bf16[384,1536]{1,0:T(8,128)(2,1)S(1)} %copy-done.8), custom_call_target="tpu_custom_call" | custom-call | flops 3019898880 | bytes 8388608 | tf_op jit(solution)/shard_map/pallas_call | solution.py:273
  148.8 4.0 %shard_map.127 = bf16[60,128,128]{2,1,0:T(8,128)(2,1)S(1)} custom-call(s32[60]{0:T(128)S(1)} %get-tuple-element.160.at, bf16[192,5120]{1,0:T(8,128)(2,1)S(1)} %constant_dynamic-update-slice_fusion.refs_2_.refs_0_, bf16[192,5120]{1,0:T(8,128)(2,1)S(1)} %constant_dynamic-update-slice_fusion.4.refs_2_.refs_1_, bf16[384,1536]{1,0:T(8,128)(2,1)S(1)} %get-tuple-element.144.refs_2_), custom_call_target="tpu_custom_call" | custom-call | flops 3019898880 | bytes 8388608 | tf_op jit(solution)/shard_map/pallas_call | solution.py:273
  152.9 4.0 %shard_map.128 = bf16[60,128,128]{2,1,0:T(8,128)(2,1)S(1)} custom-call(s32[60]{0:T(128)S(1)} %get-tuple-element.161.at, bf16[192,5120]{1,0:T(8,128)(2,1)S(1)} %constant_dynamic-update-slice_fusion.refs_2_.refs_0_, bf16[192,5120]{1,0:T(8,128)(2,1)S(1)} %constant_dynamic-update-slice_fusion.4.refs_2_.refs_1_, ...), custom_call_target="tpu_custom_call" | custom-call | flops 3019898880 | bytes 8388608 | tf_op jit(solution)/shard_map/pallas_call | solution.py:273
  163.1 5.1 %shard_map.129 = f32[60,128,128]{2,1,0:T(8,128)} custom-call(s32[60]{0:T(128)S(1)} %get-tuple-element.164.at, bf16[384,5120]{1,0:T(8,128)(2,1)S(1)} %constant_dynamic-update-slice_fusion.9.refs_1_.refs_0_, bf16[384,1536]{1,0:T(8,128)(2,1)S(1)} %copy-done.8, bf16[60,128,128]{2,1,0:T(8,128)(2,1)S(1)} %collective-permute-done.28.refs_2_), custom_call_target="tpu_custom_call" | custom-call | flops 3019898880 | bytes 8388608 | tf_op jit(solution)/shard_map/pallas_call | solution.py:273
  168.3 2.7 %collective-permute-done.30 = bf16[48,5120]{1,0:T(8,128)(2,1)S(1)} collective-permute-done((bf16[48,5120]{1,0:T(8,128)(2,1)S(1)}, bf16[48,5120]{1,0:T(8,128)(2,1)S(1)}, u32[]{:S(2)}, u32[]{:S(2)}) %collective-permute-start.30) | collective-permute-done | bytes 491552 | tf_op jit(solution)/shard_map/ppermute | solution.py:30
  175.2 5.3 %shard_map.130 = f32[60,128,128]{2,1,0:T(8,128)} custom-call(s32[60]{0:T(128)S(1)} %get-tuple-element.167.at, bf16[192,5120]{1,0:T(8,128)(2,1)S(1)} %constant_dynamic-update-slice_fusion.refs_2_.refs_0_, bf16[192,5120]{1,0:T(8,128)(2,1)S(1)} %constant_dynamic-update-slice_fusion.4.refs_2_.refs_1_, bf16[384,1536]{1,0:T(8,128)(2,1)S(1)} %copy-done.6, ...), custom_call_target="tpu_custom_call" | custom-call | flops 3019898880 | bytes 8388608 | tf_op jit(solution)/shard_map/pallas_call | solution.py:273
  180.5 5.3 %shard_map.131 = f32[60,128,128]{2,1,0:T(8,128)} custom-call(s32[60]{0:T(128)S(1)} %get-tuple-element.168.at, bf16[192,5120]{1,0:T(8,128)(2,1)S(1)} %constant_dynamic-update-slice_fusion.refs_2_.refs_0_, bf16[192,5120]{1,0:T(8,128)(2,1)S(1)} %constant_dynamic-update-slice_fusion.4.refs_2_.refs_1_, bf16[384,1536]{1,0:T(8,128)(2,1)S(1)} %get-tuple-element.145.refs_3_.refs_2_, ...), custom_call_target="tpu_custom_call" | custom-call | flops 3019898880 | bytes 8388608 | tf_op jit(solution)/shard_map/pallas_call | solution.py:273
  (137 shorter events, 55.7 us)
Async XLA Ops:
  0.7 14.5 %collective-permute-start = (bf16[48,5120]{1,0:T(8,128)(2,1)}, bf16[48,5120]{1,0:T(8,128)(2,1)S(1)}, u32[]{:S(2)}, u32[]{:S(2)}) collective-permute-start(bf16[48,5120]{1,0:T(8,128)(2,1)} %param.8), channel_id=1, source_target_pairs={{0,4},{4,8},{8,12},{12,14},{14,10},{10,6},{6,2},{2,0},{1,5},{5,9},... | collective-permute-start | bytes 1474568 | tf_op jit(solution)/shard_map/ppermute | solution.py:27
  3.7 12.9 %collective-permute-start.1 = (bf16[48,5120]{1,0:T(8,128)(2,1)}, bf16[48,5120]{1,0:T(8,128)(2,1)S(1)}, u32[]{:S(2)}, u32[]{:S(2)}) collective-permute-start(bf16[48,5120]{1,0:T(8,128)(2,1)} %param.8), channel_id=1, source_target_pairs={{4,0},{8,4},{12,8},{14,12},{10,14},{6,10},{2,6},{0,2},{5,1},{9,5},... | collective-permute-start | bytes 1474568 | tf_op jit(solution)/shard_map/ppermute | solution.py:30
  16.6 11.8 %collective-permute-start.2 = (bf16[48,5120]{1,0:T(8,128)(2,1)S(1)}, bf16[48,5120]{1,0:T(8,128)(2,1)S(1)}, u32[]{:S(2)}, u32[]{:S(2)}) collective-permute-start(bf16[48,5120]{1,0:T(8,128)(2,1)S(1)} %collective-permute-done), channel_id=1, source_target_pairs={{0,4},{4,8},{8,12},{12,14},{14,10},{10,6},{6,2},{2,0},{1,5},{5,9},... | collective-permute-start | bytes 1474568 | tf_op jit(solution)/shard_map/ppermute | solution.py:27
  18.2 11.5 %collective-permute-start.3 = (bf16[48,5120]{1,0:T(8,128)(2,1)S(1)}, bf16[48,5120]{1,0:T(8,128)(2,1)S(1)}, u32[]{:S(2)}, u32[]{:S(2)}) collective-permute-start(bf16[48,5120]{1,0:T(8,128)(2,1)S(1)} %collective-permute-done.1), channel_id=1, source_target_pairs={{4,0},{8,4},{12,8},{14,12},{10,14},{6,10},{2,6},{0,2},{5,1},{9,5},... | collective-permute-start | bytes 1474568 | tf_op jit(solution)/shard_map/ppermute | solution.py:30
  29.7 11.5 %collective-permute-start.4 = (bf16[48,5120]{1,0:T(8,128)(2,1)S(1)}, bf16[48,5120]{1,0:T(8,128)(2,1)S(1)}, u32[]{:S(2)}, u32[]{:S(2)}) collective-permute-start(bf16[48,5120]{1,0:T(8,128)(2,1)S(1)} %collective-permute-done.2), channel_id=1, source_target_pairs={{0,4},{4,8},{8,12},{12,14},{14,10},{10,6},{6,2},{2,0},{1,5},{5,9},... | collective-permute-start | bytes 1474568 | tf_op jit(solution)/shard_map/ppermute | solution.py:27
  41.6 16.7 %collective-permute-start.6 = (bf16[48,5120]{1,0:T(8,128)(2,1)S(1)}, bf16[48,5120]{1,0:T(8,128)(2,1)S(1)}, u32[]{:S(2)}, u32[]{:S(2)}) collective-permute-start(bf16[48,5120]{1,0:T(8,128)(2,1)S(1)} %copy-done.15), channel_id=1, source_target_pairs={{0,4},{4,8},{8,12},{12,14},{14,10},{10,6},{6,2},{2,0},{1,5},{5,9},... | collective-permute-start | bytes 1474568 | tf_op jit(solution)/shard_map/ppermute | solution.py:27
  43.1 15.2 %collective-permute-start.7 = (bf16[48,5120]{1,0:T(8,128)(2,1)S(1)}, bf16[48,5120]{1,0:T(8,128)(2,1)S(1)}, u32[]{:S(2)}, u32[]{:S(2)}) collective-permute-start(bf16[48,5120]{1,0:T(8,128)(2,1)S(1)} %copy-done.15), channel_id=1, source_target_pairs={{4,0},{8,4},{12,8},{14,12},{10,14},{6,10},{2,6},{0,2},{5,1},{9,5},... | collective-permute-start | bytes 1474568 | tf_op jit(solution)/shard_map/ppermute | solution.py:30
  43.6 13.5 %collective-permute-start.8 = (bf16[24,5120]{1,0:T(8,128)(2,1)S(1)}, bf16[24,5120]{1,0:T(8,128)(2,1)S(1)}, u32[]{:S(2)}, u32[]{:S(2)}) collective-permute-start(bf16[24,5120]{1,0:T(8,128)(2,1)S(1)} %slice.69), channel_id=1, source_target_pairs={{0,4},{4,8},{8,12},{12,14},{14,10},{10,6},{6,2},{2,0},{1,5},{5,9},... | collective-permute-start | bytes 737288 | tf_op jit(solution)/shard_map/ppermute | solution.py:27
  45.2 13.1 %collective-permute-start.9 = (bf16[24,5120]{1,0:T(8,128)(2,1)S(1)}, bf16[24,5120]{1,0:T(8,128)(2,1)S(1)}, u32[]{:S(2)}, u32[]{:S(2)}) collective-permute-start(bf16[24,5120]{1,0:T(8,128)(2,1)S(1)} %slice.70), channel_id=1, source_target_pairs={{4,0},{8,4},{12,8},{14,12},{10,14},{6,10},{2,6},{0,2},{5,1},{9,5},... | collective-permute-start | bytes 737288 | tf_op jit(solution)/shard_map/ppermute | solution.py:30
  58.3 12.8 %collective-permute-start.10 = (bf16[48,5120]{1,0:T(8,128)(2,1)S(1)}, bf16[48,5120]{1,0:T(8,128)(2,1)S(1)}, u32[]{:S(2)}, u32[]{:S(2)}) collective-permute-start(bf16[48,5120]{1,0:T(8,128)(2,1)S(1)} %collective-permute-done.6), channel_id=1, source_target_pairs={{0,4},{4,8},{8,12},{12,14},{14,10},{10,6},{6,2},{2,0},{1,5},{5,9},... | collective-permute-start | bytes 1474568 | tf_op jit(solution)/shard_map/ppermute | solution.py:27
  71.1 16.0 %collective-permute-start.14 = (bf16[48,5120]{1,0:T(8,128)(2,1)S(1)}, bf16[48,5120]{1,0:T(8,128)(2,1)S(1)}, u32[]{:S(2)}, u32[]{:S(2)}) collective-permute-start(bf16[48,5120]{1,0:T(8,128)(2,1)S(1)} %collective-permute-done.10), channel_id=1, source_target_pairs={{0,4},{4,8},{8,12},{12,14},{14,10},{10,6},{6,2},{2,0},{1,5},{5,9},... | collective-permute-start | bytes 1474568 | tf_op jit(solution)/shard_map/ppermute | solution.py:27
  73.1 13.9 %collective-permute-start.15 = (bf16[48,5120]{1,0:T(8,128)(2,1)S(1)}, bf16[48,5120]{1,0:T(8,128)(2,1)S(1)}, u32[]{:S(2)}, u32[]{:S(2)}) collective-permute-start(bf16[48,5120]{1,0:T(8,128)(2,1)S(1)} %collective-permute-done.11), channel_id=1, source_target_pairs={{4,0},{8,4},{12,8},{14,12},{10,14},{6,10},{2,6},{0,2},{5,1},{9,5},... | collective-permute-start | bytes 1474568 | tf_op jit(solution)/shard_map/ppermute | solution.py:30
  87.1 11.3 %collective-permute-start.16 = (bf16[24,5120]{1,0:T(8,128)(2,1)S(1)}, bf16[24,5120]{1,0:T(8,128)(2,1)S(1)}, u32[]{:S(2)}, u32[]{:S(2)}) collective-permute-start(bf16[24,5120]{1,0:T(8,128)(2,1)S(1)} %slice.76), channel_id=1, source_target_pairs={{0,4},{4,8},{8,12},{12,14},{14,10},{10,6},{6,2},{2,0},{1,5},{5,9},... | collective-permute-start | bytes 737288 | tf_op jit(solution)/shard_map/ppermute | solution.py:27
  98.4 14.1 %collective-permute-start.19 = (bf16[48,5120]{1,0:T(8,128)(2,1)S(1)}, bf16[48,5120]{1,0:T(8,128)(2,1)S(1)}, u32[]{:S(2)}, u32[]{:S(2)}) collective-permute-start(bf16[48,5120]{1,0:T(8,128)(2,1)S(1)} %get-tuple-element.127), channel_id=1, source_target_pairs={{4,0},{8,4},{12,8},{14,12},{10,14},{6,10},{2,6},{0,2},{5,1},{9,5},... | collective-permute-start | bytes 1474568 | tf_op jit(solution)/shard_map/ppermute | solution.py:30
  98.5 14.1 %collective-permute-start.18 = (bf16[48,5120]{1,0:T(8,128)(2,1)S(1)}, bf16[48,5120]{1,0:T(8,128)(2,1)S(1)}, u32[]{:S(2)}, u32[]{:S(2)}) collective-permute-start(bf16[48,5120]{1,0:T(8,128)(2,1)S(1)} %get-tuple-element.126), channel_id=1, source_target_pairs={{0,4},{4,8},{8,12},{12,14},{14,10},{10,6},{6,2},{2,0},{1,5},{5,9},... | collective-permute-start | bytes 1474568 | tf_op jit(solution)/shard_map/ppermute | solution.py:27
  112.8 13.3 %collective-permute-start.21 = (bf16[48,5120]{1,0:T(8,128)(2,1)S(1)}, bf16[48,5120]{1,0:T(8,128)(2,1)S(1)}, u32[]{:S(2)}, u32[]{:S(2)}) collective-permute-start(bf16[48,5120]{1,0:T(8,128)(2,1)S(1)} %get-tuple-element.142), channel_id=1, source_target_pairs={{4,0},{8,4},{12,8},{14,12},{10,14},{6,10},{2,6},{0,2},{5,1},{9,5},... | collective-permute-start | bytes 1474568 | tf_op jit(solution)/shard_map/ppermute | solution.py:30
  113.8 13.0 %collective-permute-start.20 = (bf16[48,5120]{1,0:T(8,128)(2,1)S(1)}, bf16[48,5120]{1,0:T(8,128)(2,1)S(1)}, u32[]{:S(2)}, u32[]{:S(2)}) collective-permute-start(bf16[48,5120]{1,0:T(8,128)(2,1)S(1)} %get-tuple-element.141), channel_id=1, source_target_pairs={{0,4},{4,8},{8,12},{12,14},{14,10},{10,6},{6,2},{2,0},{1,5},{5,9},... | collective-permute-start | bytes 1474568 | tf_op jit(solution)/shard_map/ppermute | solution.py:27
  127.0 11.8 %collective-permute-start.23 = (bf16[48,5120]{1,0:T(8,128)(2,1)S(1)}, bf16[48,5120]{1,0:T(8,128)(2,1)S(1)}, u32[]{:S(2)}, u32[]{:S(2)}) collective-permute-start(bf16[48,5120]{1,0:T(8,128)(2,1)S(1)} %get-tuple-element.148), channel_id=1, source_target_pairs={{4,0},{8,4},{12,8},{14,12},{10,14},{6,10},{2,6},{0,2},{5,1},{9,5},... | collective-permute-start | bytes 1474568 | tf_op jit(solution)/shard_map/ppermute | solution.py:30
  144.7 15.4 %collective-permute-start.28 = (bf16[60,128,128]{2,1,0:T(8,128)(2,1)S(1)}, bf16[60,128,128]{2,1,0:T(8,128)(2,1)S(1)}, u32[]{:S(2)}, u32[]{:S(2)}) collective-permute-start(bf16[60,128,128]{2,1,0:T(8,128)(2,1)S(1)} %shard_map.126), channel_id=1, source_target_pairs={{0,1},{1,0},{2,3},{3,2},{4,5},{5,4},{6,7},{7,6},{8,9},{9,8},{10,11... | collective-permute-start | bytes 5898248 | tf_op jit(solution)/shard_map/ppermute | solution.py:400
  146.8 11.9 %collective-permute-start.27 = (bf16[48,5120]{1,0:T(8,128)(2,1)S(1)}, bf16[48,5120]{1,0:T(8,128)(2,1)S(1)}, u32[]{:S(2)}, u32[]{:S(2)}) collective-permute-start(bf16[48,5120]{1,0:T(8,128)(2,1)S(1)} %get-tuple-element.159), channel_id=1, source_target_pairs={{4,0},{8,4},{12,8},{14,12},{10,14},{6,10},{2,6},{0,2},{5,1},{9,5},... | collective-permute-start | bytes 1474568 | tf_op jit(solution)/shard_map/ppermute | solution.py:30
  148.6 11.3 %collective-permute-start.26 = (bf16[48,5120]{1,0:T(8,128)(2,1)S(1)}, bf16[48,5120]{1,0:T(8,128)(2,1)S(1)}, u32[]{:S(2)}, u32[]{:S(2)}) collective-permute-start(bf16[48,5120]{1,0:T(8,128)(2,1)S(1)} %get-tuple-element.158), channel_id=1, source_target_pairs={{0,4},{4,8},{8,12},{12,14},{14,10},{10,6},{6,2},{2,0},{1,5},{5,9},... | collective-permute-start | bytes 1474568 | tf_op jit(solution)/shard_map/ppermute | solution.py:27
  152.9 20.2 %collective-permute-start.31 = (bf16[60,128,128]{2,1,0:T(8,128)(2,1)S(1)}, bf16[60,128,128]{2,1,0:T(8,128)(2,1)S(1)}, u32[]{:S(2)}, u32[]{:S(2)}) collective-permute-start(bf16[60,128,128]{2,1,0:T(8,128)(2,1)S(1)} %shard_map.127), channel_id=1, source_target_pairs={{0,1},{1,0},{2,3},{3,2},{4,5},{5,4},{6,7},{7,6},{8,9},{9,8},{10,11... | collective-permute-start | bytes 5898248 | tf_op jit(solution)/shard_map/ppermute | solution.py:400
  157.0 16.1 %collective-permute-start.32 = (bf16[60,128,128]{2,1,0:T(8,128)(2,1)S(1)}, bf16[60,128,128]{2,1,0:T(8,128)(2,1)S(1)}, u32[]{:S(2)}, u32[]{:S(2)}) collective-permute-start(bf16[60,128,128]{2,1,0:T(8,128)(2,1)S(1)} %shard_map.128), channel_id=1, source_target_pairs={{0,1},{1,0},{2,3},{3,2},{4,5},{5,4},{6,7},{7,6},{8,9},{9,8},{10,11... | collective-permute-start | bytes 5898248 | tf_op jit(solution)/shard_map/ppermute | solution.py:400
  173.1 12.7 %collective-permute-start.34 = (bf16[48,5120]{1,0:T(8,128)(2,1)S(1)}, bf16[48,5120]{1,0:T(8,128)(2,1)S(1)}, u32[]{:S(2)}, u32[]{:S(2)}) collective-permute-start(bf16[48,5120]{1,0:T(8,128)(2,1)S(1)} %get-tuple-element.166), channel_id=1, source_target_pairs={{4,0},{8,4},{12,8},{14,12},{10,14},{6,10},{2,6},{0,2},{5,1},{9,5},... | collective-permute-start | bytes 1474568 | tf_op jit(solution)/shard_map/ppermute | solution.py:30
  (30 other events, 274.5 us)

commit v4 on v3

--- a/solution.py
+++ b/solution.py
@@ -357,7 +357,7 @@
     )
 
     out_ring = Scatter(*out_strips.outs, owners)
-    events = several(g_ring, 1, events) + several(out_ring, 1)
+    events = several(g_ring, 1, events)
     g = g_ring.all_rows(events)
 
     def in_run(strips, events):
@@ -366,12 +366,19 @@
             strips, events,
         )
 
-    events = several(out_ring, 1, events) + grads_strips.run(
-        [down_at, g, down_w, act, slope], [SMEM_SPEC] + [WHOLE] * 2 + [None] * 2,
-        (0, hidden_all), events,
-    )
-    events = several(out_ring, 1, events) + in_run((0, model_all // 2), events)
-    events = several(out_ring, 1, events) + in_run((model_all // 2, model_all), events)
+    def grads_run(strips, events):
+        return grads_strips.run(
+            [down_at, g, down_w, act, slope], [SMEM_SPEC] + [WHOLE] * 2 + [None] * 2,
+            strips, events,
+        )
+
+    middle, quarter = hidden_all // 2, model_all // 4
+    events = several(out_ring, 1, events) + grads_run((0, middle), events)
+    token = grads_run((middle, hidden_all), events)
+    events = several(out_ring, 1, events) + in_run((0, quarter), token)
+    events = several(out_ring, 1, events) + in_run((quarter, 3 * quarter), events)
+    token = in_run((3 * quarter, model_all), events)
+    last_out = several(out_ring, 1, events)
     output = out_ring.result()
     gate_grad, up_grad = grads_strips.outs
 
@@ -399,8 +406,8 @@
     def swap(sent):
         return lax.ppermute(sent, "dp", [(0, 1), (1, 0)])
 
-    sent = theirs(0, events)
-    events = several(in_ring, 1, events) + (sent,)
+    sent = theirs(0, token)
+    events = several(in_ring, 1) + last_out + (sent,)
     down_arrived = swap(sent)
     sent = [theirs(1, events), theirs(2, events)]
     events = several(in_ring, 1, events) + (*sent, down_arrived)

time: 187 us -> 195 us (1.043)
  waiting for transfers between devices: 42.1 us -> 48.4 us
  Pallas kernels: 86.7 us -> 88.8 us
    ppermute x16, waiting for transfers between devices: 15.2 us -> 21.7 us  [to_left(): return lax.ppermute(value, 'tensor', back)]
    pallas_call x7 -> x9, Pallas kernels: 59.1 us -> 61.2 us  [run(): pl.pallas_call(kernel, grid=(count,), in_specs=in_specs, out_specs=[strip...]
    ppermute x16, starting transfers between devices: 12.3 us -> 14.2 us  [to_left(): return lax.ppermute(value, 'tensor', back)]
    unnamed x53 -> x41, local copies, waits for them, and re-layouts: 6.18 us -> 6.16 us
  transfers between devices with their start and end apart: 35 -> 35, of which waited for: 19 -> 18; matrix products, arithmetic and copies ran while one was open for 8% -> 7% of each run, Pallas kernels for 46% -> 43%
where the time goes in v4:
time: 195 us
  Pallas kernels  88.8 us (46%)
  waiting for transfers between devices  48.4 us (25%)
  starting transfers between devices  35.5 us (18%)
  local copies, waits for them, and re-layouts  18.1 us (9%)
  other arithmetic  3.42 us (2%)
    pallas_call x9, Pallas kernels, run(): pl.pallas_call(kernel, grid=(count,), in_specs=in_specs, out_specs=[strip...  61.2 us
    pallas_call x6, Pallas kernels, block_grads(): pl.pallas_call(kernel, grid=(count // group,), in_specs=[SMEM_SPEC] + [wh...  27.6 us
    ppermute x16, waiting for transfers between devices, to_right(): return lax.ppermute(value, 'tensor', ahead)  26.7 us
    ppermute x16, waiting for transfers between devices, to_left(): return lax.ppermute(value, 'tensor', back)  21.7 us
    ppermute x16, starting transfers between devices, to_right(): return lax.ppermute(value, 'tensor', ahead)  20.5 us
    ppermute x16, starting transfers between devices, to_left(): return lax.ppermute(value, 'tensor', back)  14.2 us
    concatenate x3, local copies, waits for them, and re-layouts, with_zero(): jnp.concatenate([blocks, jnp.zeros((1,) + blocks.shape[1:], blocks.dtype)...  11.5 us
    unnamed x41, local copies, waits for them, and re-layouts  6.16 us
  transfers between devices with their start and end apart: 35, of which 18 were waited for; matrix products, arithmetic and copies ran while one was open for 7% of the time, Pallas kernels for 43%

profile of v4, /device:TPU:0, one launch (start us, length us, event | category | flops | bytes accessed | tf_op | source)
XLA Modules:
  0.0 195.2 jit_solution(17429839071925037159)
XLA Ops:
  0.7 3.1 %collective-permute-start = (bf16[48,5120]{1,0:T(8,128)(2,1)}, bf16[48,5120]{1,0:T(8,128)(2,1)S(1)}, u32[]{:S(2)}, u32[]{:S(2)}) collective-permute-start(bf16[48,5120]{1,0:T(8,128)(2,1)} %param.8), channel_id=1, source_target_pairs={{0,4},{4,8},{8,12},{12,14},{14,10},{10,6},{6,2},{2,0},{1,5},{5,9},... | collective-permute-start | bytes 1474568 | tf_op jit(solution)/shard_map/ppermute | solution.py:27
  3.7 4.5 %concatenate.30.refs_3_.refs_4_ = bf16[121,128,128]{2,1,0:T(8,128)(2,1)} pad(bf16[120,128,128]{2,1,0:T(8,128)(2,1)} %param.10, bf16[]{:T(256)} %constant.1.clone.1), padding=0_1x0_0x0_0 | pad | bytes 7897090 | tf_op jit(solution)/shard_map/concatenate | solution.py:107
  8.5 6.6 %collective-permute-done = bf16[48,5120]{1,0:T(8,128)(2,1)S(1)} collective-permute-done((bf16[48,5120]{1,0:T(8,128)(2,1)}, bf16[48,5120]{1,0:T(8,128)(2,1)S(1)}, u32[]{:S(2)}, u32[]{:S(2)}) %collective-permute-start) | collective-permute-done | bytes 491552 | tf_op jit(solution)/shard_map/ppermute | solution.py:27
  18.6 4.7 %concatenate.31.refs_4_.refs_5_ = bf16[121,128,128]{2,1,0:T(8,128)(2,1)} pad(bf16[120,128,128]{2,1,0:T(8,128)(2,1)} %param.11, bf16[]{:T(256)} %constant.1.clone.1), padding=0_1x0_0x0_0 | pad | bytes 7897090 | tf_op jit(solution)/shard_map/concatenate | solution.py:107
  36.1 5.1 %shard_map.119 = (bf16[384,1536]{1,0:T(8,128)(2,1)S(1)}, f32[384,1536]{1,0:T(8,128)S(1)}, f32[384,1536]{1,0:T(8,128)S(1)}, s32[8,128]{1,0:T(8,128)}) custom-call(s32[480]{0:T(512)S(1)} %get-tuple-element.161.refs_0_, s32[480]{0:T(512)S(1)} %get-tuple-element.199.refs_1_, bf16[192,5120]{1,0:T(8,128)(2,1)S(1)} %constant_dynamic-update-slice_fusion.refs_2_.refs_0_, ...), custom_call_target="tpu_custom_call" | custom-call | flops 6039797760 | bytes 8388608 | tf_op jit(solution)/shard_map/pallas_call | solution.py:222
  45.8 5.1 %shard_map.120 = (bf16[384,1536]{1,0:T(8,128)(2,1)S(1)}, f32[384,1536]{1,0:T(8,128)S(1)}, f32[384,1536]{1,0:T(8,128)S(1)}, s32[8,128]{1,0:T(8,128)}) custom-call(s32[480]{0:T(512)S(1)} %get-tuple-element.161.refs_0_, s32[480]{0:T(512)S(1)} %get-tuple-element.199.refs_1_, ...), custom_call_target="tpu_custom_call", output_to_operand_aliasing={{0}: (5, {}), {1}: (6, {}), {2}: (7, {})} | custom-call | flops 6039797760 | bytes 8388608 | tf_op jit(solution)/shard_map/pallas_call | solution.py:222
  50.9 6.3 %collective-permute-done.8 = bf16[24,5120]{1,0:T(8,128)(2,1)S(1)} collective-permute-done((bf16[24,5120]{1,0:T(8,128)(2,1)S(1)}, bf16[24,5120]{1,0:T(8,128)(2,1)S(1)}, u32[]{:S(2)}, u32[]{:S(2)}) %collective-permute-start.8) | collective-permute-done | bytes 245792 | tf_op jit(solution)/shard_map/ppermute | solution.py:27
  60.6 8.9 %shard_map.121 = (bf16[384,1536]{1,0:T(8,128)(2,1)S(1)}, f32[384,1536]{1,0:T(8,128)S(1)}, f32[384,1536]{1,0:T(8,128)S(1)}, s32[8,128]{1,0:T(8,128)}) custom-call(s32[480]{0:T(512)S(1)} %get-tuple-element.161.refs_0_, s32[480]{0:T(512)S(1)} %get-tuple-element.199.refs_1_, ...), custom_call_target="tpu_custom_call", output_to_operand_aliasing={{0}: (5, {}), {1}: (6, {}), {2}: (7, {})} | custom-call | flops 12079595520 | bytes 8388608 | tf_op jit(solution)/shard_map/pallas_call | solution.py:222
  73.0 11.4 %shard_map.122 = (f32[336,5120]{1,0:T(8,128)S(1)}, bf16[48,5120]{1,0:T(8,128)(2,1)S(1)}, s32[8,128]{1,0:T(8,128)}) custom-call(s32[480]{0:T(512)S(1)} %select_reduce_fusion.2.refs_0_, bf16[384,1536]{1,0:T(8,128)(2,1)S(1)} %get-tuple-element.123.refs_1_, bf16[121,128,128]{2,1,0:T(8,128)(2,1)S(1)} %copy-done.4), custom_call_target="tpu_custom_call" | custom-call | flops 12079595520 | bytes 8388608 | tf_op jit(solution)/shard_map/pallas_call | solution.py:222
  86.6 6.1 %collective-permute-done.14 = bf16[24,5120]{1,0:T(8,128)(2,1)S(1)} collective-permute-done((bf16[24,5120]{1,0:T(8,128)(2,1)S(1)}, bf16[24,5120]{1,0:T(8,128)(2,1)S(1)}, u32[]{:S(2)}, u32[]{:S(2)}) %collective-permute-start.14) | collective-permute-done | bytes 245792 | tf_op jit(solution)/shard_map/ppermute | solution.py:27
  95.1 5.1 %shard_map.123 = (bf16[384,1536]{1,0:T(8,128)(2,1)S(1)}, bf16[384,1536]{1,0:T(8,128)(2,1)S(1)}, s32[8,128]{1,0:T(8,128)}) custom-call(s32[480]{0:T(512)S(1)} %select_reduce_fusion.2.refs_0_, bf16[384,5120]{1,0:T(8,128)(2,1)S(1)} %constant_dynamic-update-slice_fusion.9.refs_1_.refs_0_, bf16[121,128,128]{2,1,0:T(8,128)(2,1)S(1)} %copy-done.4, ...), custom_call_target="tpu_custom_call" | custom-call | flops 6039797760 | bytes 8388608 | tf_op jit(solution)/shard_map/pallas_call | solution.py:222
  104.2 5.1 %shard_map.124 = (bf16[384,1536]{1,0:T(8,128)(2,1)S(1)}, bf16[384,1536]{1,0:T(8,128)(2,1)S(1)}, s32[8,128]{1,0:T(8,128)}) custom-call(s32[480]{0:T(512)S(1)} %select_reduce_fusion.2.refs_0_, bf16[384,5120]{1,0:T(8,128)(2,1)S(1)} %constant_dynamic-update-slice_fusion.9.refs_1_.refs_0_, ...), custom_call_target="tpu_custom_call", output_to_operand_aliasing={{0}: (5, {}), {1}: (6, {})} | custom-call | flops 6039797760 | bytes 8388608 | tf_op jit(solution)/shard_map/pallas_call | solution.py:222
  109.3 5.4 %shard_map.125 = (f32[336,5120]{1,0:T(8,128)S(1)}, bf16[48,5120]{1,0:T(8,128)(2,1)S(1)}, s32[8,128]{1,0:T(8,128)}) custom-call(s32[480]{0:T(512)S(1)} %get-tuple-element.161.refs_0_, s32[480]{0:T(512)S(1)} %get-tuple-element.199.refs_1_, bf16[384,1536]{1,0:T(8,128)(2,1)S(1)} %get-tuple-element.150.refs_2_, ...), custom_call_target="tpu_custom_call" | custom-call | flops 6039797760 | bytes 8388608 | tf_op jit(solution)/shard_map/pallas_call | solution.py:222
  115.6 2.7 %collective-permute-start.21 = (bf16[48,5120]{1,0:T(8,128)(2,1)S(1)}, bf16[48,5120]{1,0:T(8,128)(2,1)S(1)}, u32[]{:S(2)}, u32[]{:S(2)}) collective-permute-start(bf16[48,5120]{1,0:T(8,128)(2,1)S(1)} %get-tuple-element.154), channel_id=1, source_target_pairs={{4,0},{8,4},{12,8},{14,12},{10,14},{6,10},{2,6},{0,2},{5,1},{9,5},... | collective-permute-start | bytes 1474568 | tf_op jit(solution)/shard_map/ppermute | solution.py:30
  118.3 9.7 %shard_map.126 = (f32[336,5120]{1,0:T(8,128)S(1)}, bf16[48,5120]{1,0:T(8,128)(2,1)S(1)}, s32[8,128]{1,0:T(8,128)}) custom-call(s32[480]{0:T(512)S(1)} %get-tuple-element.161.refs_0_, s32[480]{0:T(512)S(1)} %get-tuple-element.199.refs_1_, bf16[384,1536]{1,0:T(8,128)(2,1)S(1)} %get-tuple-element.150.refs_2_, ...), custom_call_target="tpu_custom_call", output_to_operand_aliasing={{0}: (6, {}), {1}: (7, {})} | custom-call | flops 12079595520 | bytes 8388608 | tf_op jit(solution)/shard_map/pallas_call | solution.py:222
  128.2 5.4 %shard_map.127 = (f32[336,5120]{1,0:T(8,128)S(1)}, bf16[48,5120]{1,0:T(8,128)(2,1)S(1)}, s32[8,128]{1,0:T(8,128)}) custom-call(s32[480]{0:T(512)S(1)} %get-tuple-element.161.refs_0_, s32[480]{0:T(512)S(1)} %get-tuple-element.199.refs_1_, bf16[384,1536]{1,0:T(8,128)(2,1)S(1)} %get-tuple-element.150.refs_2_, ...), custom_call_target="tpu_custom_call", output_to_operand_aliasing={{0}: (6, {}), {1}: (7, {})} | custom-call | flops 6039797760 | bytes 8388608 | tf_op jit(solution)/shard_map/pallas_call | solution.py:222
  135.8 3.8 %shard_map.128 = bf16[60,128,128]{2,1,0:T(8,128)(2,1)S(1)} custom-call(s32[60]{0:T(128)S(1)} %get-tuple-element.198.at, bf16[384,5120]{1,0:T(8,128)(2,1)S(1)} %constant_dynamic-update-slice_fusion.9.refs_1_.refs_0_, bf16[384,1536]{1,0:T(8,128)(2,1)S(1)} %get-tuple-element.123.refs_1_), custom_call_target="tpu_custom_call" | custom-call | flops 3019898880 | bytes 8388608 | tf_op jit(solution)/shard_map/pallas_call | solution.py:273
  142.1 11.2 %collective-permute-done.23 = bf16[48,5120]{1,0:T(8,128)(2,1)S(1)} collective-permute-done((bf16[48,5120]{1,0:T(8,128)(2,1)S(1)}, bf16[48,5120]{1,0:T(8,128)(2,1)S(1)}, u32[]{:S(2)}, u32[]{:S(2)}) %collective-permute-start.23) | collective-permute-done | bytes 491552 | tf_op jit(solution)/shard_map/ppermute | solution.py:30
  157.1 4.0 %shard_map.129 = bf16[60,128,128]{2,1,0:T(8,128)(2,1)S(1)} custom-call(s32[60]{0:T(128)S(1)} %get-tuple-element.168.at, bf16[192,5120]{1,0:T(8,128)(2,1)S(1)} %constant_dynamic-update-slice_fusion.refs_2_.refs_0_, bf16[192,5120]{1,0:T(8,128)(2,1)S(1)} %constant_dynamic-update-slice_fusion.4.refs_2_.refs_1_, bf16[384,1536]{1,0:T(8,128)(2,1)S(1)} %get-tuple-element.150.refs_2_), custom_call_target="tpu_custom_call" | custom-call | flops 3019898880 | bytes 8388608 | tf_op jit(solution)/shard_map/pallas_call | solution.py:273
  161.2 4.0 %shard_map.130 = bf16[60,128,128]{2,1,0:T(8,128)(2,1)S(1)} custom-call(s32[60]{0:T(128)S(1)} %get-tuple-element.169.at, bf16[192,5120]{1,0:T(8,128)(2,1)S(1)} %constant_dynamic-update-slice_fusion.refs_2_.refs_0_, bf16[192,5120]{1,0:T(8,128)(2,1)S(1)} %constant_dynamic-update-slice_fusion.4.refs_2_.refs_1_, ...), custom_call_target="tpu_custom_call" | custom-call | flops 3019898880 | bytes 8388608 | tf_op jit(solution)/shard_map/pallas_call | solution.py:273
  172.1 5.2 %shard_map.131 = f32[60,128,128]{2,1,0:T(8,128)} custom-call(s32[60]{0:T(128)S(1)} %get-tuple-element.172.at, bf16[384,5120]{1,0:T(8,128)(2,1)S(1)} %constant_dynamic-update-slice_fusion.9.refs_1_.refs_0_, bf16[384,1536]{1,0:T(8,128)(2,1)S(1)} %get-tuple-element.123.refs_1_, bf16[60,128,128]{2,1,0:T(8,128)(2,1)S(1)} %collective-permute-done.28.refs_2_), custom_call_target="tpu_custom_call" | custom-call | flops 3019898880 | bytes 8388608 | tf_op jit(solution)/shard_map/pallas_call | solution.py:273
  177.3 3.1 %collective-permute-done.30 = bf16[48,5120]{1,0:T(8,128)(2,1)S(1)} collective-permute-done((bf16[48,5120]{1,0:T(8,128)(2,1)S(1)}, bf16[48,5120]{1,0:T(8,128)(2,1)S(1)}, u32[]{:S(2)}, u32[]{:S(2)}) %collective-permute-start.30) | collective-permute-done | bytes 491552 | tf_op jit(solution)/shard_map/ppermute | solution.py:30
  183.7 5.3 %shard_map.132 = f32[60,128,128]{2,1,0:T(8,128)} custom-call(s32[60]{0:T(128)S(1)} %get-tuple-element.175.at, bf16[192,5120]{1,0:T(8,128)(2,1)S(1)} %constant_dynamic-update-slice_fusion.refs_2_.refs_0_, bf16[192,5120]{1,0:T(8,128)(2,1)S(1)} %constant_dynamic-update-slice_fusion.4.refs_2_.refs_1_, bf16[384,1536]{1,0:T(8,128)(2,1)S(1)} %get-tuple-element.150.refs_2_, ...), custom_call_target="tpu_custom_call" | custom-call | flops 3019898880 | bytes 8388608 | tf_op jit(solution)/shard_map/pallas_call | solution.py:273
  188.9 5.3 %shard_map.133 = f32[60,128,128]{2,1,0:T(8,128)} custom-call(s32[60]{0:T(128)S(1)} %get-tuple-element.176.at, bf16[192,5120]{1,0:T(8,128)(2,1)S(1)} %constant_dynamic-update-slice_fusion.refs_2_.refs_0_, bf16[192,5120]{1,0:T(8,128)(2,1)S(1)} %constant_dynamic-update-slice_fusion.4.refs_2_.refs_1_, bf16[384,1536]{1,0:T(8,128)(2,1)S(1)} %get-tuple-element.151.refs_3_.refs_2_, ...), custom_call_target="tpu_custom_call" | custom-call | flops 3019898880 | bytes 8388608 | tf_op jit(solution)/shard_map/pallas_call | solution.py:273
  (127 shorter events, 57.0 us)
Async XLA Ops:
  0.7 14.5 %collective-permute-start = (bf16[48,5120]{1,0:T(8,128)(2,1)}, bf16[48,5120]{1,0:T(8,128)(2,1)S(1)}, u32[]{:S(2)}, u32[]{:S(2)}) collective-permute-start(bf16[48,5120]{1,0:T(8,128)(2,1)} %param.8), channel_id=1, source_target_pairs={{0,4},{4,8},{8,12},{12,14},{14,10},{10,6},{6,2},{2,0},{1,5},{5,9},... | collective-permute-start | bytes 1474568 | tf_op jit(solution)/shard_map/ppermute | solution.py:27
  3.7 12.9 %collective-permute-start.1 = (bf16[48,5120]{1,0:T(8,128)(2,1)}, bf16[48,5120]{1,0:T(8,128)(2,1)S(1)}, u32[]{:S(2)}, u32[]{:S(2)}) collective-permute-start(bf16[48,5120]{1,0:T(8,128)(2,1)} %param.8), channel_id=1, source_target_pairs={{4,0},{8,4},{12,8},{14,12},{10,14},{6,10},{2,6},{0,2},{5,1},{9,5},... | collective-permute-start | bytes 1474568 | tf_op jit(solution)/shard_map/ppermute | solution.py:30
  16.6 11.8 %collective-permute-start.2 = (bf16[48,5120]{1,0:T(8,128)(2,1)S(1)}, bf16[48,5120]{1,0:T(8,128)(2,1)S(1)}, u32[]{:S(2)}, u32[]{:S(2)}) collective-permute-start(bf16[48,5120]{1,0:T(8,128)(2,1)S(1)} %collective-permute-done), channel_id=1, source_target_pairs={{0,4},{4,8},{8,12},{12,14},{14,10},{10,6},{6,2},{2,0},{1,5},{5,9},... | collective-permute-start | bytes 1474568 | tf_op jit(solution)/shard_map/ppermute | solution.py:27
  18.2 11.5 %collective-permute-start.3 = (bf16[48,5120]{1,0:T(8,128)(2,1)S(1)}, bf16[48,5120]{1,0:T(8,128)(2,1)S(1)}, u32[]{:S(2)}, u32[]{:S(2)}) collective-permute-start(bf16[48,5120]{1,0:T(8,128)(2,1)S(1)} %collective-permute-done.1), channel_id=1, source_target_pairs={{4,0},{8,4},{12,8},{14,12},{10,14},{6,10},{2,6},{0,2},{5,1},{9,5},... | collective-permute-start | bytes 1474568 | tf_op jit(solution)/shard_map/ppermute | solution.py:30
  29.7 11.5 %collective-permute-start.4 = (bf16[48,5120]{1,0:T(8,128)(2,1)S(1)}, bf16[48,5120]{1,0:T(8,128)(2,1)S(1)}, u32[]{:S(2)}, u32[]{:S(2)}) collective-permute-start(bf16[48,5120]{1,0:T(8,128)(2,1)S(1)} %collective-permute-done.2), channel_id=1, source_target_pairs={{0,4},{4,8},{8,12},{12,14},{14,10},{10,6},{6,2},{2,0},{1,5},{5,9},... | collective-permute-start | bytes 1474568 | tf_op jit(solution)/shard_map/ppermute | solution.py:27
  41.6 16.7 %collective-permute-start.6 = (bf16[48,5120]{1,0:T(8,128)(2,1)S(1)}, bf16[48,5120]{1,0:T(8,128)(2,1)S(1)}, u32[]{:S(2)}, u32[]{:S(2)}) collective-permute-start(bf16[48,5120]{1,0:T(8,128)(2,1)S(1)} %copy-done.9), channel_id=1, source_target_pairs={{0,4},{4,8},{8,12},{12,14},{14,10},{10,6},{6,2},{2,0},{1,5},{5,9},... | collective-permute-start | bytes 1474568 | tf_op jit(solution)/shard_map/ppermute | solution.py:27
  43.1 15.2 %collective-permute-start.7 = (bf16[48,5120]{1,0:T(8,128)(2,1)S(1)}, bf16[48,5120]{1,0:T(8,128)(2,1)S(1)}, u32[]{:S(2)}, u32[]{:S(2)}) collective-permute-start(bf16[48,5120]{1,0:T(8,128)(2,1)S(1)} %copy-done.9), channel_id=1, source_target_pairs={{4,0},{8,4},{12,8},{14,12},{10,14},{6,10},{2,6},{0,2},{5,1},{9,5},... | collective-permute-start | bytes 1474568 | tf_op jit(solution)/shard_map/ppermute | solution.py:30
  43.6 13.5 %collective-permute-start.8 = (bf16[24,5120]{1,0:T(8,128)(2,1)S(1)}, bf16[24,5120]{1,0:T(8,128)(2,1)S(1)}, u32[]{:S(2)}, u32[]{:S(2)}) collective-permute-start(bf16[24,5120]{1,0:T(8,128)(2,1)S(1)} %slice.69), channel_id=1, source_target_pairs={{0,4},{4,8},{8,12},{12,14},{14,10},{10,6},{6,2},{2,0},{1,5},{5,9},... | collective-permute-start | bytes 737288 | tf_op jit(solution)/shard_map/ppermute | solution.py:27
  45.2 13.1 %collective-permute-start.9 = (bf16[24,5120]{1,0:T(8,128)(2,1)S(1)}, bf16[24,5120]{1,0:T(8,128)(2,1)S(1)}, u32[]{:S(2)}, u32[]{:S(2)}) collective-permute-start(bf16[24,5120]{1,0:T(8,128)(2,1)S(1)} %slice.70), channel_id=1, source_target_pairs={{4,0},{8,4},{12,8},{14,12},{10,14},{6,10},{2,6},{0,2},{5,1},{9,5},... | collective-permute-start | bytes 737288 | tf_op jit(solution)/shard_map/ppermute | solution.py:30
  58.3 12.7 %collective-permute-start.10 = (bf16[48,5120]{1,0:T(8,128)(2,1)S(1)}, bf16[48,5120]{1,0:T(8,128)(2,1)S(1)}, u32[]{:S(2)}, u32[]{:S(2)}) collective-permute-start(bf16[48,5120]{1,0:T(8,128)(2,1)S(1)} %collective-permute-done.6), channel_id=1, source_target_pairs={{0,4},{4,8},{8,12},{12,14},{14,10},{10,6},{6,2},{2,0},{1,5},{5,9},... | collective-permute-start | bytes 1474568 | tf_op jit(solution)/shard_map/ppermute | solution.py:27
  70.9 13.4 %collective-permute-start.12 = (bf16[48,5120]{1,0:T(8,128)(2,1)S(1)}, bf16[48,5120]{1,0:T(8,128)(2,1)S(1)}, u32[]{:S(2)}, u32[]{:S(2)}) collective-permute-start(bf16[48,5120]{1,0:T(8,128)(2,1)S(1)} %collective-permute-done.10), channel_id=1, source_target_pairs={{0,4},{4,8},{8,12},{12,14},{14,10},{10,6},{6,2},{2,0},{1,5},{5,9},... | collective-permute-start | bytes 1474568 | tf_op jit(solution)/shard_map/ppermute | solution.py:27
  73.0 11.4 %collective-permute-start.13 = (bf16[48,5120]{1,0:T(8,128)(2,1)S(1)}, bf16[48,5120]{1,0:T(8,128)(2,1)S(1)}, u32[]{:S(2)}, u32[]{:S(2)}) collective-permute-start(bf16[48,5120]{1,0:T(8,128)(2,1)S(1)} %collective-permute-done.11), channel_id=1, source_target_pairs={{4,0},{8,4},{12,8},{14,12},{10,14},{6,10},{2,6},{0,2},{5,1},{9,5},... | collective-permute-start | bytes 1474568 | tf_op jit(solution)/shard_map/ppermute | solution.py:30
  102.1 12.6 %collective-permute-start.19 = (bf16[48,5120]{1,0:T(8,128)(2,1)S(1)}, bf16[48,5120]{1,0:T(8,128)(2,1)S(1)}, u32[]{:S(2)}, u32[]{:S(2)}) collective-permute-start(bf16[48,5120]{1,0:T(8,128)(2,1)S(1)} %get-tuple-element.146), channel_id=1, source_target_pairs={{4,0},{8,4},{12,8},{14,12},{10,14},{6,10},{2,6},{0,2},{5,1},{9,5},... | collective-permute-start | bytes 1474568 | tf_op jit(solution)/shard_map/ppermute | solution.py:30
  102.7 12.6 %collective-permute-start.18 = (bf16[48,5120]{1,0:T(8,128)(2,1)S(1)}, bf16[48,5120]{1,0:T(8,128)(2,1)S(1)}, u32[]{:S(2)}, u32[]{:S(2)}) collective-permute-start(bf16[48,5120]{1,0:T(8,128)(2,1)S(1)} %get-tuple-element.145), channel_id=1, source_target_pairs={{0,4},{4,8},{8,12},{12,14},{14,10},{10,6},{6,2},{2,0},{1,5},{5,9},... | collective-permute-start | bytes 1474568 | tf_op jit(solution)/shard_map/ppermute | solution.py:27
  115.6 12.4 %collective-permute-start.21 = (bf16[48,5120]{1,0:T(8,128)(2,1)S(1)}, bf16[48,5120]{1,0:T(8,128)(2,1)S(1)}, u32[]{:S(2)}, u32[]{:S(2)}) collective-permute-start(bf16[48,5120]{1,0:T(8,128)(2,1)S(1)} %get-tuple-element.154), channel_id=1, source_target_pairs={{4,0},{8,4},{12,8},{14,12},{10,14},{6,10},{2,6},{0,2},{5,1},{9,5},... | collective-permute-start | bytes 1474568 | tf_op jit(solution)/shard_map/ppermute | solution.py:30
  139.6 29.5 %collective-permute-start.28 = (bf16[60,128,128]{2,1,0:T(8,128)(2,1)S(1)}, bf16[60,128,128]{2,1,0:T(8,128)(2,1)S(1)}, u32[]{:S(2)}, u32[]{:S(2)}) collective-permute-start(bf16[60,128,128]{2,1,0:T(8,128)(2,1)S(1)} %shard_map.128), channel_id=1, source_target_pairs={{0,1},{1,0},{2,3},{3,2},{4,5},{5,4},{6,7},{7,6},{8,9},{9,8},{10,11... | collective-permute-start | bytes 5898248 | tf_op jit(solution)/shard_map/ppermute | solution.py:407
  139.7 13.6 %collective-permute-start.23 = (bf16[48,5120]{1,0:T(8,128)(2,1)S(1)}, bf16[48,5120]{1,0:T(8,128)(2,1)S(1)}, u32[]{:S(2)}, u32[]{:S(2)}) collective-permute-start(bf16[48,5120]{1,0:T(8,128)(2,1)S(1)} %get-tuple-element.160), channel_id=1, source_target_pairs={{4,0},{8,4},{12,8},{14,12},{10,14},{6,10},{2,6},{0,2},{5,1},{9,5},... | collective-permute-start | bytes 1474568 | tf_op jit(solution)/shard_map/ppermute | solution.py:30
  141.7 13.3 %collective-permute-start.22 = (bf16[48,5120]{1,0:T(8,128)(2,1)S(1)}, bf16[48,5120]{1,0:T(8,128)(2,1)S(1)}, u32[]{:S(2)}, u32[]{:S(2)}) collective-permute-start(bf16[48,5120]{1,0:T(8,128)(2,1)S(1)} %get-tuple-element.159), channel_id=1, source_target_pairs={{0,4},{4,8},{8,12},{12,14},{14,10},{10,6},{6,2},{2,0},{1,5},{5,9},... | collective-permute-start | bytes 1474568 | tf_op jit(solution)/shard_map/ppermute | solution.py:27
  155.0 12.5 %collective-permute-start.27 = (bf16[48,5120]{1,0:T(8,128)(2,1)S(1)}, bf16[48,5120]{1,0:T(8,128)(2,1)S(1)}, u32[]{:S(2)}, u32[]{:S(2)}) collective-permute-start(bf16[48,5120]{1,0:T(8,128)(2,1)S(1)} %get-tuple-element.167), channel_id=1, source_target_pairs={{4,0},{8,4},{12,8},{14,12},{10,14},{6,10},{2,6},{0,2},{5,1},{9,5},... | collective-permute-start | bytes 1474568 | tf_op jit(solution)/shard_map/ppermute | solution.py:30
  156.7 12.2 %collective-permute-start.26 = (bf16[48,5120]{1,0:T(8,128)(2,1)S(1)}, bf16[48,5120]{1,0:T(8,128)(2,1)S(1)}, u32[]{:S(2)}, u32[]{:S(2)}) collective-permute-start(bf16[48,5120]{1,0:T(8,128)(2,1)S(1)} %get-tuple-element.166), channel_id=1, source_target_pairs={{0,4},{4,8},{8,12},{12,14},{14,10},{10,6},{6,2},{2,0},{1,5},{5,9},... | collective-permute-start | bytes 1474568 | tf_op jit(solution)/shard_map/ppermute | solution.py:27
  161.1 20.5 %collective-permute-start.31 = (bf16[60,128,128]{2,1,0:T(8,128)(2,1)S(1)}, bf16[60,128,128]{2,1,0:T(8,128)(2,1)S(1)}, u32[]{:S(2)}, u32[]{:S(2)}) collective-permute-start(bf16[60,128,128]{2,1,0:T(8,128)(2,1)S(1)} %shard_map.129), channel_id=1, source_target_pairs={{0,1},{1,0},{2,3},{3,2},{4,5},{5,4},{6,7},{7,6},{8,9},{9,8},{10,11... | collective-permute-start | bytes 5898248 | tf_op jit(solution)/shard_map/ppermute | solution.py:407
  165.2 16.4 %collective-permute-start.32 = (bf16[60,128,128]{2,1,0:T(8,128)(2,1)S(1)}, bf16[60,128,128]{2,1,0:T(8,128)(2,1)S(1)}, u32[]{:S(2)}, u32[]{:S(2)}) collective-permute-start(bf16[60,128,128]{2,1,0:T(8,128)(2,1)S(1)} %shard_map.130), channel_id=1, source_target_pairs={{0,1},{1,0},{2,3},{3,2},{4,5},{5,4},{6,7},{7,6},{8,9},{9,8},{10,11... | collective-permute-start | bytes 5898248 | tf_op jit(solution)/shard_map/ppermute | solution.py:407
  169.1 11.3 %collective-permute-start.30 = (bf16[48,5120]{1,0:T(8,128)(2,1)S(1)}, bf16[48,5120]{1,0:T(8,128)(2,1)S(1)}, u32[]{:S(2)}, u32[]{:S(2)}) collective-permute-start(bf16[48,5120]{1,0:T(8,128)(2,1)S(1)} %get-tuple-element.171), channel_id=1, source_target_pairs={{4,0},{8,4},{12,8},{14,12},{10,14},{6,10},{2,6},{0,2},{5,1},{9,5},... | collective-permute-start | bytes 1474568 | tf_op jit(solution)/shard_map/ppermute | solution.py:30
  181.6 12.7 %collective-permute-start.34 = (bf16[48,5120]{1,0:T(8,128)(2,1)S(1)}, bf16[48,5120]{1,0:T(8,128)(2,1)S(1)}, u32[]{:S(2)}, u32[]{:S(2)}) collective-permute-start(bf16[48,5120]{1,0:T(8,128)(2,1)S(1)} %get-tuple-element.174), channel_id=1, source_target_pairs={{4,0},{8,4},{12,8},{14,12},{10,14},{6,10},{2,6},{0,2},{5,1},{9,5},... | collective-permute-start | bytes 1474568 | tf_op jit(solution)/shard_map/ppermute | solution.py:30
  (24 other events, 185.3 us)

commit v5 on v4

--- a/solution.py
+++ b/solution.py
@@ -406,7 +406,7 @@
     def swap(sent):
         return lax.ppermute(sent, "dp", [(0, 1), (1, 0)])
 
-    sent = theirs(0, token)
+    sent = theirs(0, token + last_out)
     events = several(in_ring, 1) + last_out + (sent,)
     down_arrived = swap(sent)
     sent = [theirs(1, events), theirs(2, events)]

time: 195 us -> 189 us (0.969)
  waiting for transfers between devices: 48.4 us -> 41.7 us
    ppermute x16, waiting for transfers between devices: 21.7 us -> 12.7 us  [to_left(): return lax.ppermute(value, 'tensor', back)]
    ppermute x16, waiting for transfers between devices: 26.7 us -> 29 us  [to_right(): return lax.ppermute(value, 'tensor', ahead)]
  transfers between devices with their start and end apart: 35 -> 35, of which waited for: 18 -> 19; matrix products, arithmetic and copies ran while one was open for 7% -> 8% of each run, Pallas kernels for 43% -> 47%
where the time goes in v5:
time: 189 us; the launch traced here: 188 us
  Pallas kernels  88.7 us (47%)
  waiting for transfers between devices  41.7 us (22%)
  starting transfers between devices  35.5 us (19%)
  local copies, waits for them, and re-layouts  18.1 us (10%)
  other arithmetic  3.46 us (2%)
    pallas_call x9, Pallas kernels, run(): pl.pallas_call(kernel, grid=(count,), in_specs=in_specs, out_specs=[strip...  61.2 us
    ppermute x16, waiting for transfers between devices, to_right(): return lax.ppermute(value, 'tensor', ahead)  29 us
    pallas_call x6, Pallas kernels, block_grads(): pl.pallas_call(kernel, grid=(count // group,), in_specs=[SMEM_SPEC] + [wh...  27.6 us
    ppermute x16, starting transfers between devices, to_right(): return lax.ppermute(value, 'tensor', ahead)  22.1 us
    ppermute x16, waiting for transfers between devices, to_left(): return lax.ppermute(value, 'tensor', back)  12.7 us
    ppermute x16, starting transfers between devices, to_left(): return lax.ppermute(value, 'tensor', back)  12.7 us
    concatenate x3, local copies, waits for them, and re-layouts, with_zero(): jnp.concatenate([blocks, jnp.zeros((1,) + blocks.shape[1:], blocks.dtype)...  11.5 us
    unnamed x41, local copies, waits for them, and re-layouts  6.16 us
  transfers between devices with their start and end apart: 35, of which 19 were waited for; matrix products, arithmetic and copies ran while one was open for 8% of the time, Pallas kernels for 47%

profile of v5, /device:TPU:0, one launch (start us, length us, event | category | flops | bytes accessed | tf_op | source)
XLA Modules:
  0.0 188.5 jit_solution(5462836755627462399)
XLA Ops:
  0.7 3.1 %collective-permute-start = (bf16[48,5120]{1,0:T(8,128)(2,1)}, bf16[48,5120]{1,0:T(8,128)(2,1)S(1)}, u32[]{:S(2)}, u32[]{:S(2)}) collective-permute-start(bf16[48,5120]{1,0:T(8,128)(2,1)} %param.8), channel_id=1, source_target_pairs={{0,4},{4,8},{8,12},{12,14},{14,10},{10,6},{6,2},{2,0},{1,5},{5,9},... | collective-permute-start | bytes 1474568 | tf_op jit(solution)/shard_map/ppermute | solution.py:27
  3.7 4.5 %concatenate.30.refs_3_.refs_4_ = bf16[121,128,128]{2,1,0:T(8,128)(2,1)} pad(bf16[120,128,128]{2,1,0:T(8,128)(2,1)} %param.10, bf16[]{:T(256)} %constant.1.clone.1), padding=0_1x0_0x0_0 | pad | bytes 7897090 | tf_op jit(solution)/shard_map/concatenate | solution.py:107
  8.5 6.6 %collective-permute-done = bf16[48,5120]{1,0:T(8,128)(2,1)S(1)} collective-permute-done((bf16[48,5120]{1,0:T(8,128)(2,1)}, bf16[48,5120]{1,0:T(8,128)(2,1)S(1)}, u32[]{:S(2)}, u32[]{:S(2)}) %collective-permute-start) | collective-permute-done | bytes 491552 | tf_op jit(solution)/shard_map/ppermute | solution.py:27
  18.6 4.7 %concatenate.31.refs_4_.refs_5_ = bf16[121,128,128]{2,1,0:T(8,128)(2,1)} pad(bf16[120,128,128]{2,1,0:T(8,128)(2,1)} %param.11, bf16[]{:T(256)} %constant.1.clone.1), padding=0_1x0_0x0_0 | pad | bytes 7897090 | tf_op jit(solution)/shard_map/concatenate | solution.py:107
  36.1 5.1 %shard_map.119 = (bf16[384,1536]{1,0:T(8,128)(2,1)S(1)}, f32[384,1536]{1,0:T(8,128)S(1)}, f32[384,1536]{1,0:T(8,128)S(1)}, s32[8,128]{1,0:T(8,128)}) custom-call(s32[480]{0:T(512)S(1)} %get-tuple-element.162.refs_0_, s32[480]{0:T(512)S(1)} %get-tuple-element.201.refs_1_, bf16[192,5120]{1,0:T(8,128)(2,1)S(1)} %constant_dynamic-update-slice_fusion.refs_2_.refs_0_, ...), custom_call_target="tpu_custom_call" | custom-call | flops 6039797760 | bytes 8388608 | tf_op jit(solution)/shard_map/pallas_call | solution.py:222
  45.8 5.1 %shard_map.120 = (bf16[384,1536]{1,0:T(8,128)(2,1)S(1)}, f32[384,1536]{1,0:T(8,128)S(1)}, f32[384,1536]{1,0:T(8,128)S(1)}, s32[8,128]{1,0:T(8,128)}) custom-call(s32[480]{0:T(512)S(1)} %get-tuple-element.162.refs_0_, s32[480]{0:T(512)S(1)} %get-tuple-element.201.refs_1_, ...), custom_call_target="tpu_custom_call", output_to_operand_aliasing={{0}: (5, {}), {1}: (6, {}), {2}: (7, {})} | custom-call | flops 6039797760 | bytes 8388608 | tf_op jit(solution)/shard_map/pallas_call | solution.py:222
  50.9 6.3 %collective-permute-done.8 = bf16[24,5120]{1,0:T(8,128)(2,1)S(1)} collective-permute-done((bf16[24,5120]{1,0:T(8,128)(2,1)S(1)}, bf16[24,5120]{1,0:T(8,128)(2,1)S(1)}, u32[]{:S(2)}, u32[]{:S(2)}) %collective-permute-start.8) | collective-permute-done | bytes 245792 | tf_op jit(solution)/shard_map/ppermute | solution.py:27
  60.6 8.9 %shard_map.121 = (bf16[384,1536]{1,0:T(8,128)(2,1)S(1)}, f32[384,1536]{1,0:T(8,128)S(1)}, f32[384,1536]{1,0:T(8,128)S(1)}, s32[8,128]{1,0:T(8,128)}) custom-call(s32[480]{0:T(512)S(1)} %get-tuple-element.162.refs_0_, s32[480]{0:T(512)S(1)} %get-tuple-element.201.refs_1_, ...), custom_call_target="tpu_custom_call", output_to_operand_aliasing={{0}: (5, {}), {1}: (6, {}), {2}: (7, {})} | custom-call | flops 12079595520 | bytes 8388608 | tf_op jit(solution)/shard_map/pallas_call | solution.py:222
  73.0 11.4 %shard_map.122 = (f32[336,5120]{1,0:T(8,128)S(1)}, bf16[48,5120]{1,0:T(8,128)(2,1)S(1)}, s32[8,128]{1,0:T(8,128)}) custom-call(s32[480]{0:T(512)S(1)} %select_reduce_fusion.2.refs_0_, bf16[384,1536]{1,0:T(8,128)(2,1)S(1)} %get-tuple-element.124.refs_1_, bf16[121,128,128]{2,1,0:T(8,128)(2,1)S(1)} %copy-done.4), custom_call_target="tpu_custom_call" | custom-call | flops 12079595520 | bytes 8388608 | tf_op jit(solution)/shard_map/pallas_call | solution.py:222
  86.6 6.1 %collective-permute-done.14 = bf16[24,5120]{1,0:T(8,128)(2,1)S(1)} collective-permute-done((bf16[24,5120]{1,0:T(8,128)(2,1)S(1)}, bf16[24,5120]{1,0:T(8,128)(2,1)S(1)}, u32[]{:S(2)}, u32[]{:S(2)}) %collective-permute-start.14) | collective-permute-done | bytes 245792 | tf_op jit(solution)/shard_map/ppermute | solution.py:27
  95.1 5.1 %shard_map.123 = (bf16[384,1536]{1,0:T(8,128)(2,1)S(1)}, bf16[384,1536]{1,0:T(8,128)(2,1)S(1)}, s32[8,128]{1,0:T(8,128)}) custom-call(s32[480]{0:T(512)S(1)} %select_reduce_fusion.2.refs_0_, bf16[384,5120]{1,0:T(8,128)(2,1)S(1)} %constant_dynamic-update-slice_fusion.9.refs_1_.refs_0_, bf16[121,128,128]{2,1,0:T(8,128)(2,1)S(1)} %copy-done.4, ...), custom_call_target="tpu_custom_call" | custom-call | flops 6039797760 | bytes 8388608 | tf_op jit(solution)/shard_map/pallas_call | solution.py:222
  104.2 5.1 %shard_map.124 = (bf16[384,1536]{1,0:T(8,128)(2,1)S(1)}, bf16[384,1536]{1,0:T(8,128)(2,1)S(1)}, s32[8,128]{1,0:T(8,128)}) custom-call(s32[480]{0:T(512)S(1)} %select_reduce_fusion.2.refs_0_, bf16[384,5120]{1,0:T(8,128)(2,1)S(1)} %constant_dynamic-update-slice_fusion.9.refs_1_.refs_0_, ...), custom_call_target="tpu_custom_call", output_to_operand_aliasing={{0}: (5, {}), {1}: (6, {})} | custom-call | flops 6039797760 | bytes 8388608 | tf_op jit(solution)/shard_map/pallas_call | solution.py:222
  109.3 5.4 %shard_map.125 = (f32[336,5120]{1,0:T(8,128)S(1)}, bf16[48,5120]{1,0:T(8,128)(2,1)S(1)}, s32[8,128]{1,0:T(8,128)}) custom-call(s32[480]{0:T(512)S(1)} %get-tuple-element.162.refs_0_, s32[480]{0:T(512)S(1)} %get-tuple-element.201.refs_1_, bf16[384,1536]{1,0:T(8,128)(2,1)S(1)} %get-tuple-element.151.refs_2_, ...), custom_call_target="tpu_custom_call" | custom-call | flops 6039797760 | bytes 8388608 | tf_op jit(solution)/shard_map/pallas_call | solution.py:222
  115.8 2.7 %collective-permute-start.21 = (bf16[48,5120]{1,0:T(8,128)(2,1)S(1)}, bf16[48,5120]{1,0:T(8,128)(2,1)S(1)}, u32[]{:S(2)}, u32[]{:S(2)}) collective-permute-start(bf16[48,5120]{1,0:T(8,128)(2,1)S(1)} %get-tuple-element.155), channel_id=1, source_target_pairs={{4,0},{8,4},{12,8},{14,12},{10,14},{6,10},{2,6},{0,2},{5,1},{9,5},... | collective-permute-start | bytes 1474568 | tf_op jit(solution)/shard_map/ppermute | solution.py:30
  118.5 9.7 %shard_map.126 = (f32[336,5120]{1,0:T(8,128)S(1)}, bf16[48,5120]{1,0:T(8,128)(2,1)S(1)}, s32[8,128]{1,0:T(8,128)}) custom-call(s32[480]{0:T(512)S(1)} %get-tuple-element.162.refs_0_, s32[480]{0:T(512)S(1)} %get-tuple-element.201.refs_1_, bf16[384,1536]{1,0:T(8,128)(2,1)S(1)} %get-tuple-element.151.refs_2_, ...), custom_call_target="tpu_custom_call", output_to_operand_aliasing={{0}: (6, {}), {1}: (7, {})} | custom-call | flops 12079595520 | bytes 8388608 | tf_op jit(solution)/shard_map/pallas_call | solution.py:222
  130.0 2.5 %collective-permute-done.20 = bf16[48,5120]{1,0:T(8,128)(2,1)S(1)} collective-permute-done((bf16[48,5120]{1,0:T(8,128)(2,1)S(1)}, bf16[48,5120]{1,0:T(8,128)(2,1)S(1)}, u32[]{:S(2)}, u32[]{:S(2)}) %collective-permute-start.20) | collective-permute-done | bytes 491552 | tf_op jit(solution)/shard_map/ppermute | solution.py:27
  134.9 5.4 %shard_map.127 = (f32[336,5120]{1,0:T(8,128)S(1)}, bf16[48,5120]{1,0:T(8,128)(2,1)S(1)}, s32[8,128]{1,0:T(8,128)}) custom-call(s32[480]{0:T(512)S(1)} %get-tuple-element.162.refs_0_, s32[480]{0:T(512)S(1)} %get-tuple-element.201.refs_1_, bf16[384,1536]{1,0:T(8,128)(2,1)S(1)} %get-tuple-element.151.refs_2_, ...), custom_call_target="tpu_custom_call", output_to_operand_aliasing={{0}: (6, {}), {1}: (7, {})} | custom-call | flops 6039797760 | bytes 8388608 | tf_op jit(solution)/shard_map/pallas_call | solution.py:222
  143.2 3.8 %shard_map.128 = bf16[60,128,128]{2,1,0:T(8,128)(2,1)S(1)} custom-call(s32[60]{0:T(128)S(1)} %get-tuple-element.167.at, bf16[384,5120]{1,0:T(8,128)(2,1)S(1)} %constant_dynamic-update-slice_fusion.9.refs_1_.refs_0_, bf16[384,1536]{1,0:T(8,128)(2,1)S(1)} %get-tuple-element.124.refs_1_), custom_call_target="tpu_custom_call" | custom-call | flops 3019898880 | bytes 8388608 | tf_op jit(solution)/shard_map/pallas_call | solution.py:273
  150.3 4.0 %shard_map.129 = bf16[60,128,128]{2,1,0:T(8,128)(2,1)S(1)} custom-call(s32[60]{0:T(128)S(1)} %get-tuple-element.170.at, bf16[192,5120]{1,0:T(8,128)(2,1)S(1)} %constant_dynamic-update-slice_fusion.refs_2_.refs_0_, bf16[192,5120]{1,0:T(8,128)(2,1)S(1)} %constant_dynamic-update-slice_fusion.4.refs_2_.refs_1_, bf16[384,1536]{1,0:T(8,128)(2,1)S(1)} %get-tuple-element.151.refs_2_), custom_call_target="tpu_custom_call" | custom-call | flops 3019898880 | bytes 8388608 | tf_op jit(solution)/shard_map/pallas_call | solution.py:273
  154.4 4.0 %shard_map.130 = bf16[60,128,128]{2,1,0:T(8,128)(2,1)S(1)} custom-call(s32[60]{0:T(128)S(1)} %get-tuple-element.171.at, bf16[192,5120]{1,0:T(8,128)(2,1)S(1)} %constant_dynamic-update-slice_fusion.refs_2_.refs_0_, bf16[192,5120]{1,0:T(8,128)(2,1)S(1)} %constant_dynamic-update-slice_fusion.4.refs_2_.refs_1_, ...), custom_call_target="tpu_custom_call" | custom-call | flops 3019898880 | bytes 8388608 | tf_op jit(solution)/shard_map/pallas_call | solution.py:273
  165.1 5.2 %shard_map.131 = f32[60,128,128]{2,1,0:T(8,128)} custom-call(s32[60]{0:T(128)S(1)} %get-tuple-element.174.at, bf16[384,5120]{1,0:T(8,128)(2,1)S(1)} %constant_dynamic-update-slice_fusion.9.refs_1_.refs_0_, bf16[384,1536]{1,0:T(8,128)(2,1)S(1)} %get-tuple-element.124.refs_1_, bf16[60,128,128]{2,1,0:T(8,128)(2,1)S(1)} %collective-permute-done.28.refs_2_), custom_call_target="tpu_custom_call" | custom-call | flops 3019898880 | bytes 8388608 | tf_op jit(solution)/shard_map/pallas_call | solution.py:273
  170.2 3.3 %collective-permute-done.30 = bf16[48,5120]{1,0:T(8,128)(2,1)S(1)} collective-permute-done((bf16[48,5120]{1,0:T(8,128)(2,1)S(1)}, bf16[48,5120]{1,0:T(8,128)(2,1)S(1)}, u32[]{:S(2)}, u32[]{:S(2)}) %collective-permute-start.30) | collective-permute-done | bytes 491552 | tf_op jit(solution)/shard_map/ppermute | solution.py:30
  176.9 5.3 %shard_map.132 = f32[60,128,128]{2,1,0:T(8,128)} custom-call(s32[60]{0:T(128)S(1)} %get-tuple-element.177.at, bf16[192,5120]{1,0:T(8,128)(2,1)S(1)} %constant_dynamic-update-slice_fusion.refs_2_.refs_0_, bf16[192,5120]{1,0:T(8,128)(2,1)S(1)} %constant_dynamic-update-slice_fusion.4.refs_2_.refs_1_, bf16[384,1536]{1,0:T(8,128)(2,1)S(1)} %get-tuple-element.151.refs_2_, ...), custom_call_target="tpu_custom_call" | custom-call | flops 3019898880 | bytes 8388608 | tf_op jit(solution)/shard_map/pallas_call | solution.py:273
  182.2 5.3 %shard_map.133 = f32[60,128,128]{2,1,0:T(8,128)} custom-call(s32[60]{0:T(128)S(1)} %get-tuple-element.178.at, bf16[192,5120]{1,0:T(8,128)(2,1)S(1)} %constant_dynamic-update-slice_fusion.refs_2_.refs_0_, bf16[192,5120]{1,0:T(8,128)(2,1)S(1)} %constant_dynamic-update-slice_fusion.4.refs_2_.refs_1_, bf16[384,1536]{1,0:T(8,128)(2,1)S(1)} %get-tuple-element.152.refs_3_.refs_2_, ...), custom_call_target="tpu_custom_call" | custom-call | flops 3019898880 | bytes 8388608 | tf_op jit(solution)/shard_map/pallas_call | solution.py:273
  (127 shorter events, 58.9 us)
Async XLA Ops:
  0.7 14.5 %collective-permute-start = (bf16[48,5120]{1,0:T(8,128)(2,1)}, bf16[48,5120]{1,0:T(8,128)(2,1)S(1)}, u32[]{:S(2)}, u32[]{:S(2)}) collective-permute-start(bf16[48,5120]{1,0:T(8,128)(2,1)} %param.8), channel_id=1, source_target_pairs={{0,4},{4,8},{8,12},{12,14},{14,10},{10,6},{6,2},{2,0},{1,5},{5,9},... | collective-permute-start | bytes 1474568 | tf_op jit(solution)/shard_map/ppermute | solution.py:27
  3.7 12.9 %collective-permute-start.1 = (bf16[48,5120]{1,0:T(8,128)(2,1)}, bf16[48,5120]{1,0:T(8,128)(2,1)S(1)}, u32[]{:S(2)}, u32[]{:S(2)}) collective-permute-start(bf16[48,5120]{1,0:T(8,128)(2,1)} %param.8), channel_id=1, source_target_pairs={{4,0},{8,4},{12,8},{14,12},{10,14},{6,10},{2,6},{0,2},{5,1},{9,5},... | collective-permute-start | bytes 1474568 | tf_op jit(solution)/shard_map/ppermute | solution.py:30
  16.6 11.8 %collective-permute-start.2 = (bf16[48,5120]{1,0:T(8,128)(2,1)S(1)}, bf16[48,5120]{1,0:T(8,128)(2,1)S(1)}, u32[]{:S(2)}, u32[]{:S(2)}) collective-permute-start(bf16[48,5120]{1,0:T(8,128)(2,1)S(1)} %collective-permute-done), channel_id=1, source_target_pairs={{0,4},{4,8},{8,12},{12,14},{14,10},{10,6},{6,2},{2,0},{1,5},{5,9},... | collective-permute-start | bytes 1474568 | tf_op jit(solution)/shard_map/ppermute | solution.py:27
  18.2 11.5 %collective-permute-start.3 = (bf16[48,5120]{1,0:T(8,128)(2,1)S(1)}, bf16[48,5120]{1,0:T(8,128)(2,1)S(1)}, u32[]{:S(2)}, u32[]{:S(2)}) collective-permute-start(bf16[48,5120]{1,0:T(8,128)(2,1)S(1)} %collective-permute-done.1), channel_id=1, source_target_pairs={{4,0},{8,4},{12,8},{14,12},{10,14},{6,10},{2,6},{0,2},{5,1},{9,5},... | collective-permute-start | bytes 1474568 | tf_op jit(solution)/shard_map/ppermute | solution.py:30
  29.7 11.5 %collective-permute-start.4 = (bf16[48,5120]{1,0:T(8,128)(2,1)S(1)}, bf16[48,5120]{1,0:T(8,128)(2,1)S(1)}, u32[]{:S(2)}, u32[]{:S(2)}) collective-permute-start(bf16[48,5120]{1,0:T(8,128)(2,1)S(1)} %collective-permute-done.2), channel_id=1, source_target_pairs={{0,4},{4,8},{8,12},{12,14},{14,10},{10,6},{6,2},{2,0},{1,5},{5,9},... | collective-permute-start | bytes 1474568 | tf_op jit(solution)/shard_map/ppermute | solution.py:27
  41.6 16.7 %collective-permute-start.6 = (bf16[48,5120]{1,0:T(8,128)(2,1)S(1)}, bf16[48,5120]{1,0:T(8,128)(2,1)S(1)}, u32[]{:S(2)}, u32[]{:S(2)}) collective-permute-start(bf16[48,5120]{1,0:T(8,128)(2,1)S(1)} %copy-done.9), channel_id=1, source_target_pairs={{0,4},{4,8},{8,12},{12,14},{14,10},{10,6},{6,2},{2,0},{1,5},{5,9},... | collective-permute-start | bytes 1474568 | tf_op jit(solution)/shard_map/ppermute | solution.py:27
  43.1 15.2 %collective-permute-start.7 = (bf16[48,5120]{1,0:T(8,128)(2,1)S(1)}, bf16[48,5120]{1,0:T(8,128)(2,1)S(1)}, u32[]{:S(2)}, u32[]{:S(2)}) collective-permute-start(bf16[48,5120]{1,0:T(8,128)(2,1)S(1)} %copy-done.9), channel_id=1, source_target_pairs={{4,0},{8,4},{12,8},{14,12},{10,14},{6,10},{2,6},{0,2},{5,1},{9,5},... | collective-permute-start | bytes 1474568 | tf_op jit(solution)/shard_map/ppermute | solution.py:30
  43.6 13.5 %collective-permute-start.8 = (bf16[24,5120]{1,0:T(8,128)(2,1)S(1)}, bf16[24,5120]{1,0:T(8,128)(2,1)S(1)}, u32[]{:S(2)}, u32[]{:S(2)}) collective-permute-start(bf16[24,5120]{1,0:T(8,128)(2,1)S(1)} %slice.69), channel_id=1, source_target_pairs={{0,4},{4,8},{8,12},{12,14},{14,10},{10,6},{6,2},{2,0},{1,5},{5,9},... | collective-permute-start | bytes 737288 | tf_op jit(solution)/shard_map/ppermute | solution.py:27
  45.2 13.1 %collective-permute-start.9 = (bf16[24,5120]{1,0:T(8,128)(2,1)S(1)}, bf16[24,5120]{1,0:T(8,128)(2,1)S(1)}, u32[]{:S(2)}, u32[]{:S(2)}) collective-permute-start(bf16[24,5120]{1,0:T(8,128)(2,1)S(1)} %slice.70), channel_id=1, source_target_pairs={{4,0},{8,4},{12,8},{14,12},{10,14},{6,10},{2,6},{0,2},{5,1},{9,5},... | collective-permute-start | bytes 737288 | tf_op jit(solution)/shard_map/ppermute | solution.py:30
  58.3 12.7 %collective-permute-start.10 = (bf16[48,5120]{1,0:T(8,128)(2,1)S(1)}, bf16[48,5120]{1,0:T(8,128)(2,1)S(1)}, u32[]{:S(2)}, u32[]{:S(2)}) collective-permute-start(bf16[48,5120]{1,0:T(8,128)(2,1)S(1)} %collective-permute-done.6), channel_id=1, source_target_pairs={{0,4},{4,8},{8,12},{12,14},{14,10},{10,6},{6,2},{2,0},{1,5},{5,9},... | collective-permute-start | bytes 1474568 | tf_op jit(solution)/shard_map/ppermute | solution.py:27
  70.9 13.4 %collective-permute-start.12 = (bf16[48,5120]{1,0:T(8,128)(2,1)S(1)}, bf16[48,5120]{1,0:T(8,128)(2,1)S(1)}, u32[]{:S(2)}, u32[]{:S(2)}) collective-permute-start(bf16[48,5120]{1,0:T(8,128)(2,1)S(1)} %collective-permute-done.10), channel_id=1, source_target_pairs={{0,4},{4,8},{8,12},{12,14},{14,10},{10,6},{6,2},{2,0},{1,5},{5,9},... | collective-permute-start | bytes 1474568 | tf_op jit(solution)/shard_map/ppermute | solution.py:27
  73.0 11.4 %collective-permute-start.13 = (bf16[48,5120]{1,0:T(8,128)(2,1)S(1)}, bf16[48,5120]{1,0:T(8,128)(2,1)S(1)}, u32[]{:S(2)}, u32[]{:S(2)}) collective-permute-start(bf16[48,5120]{1,0:T(8,128)(2,1)S(1)} %collective-permute-done.11), channel_id=1, source_target_pairs={{4,0},{8,4},{12,8},{14,12},{10,14},{6,10},{2,6},{0,2},{5,1},{9,5},... | collective-permute-start | bytes 1474568 | tf_op jit(solution)/shard_map/ppermute | solution.py:30
  102.1 12.6 %collective-permute-start.19 = (bf16[48,5120]{1,0:T(8,128)(2,1)S(1)}, bf16[48,5120]{1,0:T(8,128)(2,1)S(1)}, u32[]{:S(2)}, u32[]{:S(2)}) collective-permute-start(bf16[48,5120]{1,0:T(8,128)(2,1)S(1)} %get-tuple-element.147), channel_id=1, source_target_pairs={{4,0},{8,4},{12,8},{14,12},{10,14},{6,10},{2,6},{0,2},{5,1},{9,5},... | collective-permute-start | bytes 1474568 | tf_op jit(solution)/shard_map/ppermute | solution.py:30
  102.7 12.8 %collective-permute-start.18 = (bf16[48,5120]{1,0:T(8,128)(2,1)S(1)}, bf16[48,5120]{1,0:T(8,128)(2,1)S(1)}, u32[]{:S(2)}, u32[]{:S(2)}) collective-permute-start(bf16[48,5120]{1,0:T(8,128)(2,1)S(1)} %get-tuple-element.146), channel_id=1, source_target_pairs={{0,4},{4,8},{8,12},{12,14},{14,10},{10,6},{6,2},{2,0},{1,5},{5,9},... | collective-permute-start | bytes 1474568 | tf_op jit(solution)/shard_map/ppermute | solution.py:27
  115.8 14.3 %collective-permute-start.21 = (bf16[48,5120]{1,0:T(8,128)(2,1)S(1)}, bf16[48,5120]{1,0:T(8,128)(2,1)S(1)}, u32[]{:S(2)}, u32[]{:S(2)}) collective-permute-start(bf16[48,5120]{1,0:T(8,128)(2,1)S(1)} %get-tuple-element.155), channel_id=1, source_target_pairs={{4,0},{8,4},{12,8},{14,12},{10,14},{6,10},{2,6},{0,2},{5,1},{9,5},... | collective-permute-start | bytes 1474568 | tf_op jit(solution)/shard_map/ppermute | solution.py:30
  118.5 14.1 %collective-permute-start.20 = (bf16[48,5120]{1,0:T(8,128)(2,1)S(1)}, bf16[48,5120]{1,0:T(8,128)(2,1)S(1)}, u32[]{:S(2)}, u32[]{:S(2)}) collective-permute-start(bf16[48,5120]{1,0:T(8,128)(2,1)S(1)} %get-tuple-element.154), channel_id=1, source_target_pairs={{0,4},{4,8},{8,12},{12,14},{14,10},{10,6},{6,2},{2,0},{1,5},{5,9},... | collective-permute-start | bytes 1474568 | tf_op jit(solution)/shard_map/ppermute | solution.py:27
  147.0 15.0 %collective-permute-start.28 = (bf16[60,128,128]{2,1,0:T(8,128)(2,1)S(1)}, bf16[60,128,128]{2,1,0:T(8,128)(2,1)S(1)}, u32[]{:S(2)}, u32[]{:S(2)}) collective-permute-start(bf16[60,128,128]{2,1,0:T(8,128)(2,1)S(1)} %shard_map.128), channel_id=1, source_target_pairs={{0,1},{1,0},{2,3},{3,2},{4,5},{5,4},{6,7},{7,6},{8,9},{9,8},{10,11... | collective-permute-start | bytes 5898248 | tf_op jit(solution)/shard_map/ppermute | solution.py:407
  148.2 12.7 %collective-permute-start.27 = (bf16[48,5120]{1,0:T(8,128)(2,1)S(1)}, bf16[48,5120]{1,0:T(8,128)(2,1)S(1)}, u32[]{:S(2)}, u32[]{:S(2)}) collective-permute-start(bf16[48,5120]{1,0:T(8,128)(2,1)S(1)} %get-tuple-element.169), channel_id=1, source_target_pairs={{4,0},{8,4},{12,8},{14,12},{10,14},{6,10},{2,6},{0,2},{5,1},{9,5},... | collective-permute-start | bytes 1474568 | tf_op jit(solution)/shard_map/ppermute | solution.py:30
  149.4 12.3 %collective-permute-start.26 = (bf16[48,5120]{1,0:T(8,128)(2,1)S(1)}, bf16[48,5120]{1,0:T(8,128)(2,1)S(1)}, u32[]{:S(2)}, u32[]{:S(2)}) collective-permute-start(bf16[48,5120]{1,0:T(8,128)(2,1)S(1)} %get-tuple-element.168), channel_id=1, source_target_pairs={{0,4},{4,8},{8,12},{12,14},{14,10},{10,6},{6,2},{2,0},{1,5},{5,9},... | collective-permute-start | bytes 1474568 | tf_op jit(solution)/shard_map/ppermute | solution.py:27
  154.3 20.5 %collective-permute-start.31 = (bf16[60,128,128]{2,1,0:T(8,128)(2,1)S(1)}, bf16[60,128,128]{2,1,0:T(8,128)(2,1)S(1)}, u32[]{:S(2)}, u32[]{:S(2)}) collective-permute-start(bf16[60,128,128]{2,1,0:T(8,128)(2,1)S(1)} %shard_map.129), channel_id=1, source_target_pairs={{0,1},{1,0},{2,3},{3,2},{4,5},{5,4},{6,7},{7,6},{8,9},{9,8},{10,11... | collective-permute-start | bytes 5898248 | tf_op jit(solution)/shard_map/ppermute | solution.py:407
  158.4 16.4 %collective-permute-start.32 = (bf16[60,128,128]{2,1,0:T(8,128)(2,1)S(1)}, bf16[60,128,128]{2,1,0:T(8,128)(2,1)S(1)}, u32[]{:S(2)}, u32[]{:S(2)}) collective-permute-start(bf16[60,128,128]{2,1,0:T(8,128)(2,1)S(1)} %shard_map.130), channel_id=1, source_target_pairs={{0,1},{1,0},{2,3},{3,2},{4,5},{5,4},{6,7},{7,6},{8,9},{9,8},{10,11... | collective-permute-start | bytes 5898248 | tf_op jit(solution)/shard_map/ppermute | solution.py:407
  162.0 11.5 %collective-permute-start.30 = (bf16[48,5120]{1,0:T(8,128)(2,1)S(1)}, bf16[48,5120]{1,0:T(8,128)(2,1)S(1)}, u32[]{:S(2)}, u32[]{:S(2)}) collective-permute-start(bf16[48,5120]{1,0:T(8,128)(2,1)S(1)} %get-tuple-element.173), channel_id=1, source_target_pairs={{4,0},{8,4},{12,8},{14,12},{10,14},{6,10},{2,6},{0,2},{5,1},{9,5},... | collective-permute-start | bytes 1474568 | tf_op jit(solution)/shard_map/ppermute | solution.py:30
  174.8 12.7 %collective-permute-start.34 = (bf16[48,5120]{1,0:T(8,128)(2,1)S(1)}, bf16[48,5120]{1,0:T(8,128)(2,1)S(1)}, u32[]{:S(2)}, u32[]{:S(2)}) collective-permute-start(bf16[48,5120]{1,0:T(8,128)(2,1)S(1)} %get-tuple-element.176), channel_id=1, source_target_pairs={{4,0},{8,4},{12,8},{14,12},{10,14},{6,10},{2,6},{0,2},{5,1},{9,5},... | collective-permute-start | bytes 1474568 | tf_op jit(solution)/shard_map/ppermute | solution.py:30
  176.1 11.4 %collective-permute-start.33 = (bf16[48,5120]{1,0:T(8,128)(2,1)S(1)}, bf16[48,5120]{1,0:T(8,128)(2,1)S(1)}, u32[]{:S(2)}, u32[]{:S(2)}) collective-permute-start(bf16[48,5120]{1,0:T(8,128)(2,1)S(1)} %get-tuple-element.175), channel_id=1, source_target_pairs={{0,4},{4,8},{8,12},{12,14},{14,10},{10,6},{6,2},{2,0},{1,5},{5,9},... | collective-permute-start | bytes 1474568 | tf_op jit(solution)/shard_map/ppermute | solution.py:27
  (24 other events, 181.8 us)
